TPU v7x, 32 devices: a whole 2x2x4 slice. The times are simulated.
32 devices in a mesh: seq: 8 (over z, core), head: 4 (over y, x).
Axes of the slice: x: 2, y: 2, z: 4, core: 2. Of those that a mesh axis runs over, the one named last changes fastest.
Arguments:
- tokens: bfloat16 [8192, 1152], P('seq'), may hold values from -6 to 6
- conditioning: bfloat16 [16, 1152], replicated, may hold values from -6 to 6
- image_index: int32 [8192], replicated, may hold values from 0 to 15, as said below
- qkv_weight: bfloat16 [1152, 3, 1152], P(None, None, 'head'), may hold values from -0.1875 to 0.1875
- qv_bias: bfloat16 [2, 1152], P(None, 'head'), may hold values from -3 to 3
- out_weight: bfloat16 [1152, 1152], P('head'), may hold values from -2 to 2
- out_bias: bfloat16 [1152], replicated, may hold values from -3 to 3
- up_weight: bfloat16 [1152, 4608], P(None, 'head'), may hold values from -0.1875 to 0.1875
- up_bias: bfloat16 [4608], P('head'), may hold values from -3 to 3
- down_weight: bfloat16 [4608, 1152], P('head'), may hold values from -0.09375 to 0.09375
- down_bias: bfloat16 [1152], replicated, may hold values from -3 to 3
- ada_weight: bfloat16 [1152, 6, 1152], P(None, None, 'head'), may hold values from -0.1875 to 0.1875
- ada_bias: bfloat16 [6, 1152], P(None, 'head'), may hold values from -3 to 3
- cotangent: bfloat16 [8192, 1152], P('seq'), may hold values from -6 to 6
Outputs:
- layer_out: bfloat16 [8192, 1152], P('seq')
- grad_tokens: float32 [8192, 1152], P('seq')
- grad_conditioning: float32 [16, 1152], replicated
- grad_qkv_weight: float32 [1152, 3, 1152], P('seq', None, 'head')
- grad_qv_bias: float32 [2, 1152], P(None, 'head')
- grad_out_weight: float32 [1152, 1152], P('head', 'seq')
- grad_out_bias: float32 [1152], replicated
- grad_up_weight: float32 [1152, 4608], P('seq', 'head')
- grad_up_bias: float32 [4608], P('head')
- grad_down_weight: float32 [4608, 1152], P('head', 'seq')
- grad_down_bias: float32 [1152], replicated
- grad_ada_weight: float32 [1152, 6, 1152], P(None, None, 'head')
- grad_ada_bias: float32 [6, 1152], P(None, 'head')
Inputs may be any that keep to these rules, and one draw needn't show every extreme that they name: `image_index`: never falls along the rows and every image 0 to 15 holds a row. Each image's rows lie inside two consecutive aligned blocks of 1024 rows; every border between two aligned blocks of 1024 rows lies inside some image.
All inputs are finite; a program needn't handle non-finite values.
Results may differ from a plain program's by a relative error of at most 0.02.
The roundings to bfloat16 on the way count: a program that leaves them out, or rounds other values in their place, can miss the bound.
Values may be sent and summed in bfloat16 or wider, within the bound.
No kernel may reach another device: no remote copies, remote signals or barrier semaphores. Data moves between devices by JAX's collectives and lax.ppermute only.
A program may use at most 320 MiB of HBM per device.

v0:
```python
import jax
import jax.numpy as jnp
from jax import lax
from jax.sharding import PartitionSpec as P

HDIM = 72


EPSILON = 1e-06
MASKED = -1e30
PRECISE = lax.Precision.HIGHEST


def extended(cells, sides, width):
    for axis, dim in sides:
        count = lax.axis_size(axis)
        ends = count - 1
        head = lax.slice_in_dim(cells, 0, width, axis=dim)
        tail = lax.slice_in_dim(cells, cells.shape[dim] - width, cells.shape[dim], axis=dim)
        cells = jnp.concatenate(
            [
                lax.ppermute(tail, axis, [(i, (i + 1) % count) for i in range(ends)]),
                cells,
                lax.ppermute(head, axis, [((i + 1) % count, i) for i in range(ends)]),
            ],
            axis=dim,
        )
    return cells


def normalize(values):
    center = values - jnp.mean(values, axis=-1, keepdims=True)
    inverse = lax.rsqrt(jnp.mean(center * center, axis=-1, keepdims=True) + EPSILON)
    return (center * inverse, inverse)


def norm_back(gradient, normed, inverse):
    return (
        gradient
        - jnp.mean(gradient, axis=-1, keepdims=True)
        - normed * jnp.mean(gradient * normed, axis=-1, keepdims=True)
    ) * inverse


def gelu_tanh(values):
    return jax.nn.gelu(values, approximate=True)


def split_heads(matrix, head_count):
    amount = matrix.shape[0]
    return matrix.reshape(amount, head_count, -1).transpose(1, 0, 2)


def join_heads(tensor):
    head_count, amount, head_size = tensor.shape
    return tensor.transpose(1, 0, 2).reshape(amount, head_count * head_size)


def score_grads(
    query_heads, grad_heads, key_heads, value_heads, visible, log_total, delta, scaling
):
    scores = (
        jnp.einsum("hqd,hkd->hqk", query_heads, key_heads, preferred_element_type=jnp.float32)
        * scaling
    )
    shares = jnp.where(visible, jnp.exp(scores - log_total[..., None]), 0.0)
    grad_shares = jnp.einsum(
        "hqd,hkd->hqk", grad_heads, value_heads, preferred_element_type=jnp.float32
    )
    grad_scores = (shares * (grad_shares - delta[..., None])).astype(jnp.bfloat16)
    return (shares.astype(jnp.bfloat16), grad_scores)


def on_device(
    tokens,
    conditioning,
    image_index,
    qkv_weight,
    qv_bias,
    out_weight,
    out_bias,
    up_weight,
    up_bias,
    down_weight,
    down_bias,
    ada_weight,
    ada_bias,
    cotangent,
):
    row_count = tokens.shape[0]
    feature_count = qkv_weight.shape[2]
    head_count = feature_count // HDIM
    scaling = HDIM ** (-0.5)
    my_index = lax.axis_index("seq")
    my_images = lax.dynamic_slice_in_dim(image_index, my_index * row_count, row_count, 0)
    padded_images = jnp.pad(image_index, (row_count, row_count), constant_values=-1)
    wide_images = lax.dynamic_slice_in_dim(padded_images, my_index * row_count, 3 * row_count, 0)
    image_count = conditioning.shape[0]
    one_hot = (my_images[:, None] == jnp.arange(image_count, dtype=jnp.int32)[None, :]).astype(
        jnp.float32
    )
    cond_float = conditioning.astype(jnp.float32)
    cond_act = jax.nn.silu(cond_float).astype(jnp.bfloat16)
    mod_mine = jnp.einsum("id,dkf->ikf", cond_act, ada_weight, preferred_element_type=jnp.float32)
    mod_mine = mod_mine + ada_bias.astype(jnp.float32)[None]
    modulation = lax.all_gather(mod_mine, "head", axis=2, tiled=True)
    per_row = [
        jnp.dot(one_hot, modulation[:, component], precision=PRECISE) for component in range(6)
    ]
    shift_one, scale_one, gate_one, shift_two, scale_two, gate_two = per_row
    inputs = tokens.astype(jnp.float32)
    normed_one, inverse_one = normalize(inputs)
    hidden_one = (normed_one * (1.0 + scale_one) + shift_one).astype(jnp.bfloat16)
    projected = jnp.einsum(
        "td,dkf->tkf", hidden_one, qkv_weight, preferred_element_type=jnp.float32
    )
    bias_rows = qv_bias.astype(jnp.float32)
    query_low = (projected[:, 0] + bias_rows[0]).astype(jnp.bfloat16)
    key_low = projected[:, 1].astype(jnp.bfloat16)
    value_low = (projected[:, 2] + bias_rows[1]).astype(jnp.bfloat16)
    key_value = jnp.stack([key_low, value_low], axis=1)
    query_heads = split_heads(query_low, head_count)
    wide_kv = extended(key_value, (("seq", 0),), row_count)
    wide_keys = split_heads(wide_kv[:, 0], head_count)
    wide_values = split_heads(wide_kv[:, 1], head_count)
    visible = (my_images[:, None] == wide_images[None, :])[None]
    scores = (
        jnp.einsum("hqd,hkd->hqk", query_heads, wide_keys, preferred_element_type=jnp.float32)
        * scaling
    )
    scores = jnp.where(visible, scores, MASKED)
    row_max = jnp.max(scores, axis=-1)
    weights = jnp.where(visible, jnp.exp(scores - row_max[..., None]), 0.0)
    row_total = jnp.sum(weights, axis=-1)
    log_total = row_max + jnp.log(row_total)
    shares = (weights / row_total[..., None]).astype(jnp.bfloat16)
    attended = jnp.einsum("hqk,hkd->hqd", shares, wide_values, preferred_element_type=jnp.float32)
    attended_low = join_heads(attended).astype(jnp.bfloat16)
    attn_branch = lax.psum(
        jnp.dot(attended_low, out_weight, preferred_element_type=jnp.float32), "head"
    ) + out_bias.astype(jnp.float32)
    middle = inputs + gate_one * attn_branch
    normed_two, inverse_two = normalize(middle)
    hidden_two = (normed_two * (1.0 + scale_two) + shift_two).astype(jnp.bfloat16)
    pre_act = jnp.dot(hidden_two, up_weight, preferred_element_type=jnp.float32) + up_bias.astype(
        jnp.float32
    )
    act_low = gelu_tanh(pre_act).astype(jnp.bfloat16)
    mlp_branch = lax.psum(
        jnp.dot(act_low, down_weight, preferred_element_type=jnp.float32), "head"
    ) + down_bias.astype(jnp.float32)
    layer_out = (middle + gate_two * mlp_branch).astype(jnp.bfloat16)
    grad_out = cotangent.astype(jnp.float32)
    grad_mlp = (gate_two * grad_out).astype(jnp.bfloat16)
    grad_down_bias = jnp.sum(grad_mlp.astype(jnp.float32), axis=0)
    grad_down_weight = jnp.einsum(
        "tf,td->fd", act_low, grad_mlp, preferred_element_type=jnp.float32
    )
    grad_act = jnp.dot(grad_mlp, down_weight.T, preferred_element_type=jnp.float32)
    _, gelu_pull = jax.vjp(gelu_tanh, pre_act)
    grad_pre = gelu_pull(grad_act)[0].astype(jnp.bfloat16)
    grad_up_bias = jnp.sum(grad_pre.astype(jnp.float32), axis=0)
    grad_up_weight = jnp.einsum(
        "td,tf->df", hidden_two, grad_pre, preferred_element_type=jnp.float32
    )
    grad_hidden_two = lax.psum(
        jnp.dot(grad_pre, up_weight.T, preferred_element_type=jnp.float32), "head"
    )
    grad_middle = grad_out + norm_back(grad_hidden_two * (1.0 + scale_two), normed_two, inverse_two)
    grad_attn = (gate_one * grad_middle).astype(jnp.bfloat16)
    grad_out_bias = jnp.sum(grad_attn.astype(jnp.float32), axis=0)
    grad_out_weight = jnp.einsum(
        "tf,td->fd", attended_low, grad_attn, preferred_element_type=jnp.float32
    )
    grad_attended = jnp.dot(grad_attn, out_weight.T, preferred_element_type=jnp.float32).astype(
        jnp.bfloat16
    )
    grad_heads = split_heads(grad_attended, head_count)
    delta = jnp.sum(grad_heads.astype(jnp.float32) * attended, axis=-1)
    shares_low, grad_scores = score_grads(
        query_heads, grad_heads, wide_keys, wide_values, visible, log_total, delta, scaling
    )
    grad_query_heads = (
        jnp.einsum("hqk,hkd->hqd", grad_scores, wide_keys, preferred_element_type=jnp.float32)
        * scaling
    )
    grad_keys_wide = (
        jnp.einsum("hqk,hqd->hkd", grad_scores, query_heads, preferred_element_type=jnp.float32)
        * scaling
    )
    grad_values_wide = jnp.einsum(
        "hqk,hqd->hkd", shares_low, grad_heads, preferred_element_type=jnp.float32
    )
    grad_wide = jnp.stack([join_heads(grad_keys_wide), join_heads(grad_values_wide)], axis=1)
    outward = jnp.concatenate([grad_wide[:row_count], grad_wide[2 * row_count :]], axis=0)
    inward = extended(outward, (("seq", 0),), row_count)
    grad_kv_mine = (
        grad_wide[row_count : 2 * row_count] + inward[:row_count] + inward[3 * row_count :]
    )
    grad_key_low = grad_kv_mine[:, 0].astype(jnp.bfloat16)
    grad_value_low = grad_kv_mine[:, 1].astype(jnp.bfloat16)
    grad_query_low = join_heads(grad_query_heads).astype(jnp.bfloat16)
    grad_qkv = jnp.stack([grad_query_low, grad_key_low, grad_value_low], axis=1)
    grad_qkv_weight = jnp.einsum(
        "td,tkf->dkf", hidden_one, grad_qkv, preferred_element_type=jnp.float32
    )
    grad_qv_bias = jnp.stack(
        [
            jnp.sum(grad_query_low.astype(jnp.float32), axis=0),
            jnp.sum(grad_value_low.astype(jnp.float32), axis=0),
        ]
    )
    grad_hidden_one = lax.psum(
        jnp.einsum("tkf,dkf->td", grad_qkv, qkv_weight, preferred_element_type=jnp.float32), "head"
    )
    grad_tokens = grad_middle + norm_back(
        grad_hidden_one * (1.0 + scale_one), normed_one, inverse_one
    )
    image_terms = [
        grad_hidden_one,
        grad_hidden_one * normed_one,
        grad_middle * attn_branch,
        grad_hidden_two,
        grad_hidden_two * normed_two,
        grad_out * mlp_branch,
    ]
    grad_mod_rows = jnp.stack(
        [jnp.dot(one_hot.T, term, precision=PRECISE) for term in image_terms], axis=1
    )
    ada_columns = ada_weight.shape[2]
    grad_mod_mine = lax.dynamic_slice_in_dim(
        grad_mod_rows, lax.axis_index("head") * ada_columns, ada_columns, 2
    )
    grad_mod_sum, grad_qv_bias, grad_up_bias, grad_out_bias, grad_down_bias = lax.psum(
        (grad_mod_mine, grad_qv_bias, grad_up_bias, grad_out_bias, grad_down_bias), "seq"
    )
    grad_ada_bias = jnp.sum(grad_mod_sum, axis=0)
    grad_ada_weight = jnp.einsum(
        "id,ikf->dkf", cond_act.astype(jnp.float32), grad_mod_sum, precision=PRECISE
    )
    grad_cond_act = lax.psum(
        jnp.einsum("ikf,dkf->id", grad_mod_sum, ada_weight.astype(jnp.float32), precision=PRECISE),
        "head",
    )
    _, silu_pull = jax.vjp(jax.nn.silu, cond_float)
    grad_conditioning = silu_pull(grad_cond_act)[0]
    grad_qkv_weight, grad_out_weight, grad_up_weight, grad_down_weight = (
        lax.psum_scatter(grad_qkv_weight, "seq", scatter_dimension=0, tiled=True),
        lax.psum_scatter(grad_out_weight, "seq", scatter_dimension=1, tiled=True),
        lax.psum_scatter(grad_up_weight, "seq", scatter_dimension=0, tiled=True),
        lax.psum_scatter(grad_down_weight, "seq", scatter_dimension=1, tiled=True),
    )
    return (
        layer_out,
        grad_tokens,
        grad_conditioning,
        grad_qkv_weight,
        grad_qv_bias,
        grad_out_weight,
        grad_out_bias,
        grad_up_weight,
        grad_up_bias,
        grad_down_weight,
        grad_down_bias,
        grad_ada_weight,
        grad_ada_bias,
    )


def solution(mesh):
    placed = (
        P("seq", None),
        P(),
        P(),
        P(None, None, "head"),
        P(None, "head"),
        P("head", None),
        P(),
        P(None, "head"),
        P("head"),
        P("head", None),
        P(),
        P(None, None, "head"),
        P(None, "head"),
        P("seq", None),
    )
    return jax.shard_map(
        on_device,
        mesh=mesh,
        in_specs=placed,
        out_specs=(
            P("seq", None),
            P("seq", None),
            P(),
            P("seq", None, "head"),
            P(None, "head"),
            P("head", "seq"),
            P(),
            P("seq", "head"),
            P("head"),
            P("head", "seq"),
            P(),
            P(None, None, "head"),
            P(None, "head"),
        ),
        check_vma=False,
    )
```

profile of v0, /device:TPU:0, one launch (start us, length us, event | category | flops | bytes accessed | tf_op | source)
XLA Modules:
  0.0 1089.1 jit_solution(17067473055612565872)
XLA Ops:
  15.9 45.7 %all_gather.3 = f32[16,6,1152]{0,1,2:T(8,128)S(1)} all-gather(f32[16,6,288]{0,1,2:T(8,128)} %copy.28), channel_id=1, replica_groups=mesh['seq'=8,'head'=4] {'head'}, dimensions={2}, use_global_device_ids=true | all-gather | bytes 552960 | tf_op jit(solution)/shard_map/all_gather | solution.py:106
  88.1 19.7 %select_reduce_fusion = (f32[4,1024]{1,0:T(4,128)S(1)}, f32[4,1024,3072]{2,1,0:T(8,128)}) fusion(pred[1024,3072]{1,0:T(8,128)(4,1)S(1)} %broadcast_compare_fusion, bf16[4,3072,72]{1,2,0:T(8,128)(2,1)S(1)} %bitcast.127, f32[1024,4,72]{0,2,1:T(8,128)S(1)} %bitcast.129, f32[4,72]{1,0:T(4,128)S(1)} %add.169), kind=kOutput, calls=%fused_computation.4 | convolution fusion | flops 1850273792 | bytes 56444032 | tf_op jit(solution)/shard_map/hqd,hkd->hqk/dot_general | solution.py:128
  107.8 24.3 %fusion.1 = f32[4,1024]{1,0:T(4,128)S(1)} fusion(f32[4,1024,3072]{2,1,0:T(8,128)} %get-tuple-element.51, f32[4,1024]{1,0:T(4,128)S(1)} %get-tuple-element.50, pred[1024,3072]{1,0:T(8,128)(4,1)} %copy-done.11), kind=kLoop, calls=%fused_computation.6 | loop fusion | flops 62910464 | bytes 53510144 | tf_op jit(solution)/shard_map/reduce_sum | solution.py:134
  132.2 22.8 %fusion.119 = (bf16[4,1024,72]{1,2,0:T(8,128)(2,1)S(1)}, f32[4,1024,72]{1,2,0:T(8,128)}) fusion(bf16[4,3072,72]{1,2,0:T(8,128)(2,1)} %bitcast.137, f32[4,1024,3072]{2,1,0:T(8,128)} %get-tuple-element.51, f32[4,1024]{1,0:T(4,128)S(1)} %fusion.1, f32[4,1024]{1,0:T(4,128)S(1)} %get-tuple-element.50, pred[1024,3072]{1,0:T(8,128)(4,1)} %copy-done.11), kind=kOutput, calls=%fused_computation.170 | convolution fusion | flops 1887731712 | bytes 57049088 | tf_op jit(solution)/shard_map/hqk,hkd->hqd/dot_general | solution.py:137
  159.5 9.8 all-reduce.11.cloned.1.call-start
  185.5 98.4 %all-reduce.9.cloned.1.call-done = f32[1024,1152]{1,0:T(8,128)} async-done(((f32[1024,1152]{1,0:T(8,128)}), f32[1024,1152]{1,0:T(8,128)}) %all-reduce.9.cloned.1.call-update) | async-done | bytes 4718608 | tf_op jit(solution)/shard_map/psum | solution.py:139
  283.9 6.7 fusion.115
  295.1 7.5 convert_reduce_fusion.2
  309.3 112.6 %all-reduce.11.cloned.1.call-done = f32[1024,1152]{1,0:T(8,128)} async-done(((f32[1024,1152]{1,0:T(8,128)}), f32[1024,1152]{1,0:T(8,128)}) %all-reduce.11.cloned.1.call-update) | async-done | bytes 4718608 | tf_op jit(solution)/shard_map/psum | solution.py:166
  437.2 21.1 %fusion.2 = f32[4,3072,72]{1,2,0:T(8,128)} fusion(bf16[4,1024,72]{1,2,0:T(8,128)(2,1)S(1)} %bitcast.144, f32[4,1024,3072]{2,1,0:T(8,128)} %get-tuple-element.51, f32[4,1024]{1,0:T(4,128)S(1)} %log_add_fusion, pred[1024,3072]{1,0:T(8,128)(4,1)} %copy-done.11), kind=kOutput, calls=%fused_computation.7 | convolution fusion | flops 1862270976 | bytes 57622528 | tf_op jit(solution)/shard_map/hqk,hqd->hkd/dot_general | solution.py:191
  458.3 30.9 %multiply_convert_fusion = bf16[4,1024,3072]{2,1,0:T(8,128)(2,1)} fusion(f32[4,1024,3072]{2,1,0:T(8,128)} %get-tuple-element.51, bf16[4,1024,72]{1,2,0:T(8,128)(2,1)S(1)} %bitcast.145, bf16[4,3072,72]{1,2,0:T(8,128)(2,1)} %bitcast.138, f32[4,1024]{1,0:T(4,128)S(1)} %multiply_reduce_fusion.2, f32[4,1024]{1,0:T(4,128)S(1)} %log_add_fusion, ...), kind=kOutput, calls=%fused_computation | convolution fusion | flops 1887436800 | bytes 81035264 | tf_op jit(solution)/shard_map/hqd,hkd->hqk/dot_general | solution.py:67
  489.2 12.9 %convolution_multiply_fusion = f32[4,3072,72]{1,2,0:T(8,128)} fusion(bf16[4,1024,3072]{2,1,0:T(8,128)(2,1)} %multiply_convert_fusion, f32[1024,4,72]{0,2,1:T(8,128)S(1)} %bitcast.130, f32[4,72]{1,0:T(4,128)S(1)} %copy-done.43), kind=kOutput, calls=%fused_computation.65 | convolution fusion | flops 1813413888 | bytes 29885568 | tf_op jit(solution)/shard_map/hqk,hqd->hkd/dot_general | solution.py:188
  512.1 8.8 fusion.110
  520.9 12.6 %convert_reduce_fusion.5 = (f32[4,72]{1,0:T(4,128)S(1)}, bf16[4,1024,72]{1,2,0:T(8,128)(2,1)S(1)}) fusion(bf16[4,1024,3072]{2,1,0:T(8,128)(2,1)} %multiply_convert_fusion, bf16[4,3072,72]{1,2,0:T(8,128)(2,1)S(1)} %bitcast.128), kind=kOutput, calls=%fused_computation.105 | convolution fusion | flops 1813118720 | bytes 27526272 | tf_op jit(solution)/shard_map/hqk,hkd->hqd/dot_general | solution.py:184
  542.9 195.2 %all-reduce.17.cloned.1.call-done = (f32[1024,1152]{1,0:T(8,128)}, f32[1024,1152]{1,0:T(8,128)}) async-done(((f32[1024,1152]{1,0:T(8,128)}, f32[1024,1152]{1,0:T(8,128)}), (f32[1024,1152]{1,0:T(8,128)}, f32[1024,1152]{1,0:T(8,128)})) %all-reduce.17.cloned.1.call-update) | async-done | bytes 9437200 | tf_op jit(solution)/shard_map/psum | solution.py:149
  759.0 52.2 %all-reduce.13.cloned.1.call-done = f32[16,6,288]{2,0,1:T(8,128)} async-done(((f32[16,6,288]{2,0,1:T(8,128)}), f32[16,6,288]{2,0,1:T(8,128)}) %all-reduce.13.cloned.1.call-update) | async-done | bytes 110608 | tf_op jit(solution)/shard_map/psum | solution.py:234
  820.5 8.0 fusion.125
  828.6 8.9 fusion.109
  838.5 7.5 fusion.71
  846.8 29.4 %all-reduce.1 = (f32[2,288]{1,0:T(2,128)}, f32[1152]{0:T(1024)}, f32[1152]{0:T(1024)}, f32[1152]{0:T(1024)}) all-reduce(f32[2,288]{1,0:T(2,128)S(1)} %pad_maximum_fusion.6, f32[1152]{0:T(1024)S(1)} %get-tuple-element.29, f32[1152]{0:T(1024)S(1)} %copy-done.46, f32[1152]{0:T(1024)S(1)} %copy-done.45), channel_id=1, replica_groups=mesh['seq'=8,'head'=4] {'seq'}, use_global_device_ids=true, to_apply=%region_20.21 | all-reduce | flops 4032 | bytes 32256 | tf_op jit(solution)/shard_map/psum | solution.py:234
  882.5 6.7 add_convert_fusion
  901.9 56.7 %reduce-scatter.9.cloned.1.call-done = f32[144,1152]{1,0:T(8,128)} async-done(((f32[1152,1152]{1,0:T(8,128)}), f32[144,1152]{1,0:T(8,128)}) %reduce-scatter.9.cloned.1.call-update) | async-done | bytes 663568 | tf_op jit(solution)/shard_map/reduce_scatter | solution.py:250
  958.6 61.8 %reduce-scatter.11.cloned.1.call-done = f32[1152,144]{0,1:T(8,128)} async-done(((f32[1152,1152]{0,1:T(8,128)}), f32[1152,144]{0,1:T(8,128)}) %reduce-scatter.11.cloned.1.call-update) | async-done | bytes 663568 | tf_op jit(solution)/shard_map/reduce_scatter | solution.py:251
  1020.4 61.8 %reduce-scatter.5.cloned.1.call-done = f32[144,3,288]{2,0,1:T(8,128)} async-done(((f32[1152,3,288]{2,0,1:T(8,128)}), f32[144,3,288]{2,0,1:T(8,128)}) %reduce-scatter.5.cloned.1.call-update) | async-done | bytes 497680 | tf_op jit(solution)/shard_map/reduce_scatter | solution.py:248
  (243 shorter events, 151.9 us)
Async XLA Ops:
  7.2 287.9 %copy-start = (bf16[1152,1152]{1,0:T(8,128)(2,1)S(1)}, bf16[1152,1152]{1,0:T(8,128)(2,1)}, u32[]{:S(2)}) copy-start(bf16[1152,1152]{1,0:T(8,128)(2,1)} %param.21) | copy-start | bytes 7962628
  7.2 276.7 %all-reduce.9.cloned.1.call-start = ((), (), s32[]{:S(2)}) async-start(), calls=%async_computation.4 | async-start | bytes 9437184 | tf_op jit(solution)/shard_map/psum | solution.py:139
  10.6 57.0 %copy-start.38 = (f32[1024]{0:T(1024)}, f32[1024]{0:T(1024)S(1)}, u32[]{:S(2)}) copy-start(f32[1024]{0:T(1024)S(1)} %broadcast_multiply_fusion.5) | copy-start | bytes 12292
  13.1 54.5 %copy-start.40 = (f32[1024]{0:T(1024)}, f32[1024]{0:T(1024)S(1)}, u32[]{:S(2)}) copy-start(f32[1024]{0:T(1024)S(1)} %add_rsqrt_fusion.1) | copy-start | bytes 12292
  76.1 7.4 collective-permute-start.1
  77.4 6.2 collective-permute-start
  159.5 262.4 %all-reduce.11.cloned.1.call-start = ((), (), s32[]{:S(2)}) async-start(), calls=%async_computation.5 | async-start | bytes 9437184 | tf_op jit(solution)/shard_map/psum | solution.py:166
  180.3 103.5 %copy-start.19 = (f32[16,1,1152]{0,1,2:T(1,128)S(1)}, f32[16,1,1152]{0,1,2:T(1,128)}, u32[]{:S(2)}) copy-start(f32[16,1,1152]{0,1,2:T(1,128)} %get-tuple-element.45) | copy-start | bytes 221188
  309.2 428.9 %all-reduce.17.cloned.1.call-start = ((), (), s32[]{:S(2)}) async-start(), calls=%async_computation.12 | async-start | bytes 18874368 | tf_op jit(solution)/shard_map/psum | solution.py:149
  309.3 118.9 %copy-start.8 = (bf16[1024,1152]{1,0:T(8,128)(2,1)S(1)}, bf16[1024,1152]{1,0:T(8,128)(2,1)}, u32[]{:S(2)}) copy-start(bf16[1024,1152]{1,0:T(8,128)(2,1)} %param.27) | copy-start | bytes 7077892
  507.6 25.9 %collective-permute-start.2 = (f32[1024,2,288]{0,2,1:T(8,128)}, f32[1024,2,288]{0,2,1:T(8,128)}, u32[]{:S(2)}, u32[]{:S(2)}) collective-permute-start(f32[1024,2,288]{0,2,1:T(8,128)} %get-tuple-element.38), channel_id=1, source_target_pairs={{0,4},{4,8},{8,12},{12,16},{16,20},{20,24},{24,28},{1,5},{5,9},{9,... | collective-permute-start | bytes 7077896 | tf_op jit(solution)/shard_map/ppermute | solution.py:22
  510.8 22.7 %collective-permute-start.3 = (f32[1024,2,288]{0,2,1:T(8,128)}, f32[1024,2,288]{0,2,1:T(8,128)}, u32[]{:S(2)}, u32[]{:S(2)}) collective-permute-start(f32[1024,2,288]{0,2,1:T(8,128)} %get-tuple-element.39), channel_id=1, source_target_pairs={{4,0},{8,4},{12,8},{16,12},{20,16},{24,20},{28,24},{5,1},{9,5},{13... | collective-permute-start | bytes 7077896 | tf_op jit(solution)/shard_map/ppermute | solution.py:24
  542.2 205.0 %slice-start.4 = ((s8[4718592]{0:T(1024)(128)(4,1)}), s8[524288]{0:T(1024)(128)(4,1)S(1)}, s32[]{:S(2)}) async-start(s8[4718592]{0:T(1024)(128)(4,1)} %bitcast.113), calls=%async_computation.17 | async-start | bytes 1048576
  542.3 200.1 %copy-start.4 = (bf16[1024,1152]{1,0:T(8,128)(2,1)S(1)}, bf16[1024,1152]{1,0:T(8,128)(2,1)}, u32[]{:S(2)}) copy-start(bf16[1024,1152]{1,0:T(8,128)(2,1)} %param.14) | copy-start | bytes 7077892
  542.3 200.1 %copy-start.39 = (f32[1024]{0:T(1024)S(1)}, f32[1024]{0:T(1024)}, u32[]{:S(2)}) copy-start(f32[1024]{0:T(1024)} %copy-done.38) | copy-start | bytes 12292
  542.3 200.1 %copy-start.41 = (f32[1024]{0:T(1024)S(1)}, f32[1024]{0:T(1024)}, u32[]{:S(2)}) copy-start(f32[1024]{0:T(1024)} %copy-done.40) | copy-start | bytes 12292
  542.3 268.8 %all-reduce.13.cloned.1.call-start = ((), (), s32[]{:S(2)}) async-start(), calls=%async_computation.6 | async-start | bytes 294912 | tf_op jit(solution)/shard_map/psum | solution.py:234
  755.9 60.2 %copy-start.27 = (bf16[4,1024,72]{1,2,0:T(8,128)(2,1)S(1)}, bf16[4,1024,72]{1,2,0:T(8,128)(2,1)}, u32[]{:S(2)}) copy-start(bf16[4,1024,72]{1,2,0:T(8,128)(2,1)} %copy-done.26) | copy-start | bytes 1769476
  758.9 141.4 %all-reduce.15.cloned.1.call-start = ((), (), s32[]{:S(2)}) async-start(), calls=%async_computation.7 | async-start | bytes 147456 | tf_op jit(solution)/shard_map/psum | solution.py:241
  815.8 86.1 %reduce-scatter.7.cloned.1.call-start = ((), (), s32[]{:S(2)}) async-start(), calls=%async_computation.9 | async-start | bytes 1990656 | tf_op jit(solution)/shard_map/reduce_scatter | solution.py:249
  820.5 138.1 %reduce-scatter.9.cloned.1.call-start = ((), (), s32[]{:S(2)}) async-start(), calls=%async_computation.10 | async-start | bytes 5971968 | tf_op jit(solution)/shard_map/reduce_scatter | solution.py:250
  828.6 191.8 %reduce-scatter.11.cloned.1.call-start = ((), (), s32[]{:S(2)}) async-start(), calls=%async_computation.11 | async-start | bytes 5971968 | tf_op jit(solution)/shard_map/reduce_scatter | solution.py:251
  837.5 244.7 %reduce-scatter.5.cloned.1.call-start = ((), (), s32[]{:S(2)}) async-start(), calls=%async_computation.8 | async-start | bytes 5971968 | tf_op jit(solution)/shard_map/reduce_scatter | solution.py:248
  889.2 192.9 %copy-start.1 = (bf16[1152,1152]{1,0:T(8,128)(2,1)S(1)}, bf16[1152,1152]{1,0:T(8,128)(2,1)}, u32[]{:S(2)}) copy-start(bf16[1152,1152]{1,0:T(8,128)(2,1)} %param.21) | copy-start | bytes 7962628
  (61 other events, 436.2 us)
Sparse Core Ops, SparseCore 0:
  159.6 124.2 all-reduce.8
  309.4 112.4 all-reduce.10
  542.4 195.7 all-reduce.16
  759.0 52.0 all-reduce.12
  815.9 41.9 all-reduce.14
  860.7 36.2 reduce-scatter.6
  899.9 58.6 reduce-scatter.8
  961.5 58.8 reduce-scatter.10
  1023.3 58.8 reduce-scatter.4
where the time goes:
time: 1100 us; the launch traced here: 1090 us
  waiting for transfers between devices  639 us (58%)
  matrix products  243 us (22%)
  other arithmetic  80.6 us (7%)
  blocking collectives  75.2 us (7%)
  starting transfers between devices  20.1 us (2%)
  local copies, waits for them, and re-layouts  16.2 us (1%)
  between operations  15.3 us (1%)
    psum x1, waiting for transfers between devices, on_device(): lax.psum(jnp.dot(act_low, down_weight, preferred_element_type=jnp.float32...  195 us
    psum x1, waiting for transfers between devices, on_device(): lax.psum(jnp.dot(grad_pre, up_weight.T, preferred_element_type=jnp.float3...  113 us
    psum x1, waiting for transfers between devices, on_device(): lax.psum(jnp.dot(attended_low, out_weight, preferred_element_type=jnp.flo...  98.4 us
    reduce_scatter x1, waiting for transfers between devices, on_device(): lax.psum_scatter(grad_qkv_weight, 'seq', scatter_dimension=0, tiled=True)  61.8 us
    reduce_scatter x1, waiting for transfers between devices, on_device(): lax.psum_scatter(grad_down_weight, 'seq', scatter_dimension=1, tiled=True)  61.8 us
    reduce_scatter x1, waiting for transfers between devices, on_device(): lax.psum_scatter(grad_up_weight, 'seq', scatter_dimension=0, tiled=True)  56.7 us
    psum x1, waiting for transfers between devices, on_device(): lax.psum((grad_mod_mine, grad_qv_bias, grad_up_bias, grad_out_bias, grad_...  52.2 us
    all_gather x1, blocking collectives, on_device(): modulation = lax.all_gather(mod_mine, 'head', axis=2, tiled=True)  45.7 us
  transfers between devices with their start and end apart: 13, of which 7 were waited for; matrix products, arithmetic and copies ran while one was open for 8% of the time, Pallas kernels for 0%

commit v1 on v0

v1 whole, which is shorter than its diff:
```python
import jax
import jax.numpy as jnp
from jax import lax
from jax.sharding import PartitionSpec as P

HDIM = 72


EPSILON = 1e-06
MASKED = -1e30
PRECISE = lax.Precision.HIGHEST
CHUNKS = 2


def peers(axis):
    return range(1, lax.axis_size(axis))


def swap(value, axis, mask):
    count = lax.axis_size(axis)
    return lax.ppermute(value, axis, [(i, i ^ mask) for i in range(count)])


def gather_pieces(value, axis):
    return [value] + [swap(value, axis, mask) for mask in peers(axis)]


def trade_pieces(blocks, axis):
    me = lax.axis_index(axis)
    own = lax.dynamic_index_in_dim(blocks, me, 0, keepdims=False)
    return [own] + [
        swap(lax.dynamic_index_in_dim(blocks, me ^ mask, 0, keepdims=False), axis, mask)
        for mask in peers(axis)
    ]


def place_pieces(pieces, axis, dim=0):
    me = lax.axis_index(axis)
    width = pieces[0].shape[dim]
    shape = list(pieces[0].shape)
    shape[dim] = width * len(pieces)
    result = jnp.zeros(shape, pieces[0].dtype)
    for mask, piece in enumerate(pieces):
        result = lax.dynamic_update_slice_in_dim(result, piece, (me ^ mask) * width, dim)
    return result


def butterfly_sum(value, axis):
    mask = 1
    while mask < lax.axis_size(axis):
        value = value + swap(value, axis, mask)
        mask *= 2
    return value


def three_parts(values):
    first = lax.reduce_precision(values, 8, 7)
    second = lax.reduce_precision(values - first, 8, 7)
    third = values - first - second
    return [part.astype(jnp.bfloat16) for part in (first, second, third)]


def image_sums(one_hot_low, values):
    first = lax.reduce_precision(values, 8, 7)
    second = (values - first).astype(jnp.bfloat16)
    return sum(
        lax.dot_general(
            one_hot_low, part, (((0,), (0,)), ((), ())), preferred_element_type=jnp.float32
        )
        for part in (first.astype(jnp.bfloat16), second)
    )


def extended(cells, sides, width):
    for axis, dim in sides:
        count = lax.axis_size(axis)
        ends = count - 1
        head = lax.slice_in_dim(cells, 0, width, axis=dim)
        tail = lax.slice_in_dim(cells, cells.shape[dim] - width, cells.shape[dim], axis=dim)
        cells = jnp.concatenate(
            [
                lax.ppermute(tail, axis, [(i, (i + 1) % count) for i in range(ends)]),
                cells,
                lax.ppermute(head, axis, [((i + 1) % count, i) for i in range(ends)]),
            ],
            axis=dim,
        )
    return cells


def normalize(values):
    center = values - jnp.mean(values, axis=-1, keepdims=True)
    inverse = lax.rsqrt(jnp.mean(center * center, axis=-1, keepdims=True) + EPSILON)
    return (center * inverse, inverse)


def norm_back(gradient, normed, inverse):
    return (
        gradient
        - jnp.mean(gradient, axis=-1, keepdims=True)
        - normed * jnp.mean(gradient * normed, axis=-1, keepdims=True)
    ) * inverse


def gelu_tanh(values):
    return jax.nn.gelu(values, approximate=True)


def split_heads(matrix, head_count):
    amount = matrix.shape[0]
    return matrix.reshape(amount, head_count, -1).transpose(1, 0, 2)


def join_heads(tensor):
    head_count, amount, head_size = tensor.shape
    return tensor.transpose(1, 0, 2).reshape(amount, head_count * head_size)


def score_grads(
    query_heads, grad_heads, key_heads, value_heads, visible, log_total, delta, scaling
):
    scores = (
        jnp.einsum("hqd,hkd->hqk", query_heads, key_heads, preferred_element_type=jnp.float32)
        * scaling
    )
    shares = jnp.where(visible, jnp.exp(scores - log_total[..., None]), 0.0)
    grad_shares = jnp.einsum(
        "hqd,hkd->hqk", grad_heads, value_heads, preferred_element_type=jnp.float32
    )
    grad_scores = (shares * (grad_shares - delta[..., None])).astype(jnp.bfloat16)
    return (shares.astype(jnp.bfloat16), grad_scores)


def on_device(
    tokens,
    conditioning,
    image_index,
    qkv_weight,
    qv_bias,
    out_weight,
    out_bias,
    up_weight,
    up_bias,
    down_weight,
    down_bias,
    ada_weight,
    ada_bias,
    cotangent,
):
    row_count, width = tokens.shape
    feature_count = qkv_weight.shape[2]
    head_count = feature_count // HDIM
    scaling = HDIM ** (-0.5)
    head_size = lax.axis_size("head")
    me = lax.axis_index("head")
    chunk_rows = row_count // CHUNKS
    own_rows = chunk_rows // head_size
    my_index = lax.axis_index("seq")
    my_images = lax.dynamic_slice_in_dim(image_index, my_index * row_count, row_count, 0)
    padded_images = jnp.pad(image_index, (row_count, row_count), constant_values=-1)
    wide_images = lax.dynamic_slice_in_dim(padded_images, my_index * row_count, 3 * row_count, 0)
    image_count = conditioning.shape[0]
    one_hot = (
        my_images[:, None] == jnp.arange(image_count, dtype=jnp.int32)[None, :]
    ).astype(jnp.bfloat16)

    def chunk_of(values, c):
        return lax.slice_in_dim(values, c * chunk_rows, (c + 1) * chunk_rows, axis=0)

    def own_of(values, c):
        return lax.dynamic_slice_in_dim(values, c * chunk_rows + me * own_rows, own_rows, 0)

    def own_all(values):
        return jnp.concatenate([own_of(values, c) for c in range(CHUNKS)], axis=0)

    cond_float = conditioning.astype(jnp.float32)
    cond_act = jax.nn.silu(cond_float).astype(jnp.bfloat16)
    mod_mine = jnp.einsum("id,dkf->ikf", cond_act, ada_weight, preferred_element_type=jnp.float32)
    mod_mine = mod_mine + ada_bias.astype(jnp.float32)[None]
    modulation = place_pieces(gather_pieces(mod_mine, "head"), "head", 2)
    out_full = jnp.stack(gather_pieces(out_weight, "head"))
    hot_three = jnp.concatenate([one_hot] * 3, axis=1)

    def per_row(hot, component):
        return jnp.dot(
            hot,
            jnp.concatenate(three_parts(modulation[:, component]), axis=0),
            preferred_element_type=jnp.float32,
        )

    shift_one, scale_one, gate_one, shift_two, scale_two, gate_two = [
        per_row(hot_three, component) for component in range(6)
    ]
    inputs = tokens.astype(jnp.float32)
    normed_one, inverse_one = normalize(inputs)
    hidden_one = (normed_one * (1.0 + scale_one) + shift_one).astype(jnp.bfloat16)
    projected = jnp.einsum(
        "td,dkf->tkf", hidden_one, qkv_weight, preferred_element_type=jnp.float32
    )
    bias_rows = qv_bias.astype(jnp.float32)
    query_low = (projected[:, 0] + bias_rows[0]).astype(jnp.bfloat16)
    key_low = projected[:, 1].astype(jnp.bfloat16)
    value_low = (projected[:, 2] + bias_rows[1]).astype(jnp.bfloat16)
    key_value = jnp.stack([key_low, value_low], axis=1)
    query_heads = split_heads(query_low, head_count)
    wide_kv = extended(key_value, (("seq", 0),), row_count)

    grad_out = cotangent.astype(jnp.float32)
    grad_mlp = (gate_two * grad_out).astype(jnp.bfloat16)
    grad_down_bias = jnp.sum(grad_mlp.astype(jnp.float32), axis=0)
    grad_act = jnp.dot(grad_mlp, down_weight.T, preferred_element_type=jnp.float32)

    wide_keys = split_heads(wide_kv[:, 0], head_count)
    wide_values = split_heads(wide_kv[:, 1], head_count)
    visible = (my_images[:, None] == wide_images[None, :])[None]
    scores = (
        jnp.einsum("hqd,hkd->hqk", query_heads, wide_keys, preferred_element_type=jnp.float32)
        * scaling
    )
    scores = jnp.where(visible, scores, MASKED)
    row_max = jnp.max(scores, axis=-1)
    weights = jnp.where(visible, jnp.exp(scores - row_max[..., None]), 0.0)
    row_total = jnp.sum(weights, axis=-1)
    log_total = row_max + jnp.log(row_total)
    shares = (weights / row_total[..., None]).astype(jnp.bfloat16)
    attended = jnp.einsum("hqk,hkd->hqd", shares, wide_values, preferred_element_type=jnp.float32)
    attended_low = join_heads(attended).astype(jnp.bfloat16)

    hidden_two, act_low, grad_pre = [], [], []
    mlp_parts, hidden_parts = [], []
    attn_own, middle_own, normed_own, inverse_own = [], [], [], []
    late_sums = []
    for c in range(CHUNKS):
        pieces = gather_pieces(chunk_of(attended_low, c), "head")
        attn_branch = sum(
            jnp.dot(piece, out_full[m], preferred_element_type=jnp.float32)
            for m, piece in enumerate(pieces)
        ) + out_bias.astype(jnp.float32)
        middle = chunk_of(inputs, c) + chunk_of(gate_one, c) * attn_branch
        normed_two, inverse_two = normalize(middle)
        hidden = (
            normed_two * (1.0 + chunk_of(scale_two, c)) + chunk_of(shift_two, c)
        ).astype(jnp.bfloat16)
        pre_act = jnp.dot(
            hidden, up_weight, preferred_element_type=jnp.float32
        ) + up_bias.astype(jnp.float32)
        act, gelu_pull = jax.vjp(gelu_tanh, pre_act)
        grad_p = gelu_pull(chunk_of(grad_act, c))[0].astype(jnp.bfloat16)
        part = jnp.dot(grad_p, up_weight.T, preferred_element_type=jnp.float32)
        hidden_parts.append(
            trade_pieces(
                part.astype(jnp.bfloat16).reshape(head_size, own_rows, width), "head"
            )
        )
        act = act.astype(jnp.bfloat16)
        mlp_part = jnp.dot(act, down_weight, preferred_element_type=jnp.float32)
        mlp_parts.append(
            trade_pieces(
                mlp_part.astype(jnp.bfloat16).reshape(head_size, own_rows, width), "head"
            )
        )
        hot = chunk_of(one_hot, c)
        late_sums.append(
            [
                image_sums(hot, part),
                image_sums(hot, part * normed_two),
                image_sums(hot, chunk_of(grad_out, c) * mlp_part),
            ]
        )
        hidden_two.append(hidden)
        act_low.append(act)
        grad_pre.append(grad_p)

        def mine(values):
            return lax.dynamic_slice_in_dim(values, me * own_rows, own_rows, 0)

        attn_own.append(mine(attn_branch))
        middle_own.append(mine(middle))
        normed_own.append(mine(normed_two))
        inverse_own.append(mine(inverse_two))
    hidden_two = jnp.concatenate(hidden_two, axis=0)
    act_low = jnp.concatenate(act_low, axis=0)
    grad_pre = jnp.concatenate(grad_pre, axis=0)

    grad_middle_own, grad_attended_rows, grad_attn_rows = [], [], []
    gate_sums, grad_out_bias = 0.0, 0.0
    for c in range(CHUNKS):
        grad_hidden_two = sum(piece.astype(jnp.float32) for piece in hidden_parts[c])
        grad_middle = own_of(grad_out, c) + norm_back(
            grad_hidden_two * (1.0 + own_of(scale_two, c)), normed_own[c], inverse_own[c]
        )
        grad_attn = (own_of(gate_one, c) * grad_middle).astype(jnp.bfloat16)
        blocks = jnp.stack(
            [
                lax.dot_general(
                    grad_attn,
                    out_full[m],
                    (((1,), (1,)), ((), ())),
                    preferred_element_type=jnp.float32,
                ).astype(jnp.bfloat16)
                for m in range(head_size)
            ]
        )
        got = [blocks[0]] + [swap(blocks[m], "head", m) for m in peers("head")]
        grad_attended_rows.append(place_pieces(got, "head", 0))
        grad_attn_rows.append(place_pieces(gather_pieces(grad_attn, "head"), "head", 0))
        grad_middle_own.append(grad_middle)
        gate_sums = gate_sums + image_sums(own_of(one_hot, c), grad_middle * attn_own[c])
        grad_out_bias = grad_out_bias + jnp.sum(grad_attn.astype(jnp.float32), axis=0)
    grad_attended = jnp.concatenate(grad_attended_rows, axis=0)
    grad_attn = jnp.concatenate(grad_attn_rows, axis=0)

    grad_heads = split_heads(grad_attended, head_count)
    delta = jnp.sum(grad_heads.astype(jnp.float32) * attended, axis=-1)
    shares_low, grad_scores = score_grads(
        query_heads, grad_heads, wide_keys, wide_values, visible, log_total, delta, scaling
    )
    grad_query_heads = (
        jnp.einsum("hqk,hkd->hqd", grad_scores, wide_keys, preferred_element_type=jnp.float32)
        * scaling
    )
    grad_keys_wide = (
        jnp.einsum("hqk,hqd->hkd", grad_scores, query_heads, preferred_element_type=jnp.float32)
        * scaling
    )
    grad_values_wide = jnp.einsum(
        "hqk,hqd->hkd", shares_low, grad_heads, preferred_element_type=jnp.float32
    )
    grad_wide = jnp.stack([join_heads(grad_keys_wide), join_heads(grad_values_wide)], axis=1)
    outward = jnp.concatenate(
        [grad_wide[:row_count], grad_wide[2 * row_count :]], axis=0
    ).astype(jnp.bfloat16)
    inward = extended(outward, (("seq", 0),), row_count)
    grad_kv_mine = (
        grad_wide[row_count : 2 * row_count]
        + inward[:row_count].astype(jnp.float32)
        + inward[3 * row_count :].astype(jnp.float32)
    )
    grad_key_low = grad_kv_mine[:, 0].astype(jnp.bfloat16)
    grad_value_low = grad_kv_mine[:, 1].astype(jnp.bfloat16)
    grad_query_low = join_heads(grad_query_heads).astype(jnp.bfloat16)
    grad_qkv = jnp.stack([grad_query_low, grad_key_low, grad_value_low], axis=1)
    grad_qv_bias = jnp.stack(
        [
            jnp.sum(grad_query_low.astype(jnp.float32), axis=0),
            jnp.sum(grad_value_low.astype(jnp.float32), axis=0),
        ]
    )

    one_parts = []
    first_sums = []
    for c in range(CHUNKS):
        part = jnp.einsum(
            "tkf,dkf->td", chunk_of(grad_qkv, c), qkv_weight, preferred_element_type=jnp.float32
        )
        one_parts.append(
            trade_pieces(
                part.astype(jnp.bfloat16).reshape(head_size, own_rows, width), "head"
            )
        )
        hot = chunk_of(one_hot, c)
        first_sums.append(
            [image_sums(hot, part), image_sums(hot, part * chunk_of(normed_one, c))]
        )
    token_rows, out_rows = [], []
    for c in range(CHUNKS):
        grad_hidden_one = sum(piece.astype(jnp.float32) for piece in one_parts[c])
        rows = grad_middle_own[c] + norm_back(
            grad_hidden_one * (1.0 + own_of(scale_one, c)),
            own_of(normed_one, c),
            own_of(inverse_one, c),
        )
        token_rows.append(
            place_pieces(gather_pieces(rows.astype(jnp.bfloat16), "head"), "head", 0)
        )
        mlp_branch = sum(
            piece.astype(jnp.float32) for piece in mlp_parts[c]
        ) + down_bias.astype(jnp.float32)
        rows = (middle_own[c] + own_of(gate_two, c) * mlp_branch).astype(jnp.bfloat16)
        out_rows.append(place_pieces(gather_pieces(rows, "head"), "head", 0))
    grad_tokens = jnp.concatenate(token_rows, axis=0).astype(jnp.float32)
    layer_out = jnp.concatenate(out_rows, axis=0)

    columns = ada_weight.shape[2]

    def to_owners(values):
        amount = values.shape[0]
        blocks = values.reshape(amount, head_size, columns).transpose(1, 0, 2)
        return sum(trade_pieces(blocks, "head"))

    late = [sum(values) for values in zip(*late_sums)]
    late_mine = to_owners(
        jnp.concatenate([gate_sums] + late + [grad_out_bias[None]], axis=0)
    )
    bias_sums = jnp.dot(one_hot.T, cotangent, preferred_element_type=jnp.float32)
    bias_sums = bias_sums * down_bias.astype(jnp.float32)
    bias_sums = lax.dynamic_slice_in_dim(bias_sums, me * columns, columns, 1)
    late_mine = lax.dynamic_update_slice_in_dim(
        late_mine,
        lax.slice_in_dim(late_mine, 3 * image_count, 4 * image_count, axis=0) + bias_sums,
        3 * image_count,
        0,
    )
    grad_up_bias = jnp.sum(grad_pre.astype(jnp.float32), axis=0)
    low_bias = jnp.concatenate([grad_up_bias, grad_down_bias])
    late_mine = butterfly_sum(late_mine, "seq")
    low_bias = butterfly_sum(low_bias, "seq")
    grad_up_bias, grad_down_bias = jnp.split(low_bias, [grad_up_bias.shape[0]])
    first = [sum(values) for values in zip(*first_sums)]
    first_mine = to_owners(jnp.concatenate(first, axis=0))
    first_mine = butterfly_sum(jnp.concatenate([first_mine, grad_qv_bias], axis=0), "seq")
    grad_qv_bias = first_mine[2 * image_count :]
    grad_mod = jnp.stack(
        [
            first_mine[:image_count],
            first_mine[image_count : 2 * image_count],
            late_mine[:image_count],
            late_mine[image_count : 2 * image_count],
            late_mine[2 * image_count : 3 * image_count],
                late_mine[3 * image_count : 4 * image_count],
        ],
        axis=1,
    )
    grad_ada_bias = jnp.sum(grad_mod, axis=0)
    grad_ada_weight = jnp.einsum(
        "id,ikf->dkf", cond_act.astype(jnp.float32), grad_mod, precision=PRECISE
    )
    grad_cond_act = jnp.einsum(
        "ikf,dkf->id", grad_mod, ada_weight.astype(jnp.float32), precision=PRECISE
    )
    spread_bias = lax.dynamic_update_slice(
        jnp.zeros((1, width), jnp.float32), late_mine[4 * image_count :], (0, me * columns)
    )
    last = butterfly_sum(jnp.concatenate([grad_cond_act, spread_bias], axis=0), "head")
    _, silu_pull = jax.vjp(jax.nn.silu, cond_float)
    grad_conditioning = silu_pull(last[:image_count])[0]
    grad_out_bias = last[image_count]

    def weight_sum(parts):
        low = [part.astype(jnp.bfloat16) for part in parts]
        total = lax.psum_scatter(
            jnp.concatenate(low, axis=1), "seq", scatter_dimension=0, tiled=True
        ).astype(jnp.float32)
        cuts = [part.shape[1] for part in parts]
        result, place = [], 0
        for cut in cuts:
            result.append(lax.slice_in_dim(total, place, place + cut, axis=1))
            place += cut
        return result

    def outer(left, right):
        return lax.dot_general(
            left, right, (((0,), (0,)), ((), ())), preferred_element_type=jnp.float32
        )

    grad_up_weight, grad_down_weight = weight_sum(
        [outer(hidden_two, grad_pre), outer(grad_mlp, act_low)]
    )
    grad_out_weight, grad_qkv_weight = weight_sum(
        [
            outer(grad_attn, attended_low),
            outer(hidden_one, grad_qkv.reshape(row_count, 3 * feature_count)),
        ]
    )
    return (
        layer_out,
        grad_tokens,
        grad_conditioning,
        grad_qkv_weight.reshape(-1, 3, feature_count),
        grad_qv_bias,
        grad_out_weight.T,
        grad_out_bias,
        grad_up_weight,
        grad_up_bias,
        grad_down_weight.T,
        grad_down_bias,
        grad_ada_weight,
        grad_ada_bias,
    )


def solution(mesh):
    placed = (
        P("seq", None),
        P(),
        P(),
        P(None, None, "head"),
        P(None, "head"),
        P("head", None),
        P(),
        P(None, "head"),
        P("head"),
        P("head", None),
        P(),
        P(None, None, "head"),
        P(None, "head"),
        P("seq", None),
    )
    return jax.shard_map(
        on_device,
        mesh=mesh,
        in_specs=placed,
        out_specs=(
            P("seq", None),
            P("seq", None),
            P(),
            P("seq", None, "head"),
            P(None, "head"),
            P("head", "seq"),
            P(),
            P("seq", "head"),
            P("head"),
            P("head", "seq"),
            P(),
            P(None, None, "head"),
            P(None, "head"),
        ),
        check_vma=False,
    )
```

time: 1100 us -> 650 us (0.59)
  waiting for transfers between devices: 639 us -> 110 us
  starting transfers between devices: 20.1 us -> 109 us
  blocking collectives: 75.2 us -> 0 us
  local copies, waits for them, and re-layouts: 16.2 us -> 76.3 us
    psum x5 -> x0, waiting for transfers between devices: 458 us -> none  [the longest x1 195 us: on_device(): lax.psum(jnp.dot(act_low, down_weight, preferred_element_type=jnp.float32...]
    reduce_scatter x4 -> x0, waiting for transfers between devices: 180 us -> none  [the longest x1 61.8 us: on_device(): lax.psum_scatter(grad_qkv_weight, 'seq', scatter_dimension=0, tiled=True)]
    ppermute x0 -> x71, waiting for transfers between devices: none -> 110 us  [swap(): return lax.ppermute(value, axis, [(i, i ^ mask) for i in range(count)])]
    ppermute x0 -> x71, starting transfers between devices: none -> 102 us  [swap(): return lax.ppermute(value, axis, [(i, i ^ mask) for i in range(count)])]
    all_gather x1 -> x0, blocking collectives: 45.7 us -> none  [on_device(): modulation = lax.all_gather(mod_mine, 'head', axis=2, tiled=True)]
    unnamed x144 -> x257, local copies, waits for them, and re-layouts: 8.39 us -> 42.2 us
    psum x1 -> x0, blocking collectives: 29.4 us -> none  [on_device(): lax.psum((grad_mod_mine, grad_qv_bias, grad_up_bias, grad_out_bias, grad_...]
    dynamic_update_slice x0 -> x29, local copies, waits for them, and re-layouts: none -> 17.2 us  [the longest x28 17.1 us: place_pieces(): lax.dynamic_update_slice_in_dim(result, piece, (me ^ mask) * width, dim)]
  transfers between devices with their start and end apart: 13 -> 77, of which waited for: 7 -> 33; matrix products, arithmetic and copies ran while one was open for 8% -> 56% of each run, Pallas kernels for 0% -> 0%
where the time goes in v1:
time: 650 us; the launch traced here: 644 us
  matrix products  247 us (38%)
  waiting for transfers between devices  110 us (17%)
  starting transfers between devices  109 us (17%)
  other arithmetic  86.6 us (13%)
  local copies, waits for them, and re-layouts  76.3 us (12%)
  between operations  16.3 us (3%)
    ppermute x71, waiting for transfers between devices, swap(): return lax.ppermute(value, axis, [(i, i ^ mask) for i in range(count)])  110 us
    ppermute x71, starting transfers between devices, swap(): return lax.ppermute(value, axis, [(i, i ^ mask) for i in range(count)])  102 us
    unnamed x257, local copies, waits for them, and re-layouts  42.2 us
    dot_general x1, matrix products, on_device(): jnp.einsum('hqk,hkd->hqd', shares, wide_values, preferred_element_type=jn...  31 us
    dot_general x1, matrix products, score_grads(): jnp.einsum('hqd,hkd->hqk', grad_heads, value_heads, preferred_element_typ...  30.7 us
    reduce_sum x1, other arithmetic, on_device(): row_total = jnp.sum(weights, axis=-1)  24.3 us
    dot_general x8, matrix products, on_device(): jnp.dot(piece, out_full[m], preferred_element_type=jnp.float32)  23.6 us
    dot_general x1, matrix products, on_device(): jnp.einsum('hqk,hqd->hkd', shares_low, grad_heads, preferred_element_type...  21.1 us
  transfers between devices with their start and end apart: 77, of which 33 were waited for; matrix products, arithmetic and copies ran while one was open for 56% of the time, Pallas kernels for 0%

profile of v1, /device:TPU:0, one launch (start us, length us, event | category | flops | bytes accessed | tf_op | source)
XLA Modules:
  0.0 644.4 jit_solution(16563475495224698541)
XLA Ops:
  76.1 5.2 fusion.261
  84.3 19.9 %select_reduce_fusion = (f32[4,1024]{1,0:T(4,128)S(1)}, f32[4,1024,3072]{2,1,0:T(8,128)}) fusion(pred[1024,3072]{1,0:T(8,128)(4,1)S(1)} %copy-done.22, bf16[4,3072,72]{1,2,0:T(8,128)(2,1)S(1)} %bitcast.315, f32[1024,4,72]{0,2,1:T(8,128)S(1)} %bitcast.317, f32[4,72]{1,0:T(4,128)S(1)} %add.557), kind=kOutput, calls=%fused_computation.4 | convolution fusion | flops 1850273792 | bytes 56444032 | tf_op jit(solution)/shard_map/hqd,hkd->hqk/dot_general | solution.py:217
  104.2 24.3 %fusion.1 = f32[4,1024]{1,0:T(4,128)S(1)} fusion(f32[4,1024,3072]{2,1,0:T(8,128)} %get-tuple-element.147, f32[4,1024]{1,0:T(4,128)S(1)} %get-tuple-element.146, pred[1024,3072]{1,0:T(8,128)(4,1)} %broadcast_compare_fusion), kind=kLoop, calls=%fused_computation.6 | loop fusion | flops 62910464 | bytes 53510144 | tf_op jit(solution)/shard_map/reduce_sum | solution.py:223
  128.5 31.0 %fusion.250 = (bf16[4,1024,72]{1,2,0:T(8,128)(2,1)S(1)}, f32[4,1024,72]{1,2,0:T(8,128)}) fusion(bf16[4,3072,72]{1,2,0:T(8,128)(2,1)} %bitcast.324, f32[4,1024,3072]{2,1,0:T(8,128)} %get-tuple-element.147, f32[4,1024]{1,0:T(4,128)S(1)} %fusion.1, f32[4,1024]{1,0:T(4,128)S(1)} %get-tuple-element.146, pred[1024,3072]{1,0:T(8,128)(4,1)} %broadcast_compare_fusion), kind=kOutput, calls=%fused_computation.497 | convolution fusion | flops 1887731712 | bytes 57049088 | tf_op jit(solution)/shard_map/hqk,hkd->hqd/dot_general | solution.py:226
  168.9 5.2 collective-permute-done.17
  184.0 10.3 %collective-permute-done.18 = bf16[512,288]{0,1:T(8,128)(2,1)S(1)} collective-permute-done((bf16[512,288]{0,1:T(8,128)(2,1)S(1)}, bf16[512,288]{0,1:T(8,128)(2,1)S(1)}, u32[]{:S(2)}, u32[]{:S(2)}) %collective-permute-start.18) | collective-permute-done | bytes 294944 | tf_op jit(solution)/shard_map/ppermute | solution.py:21
  195.3 4.8 convolution_add_fusion.4
  204.4 5.9 fusion.239
  215.6 6.8 %fusion.18 = (bf16[512,1152]{1,0:T(8,128)(2,1)S(1)}, bf16[512,1152]{1,0:T(8,128)(2,1)S(1)}, bf16[512,1152]{1,0:T(8,128)(2,1)}, bf16[512,1152]{1,0:T(8,128)(2,1)S(1)}) fusion(f32[1024,1152]{1,0:T(8,128)S(1)} %bitcast.356, f32[512,1152]{1,0:T(8,128)S(1)} %convolution_add_fusion.5, f32[1152]{0:T(1024)S(1)} %copy-done.88, ...), kind=kOutput, calls=%fused_computation.73 | convolution fusion | flops 1385496576 | bytes 15634944 | tf_op jit(solution)/shard_map/dot_general | solution.py:244
  246.3 8.4 %collective-permute-done.33 = bf16[128,1152]{1,0:T(8,128)(2,1)S(1)} collective-permute-done((bf16[128,1152]{1,0:T(8,128)(2,1)S(1)}, bf16[128,1152]{1,0:T(8,128)(2,1)S(1)}, u32[]{:S(2)}, u32[]{:S(2)}) %collective-permute-start.33) | collective-permute-done | bytes 294944 | tf_op jit(solution)/shard_map/ppermute | solution.py:21
  299.7 21.1 %fusion.2 = f32[4,3072,72]{1,2,0:T(8,128)} fusion(bf16[4,1024,72]{1,2,0:T(8,128)(2,1)S(1)} %bitcast.322, f32[4,1024,3072]{2,1,0:T(8,128)} %get-tuple-element.147, f32[4,1024]{1,0:T(4,128)S(1)} %copy-done.83, pred[1024,3072]{1,0:T(8,128)(4,1)} %broadcast_compare_fusion), kind=kOutput, calls=%fused_computation.7 | convolution fusion | flops 1862270976 | bytes 57622528 | tf_op jit(solution)/shard_map/hqk,hqd->hkd/dot_general | solution.py:326
  320.8 30.7 %multiply_convert_fusion = bf16[4,1024,3072]{2,1,0:T(8,128)(2,1)} fusion(f32[4,1024,3072]{2,1,0:T(8,128)} %get-tuple-element.147, bf16[4,1024,72]{1,2,0:T(8,128)(2,1)S(1)} %bitcast.323, bf16[4,3072,72]{1,2,0:T(8,128)(2,1)} %bitcast.325, f32[4,1024]{1,0:T(4,128)S(1)} %multiply_reduce_fusion.3, f32[4,1024]{1,0:T(4,128)S(1)} %copy-done.83, ...), kind=kOutput, calls=%fused_computation | convolution fusion | flops 1887436800 | bytes 81035264 | tf_op jit(solution)/shard_map/hqd,hkd->hqk/dot_general | solution.py:127
  351.5 13.1 %convert_reduce_fusion.4 = (f32[4,72]{1,0:T(4,128)}, bf16[4,1024,72]{1,2,0:T(8,128)(2,1)S(1)}) fusion(bf16[4,1024,3072]{2,1,0:T(8,128)(2,1)} %multiply_convert_fusion, bf16[4,3072,72]{1,2,0:T(8,128)(2,1)S(1)} %bitcast.316), kind=kOutput, calls=%fused_computation.170 | convolution fusion | flops 1813118720 | bytes 27526272 | tf_op jit(solution)/shard_map/hqk,hkd->hqd/dot_general | solution.py:319
  364.7 12.6 %convolution_multiply_fusion = f32[4,3072,72]{1,2,0:T(8,128)} fusion(bf16[4,1024,3072]{2,1,0:T(8,128)(2,1)} %multiply_convert_fusion, f32[1024,4,72]{0,2,1:T(8,128)} %bitcast.318, f32[4,72]{1,0:T(4,128)S(1)} %copy-done.81), kind=kOutput, calls=%fused_computation.24 | convolution fusion | flops 1813413888 | bytes 29885568 | tf_op jit(solution)/shard_map/hqk,hqd->hkd/dot_general | solution.py:323
  404.9 5.3 copy.35
  437.6 10.2 %collective-permute-start.73 = (f32[2304]{0:T(1024)S(1)}, f32[2304]{0:T(1024)S(1)}, u32[]{:S(2)}, u32[]{:S(2)}) collective-permute-start(f32[2304]{0:T(1024)S(1)} %fusion.328), channel_id=1, source_target_pairs={{0,8},{4,12},{8,0},{12,4},{16,24},{20,28},{24,16},{28,20},{1,9},{5... | collective-permute-start | bytes 27656 | tf_op jit(solution)/shard_map/ppermute | solution.py:21
  454.2 8.7 %copy.37 = bf16[1152,2304]{1,0:T(8,128)(2,1)} copy(bf16[1152,2304]{0,1:T(8,128)(2,1)} %pad_maximum_fusion.1) | data formatting | bytes 10616832
  480.1 6.8 %collective-permute-done.59 = f32[65,288]{1,0:T(8,128)S(1)} collective-permute-done((f32[65,288]{1,0:T(8,128)S(1)}, f32[65,288]{1,0:T(8,128)S(1)}, u32[]{:S(2)}, u32[]{:S(2)}) %collective-permute-start.59) | collective-permute-done | bytes 74912 | tf_op jit(solution)/shard_map/ppermute | solution.py:21
  512.4 5.7 collective-permute-start.63
  564.4 5.7 fusion.178
  579.6 11.8 %collective-permute-done.41 = bf16[128,1152]{1,0:T(8,128)(2,1)S(1)} collective-permute-done((bf16[128,1152]{1,0:T(8,128)(2,1)S(1)}, bf16[128,1152]{1,0:T(8,128)(2,1)S(1)}, u32[]{:S(2)}, u32[]{:S(2)}) %collective-permute-start.41) | collective-permute-done | bytes 294944 | tf_op jit(solution)/shard_map/ppermute | solution.py:21
  607.5 5.2 collective-permute-done.44
  612.9 4.7 collective-permute-done.49
  617.6 4.8 collective-permute-done.50
  (623 shorter events, 359.7 us)
Async XLA Ops:
  7.2 617.9 %reduce-scatter.7.cloned.1.call-start = ((), (), s32[]{:S(2)}) async-start(), calls=%async_computation.2 | async-start | bytes 2985984
  11.6 32.8 %collective-permute-start = (f32[16,6,288]{2,0,1:T(8,128)S(1)}, f32[16,6,288]{2,0,1:T(8,128)}, u32[]{:S(2)}, u32[]{:S(2)}) collective-permute-start(f32[16,6,288]{2,0,1:T(8,128)S(1)} %convolution_add_fusion.19), channel_id=1, source_target_pairs={{0,1},{1,0},{2,3},{3,2},{4,5},{5,4},{6,7},{7,6},{8,9},{9,8},{10,11... | collective-permute-start | bytes 331784 | tf_op jit(solution)/shard_map/ppermute | solution.py:21
  14.5 33.3 %collective-permute-start.1 = (f32[16,6,288]{2,0,1:T(8,128)S(1)}, f32[16,6,288]{2,0,1:T(8,128)}, u32[]{:S(2)}, u32[]{:S(2)}) collective-permute-start(f32[16,6,288]{2,0,1:T(8,128)S(1)} %convolution_add_fusion.19), channel_id=1, source_target_pairs={{0,2},{1,3},{2,0},{3,1},{4,6},{5,7},{6,4},{7,5},{8,10},{9,11},{10,... | collective-permute-start | bytes 331784 | tf_op jit(solution)/shard_map/ppermute | solution.py:21
  16.1 34.4 %collective-permute-start.2 = (f32[16,6,288]{2,0,1:T(8,128)S(1)}, f32[16,6,288]{2,0,1:T(8,128)}, u32[]{:S(2)}, u32[]{:S(2)}) collective-permute-start(f32[16,6,288]{2,0,1:T(8,128)S(1)} %convolution_add_fusion.19), channel_id=1, source_target_pairs={{0,3},{1,2},{2,1},{3,0},{4,7},{5,6},{6,5},{7,4},{8,11},{9,10},{10,... | collective-permute-start | bytes 331784 | tf_op jit(solution)/shard_map/ppermute | solution.py:21
  16.1 150.2 %collective-permute-start.6 = (bf16[288,1152]{1,0:T(8,128)(2,1)}, bf16[288,1152]{1,0:T(8,128)(2,1)}, u32[]{:S(2)}, u32[]{:S(2)}) collective-permute-start(bf16[288,1152]{1,0:T(8,128)(2,1)} %param.19), channel_id=1, source_target_pairs={{0,1},{1,0},{2,3},{3,2},{4,5},{5,4},{6,7},{7,6},{8,9},{9,8},{10,11... | collective-permute-start | bytes 1990664 | tf_op jit(solution)/shard_map/ppermute | solution.py:21
  18.0 159.4 %collective-permute-start.10 = (bf16[288,1152]{1,0:T(8,128)(2,1)}, bf16[288,1152]{1,0:T(8,128)(2,1)}, u32[]{:S(2)}, u32[]{:S(2)}) collective-permute-start(bf16[288,1152]{1,0:T(8,128)(2,1)} %param.19), channel_id=1, source_target_pairs={{0,3},{1,2},{2,1},{3,0},{4,7},{5,6},{6,5},{7,4},{8,11},{9,10},{10,... | collective-permute-start | bytes 1990664 | tf_op jit(solution)/shard_map/ppermute | solution.py:21
  44.3 139.6 %collective-permute-start.8 = (bf16[288,1152]{1,0:T(8,128)(2,1)}, bf16[288,1152]{1,0:T(8,128)(2,1)S(1)}, u32[]{:S(2)}, u32[]{:S(2)}) collective-permute-start(bf16[288,1152]{1,0:T(8,128)(2,1)} %param.19), channel_id=1, source_target_pairs={{0,2},{1,3},{2,0},{3,1},{4,6},{5,7},{6,4},{7,5},{8,10},{9,11},{10,... | collective-permute-start | bytes 1990664 | tf_op jit(solution)/shard_map/ppermute | solution.py:21
  160.3 34.9 %collective-permute-start.5 = (bf16[512,288]{0,1:T(8,128)(2,1)S(1)}, bf16[512,288]{0,1:T(8,128)(2,1)S(1)}, u32[]{:S(2)}, u32[]{:S(2)}) collective-permute-start(bf16[512,288]{0,1:T(8,128)(2,1)S(1)} %bitcast.339), channel_id=1, source_target_pairs={{0,1},{1,0},{2,3},{3,2},{4,5},{5,4},{6,7},{7,6},{8,9},{9,8},{10,11... | collective-permute-start | bytes 884744 | tf_op jit(solution)/shard_map/ppermute | solution.py:21
  181.3 23.0 %collective-permute-start.7 = (bf16[512,288]{0,1:T(8,128)(2,1)S(1)}, bf16[512,288]{0,1:T(8,128)(2,1)}, u32[]{:S(2)}, u32[]{:S(2)}) collective-permute-start(bf16[512,288]{0,1:T(8,128)(2,1)S(1)} %bitcast.342), channel_id=1, source_target_pairs={{0,2},{1,3},{2,0},{3,1},{4,6},{5,7},{6,4},{7,5},{8,10},{9,11},{10,... | collective-permute-start | bytes 884744 | tf_op jit(solution)/shard_map/ppermute | solution.py:21
  241.8 194.7 %collective-permute-start.72 = (f32[2304]{0:T(1024)}, f32[2304]{0:T(1024)}, u32[]{:S(2)}, u32[]{:S(2)}) collective-permute-start(f32[2304]{0:T(1024)} %pad_maximum_fusion.13), channel_id=1, source_target_pairs={{0,4},{4,0},{8,12},{12,8},{16,20},{20,16},{24,28},{28,24},{1,5},{5... | collective-permute-start | bytes 27656 | tf_op jit(solution)/shard_map/ppermute | solution.py:21
  256.4 124.8 %collective-permute-start.66 = (bf16[128,1152]{1,0:T(8,128)(2,1)S(1)}, bf16[128,1152]{1,0:T(8,128)(2,1)}, u32[]{:S(2)}, u32[]{:S(2)}) collective-permute-start(bf16[128,1152]{1,0:T(8,128)(2,1)S(1)} %get-tuple-element.52), channel_id=1, source_target_pairs={{0,1},{1,0},{2,3},{3,2},{4,5},{5,4},{6,7},{7,6},{8,9},{9,8},{10,11... | collective-permute-start | bytes 884744 | tf_op jit(solution)/shard_map/ppermute | solution.py:21
  257.7 125.7 %collective-permute-start.67 = (bf16[128,1152]{1,0:T(8,128)(2,1)S(1)}, bf16[128,1152]{1,0:T(8,128)(2,1)}, u32[]{:S(2)}, u32[]{:S(2)}) collective-permute-start(bf16[128,1152]{1,0:T(8,128)(2,1)S(1)} %get-tuple-element.52), channel_id=1, source_target_pairs={{0,2},{1,3},{2,0},{3,1},{4,6},{5,7},{6,4},{7,5},{8,10},{9,11},{10,... | collective-permute-start | bytes 884744 | tf_op jit(solution)/shard_map/ppermute | solution.py:21
  258.8 127.2 %collective-permute-start.68 = (bf16[128,1152]{1,0:T(8,128)(2,1)S(1)}, bf16[128,1152]{1,0:T(8,128)(2,1)S(1)}, u32[]{:S(2)}, u32[]{:S(2)}) collective-permute-start(bf16[128,1152]{1,0:T(8,128)(2,1)S(1)} %get-tuple-element.52), channel_id=1, source_target_pairs={{0,3},{1,2},{2,1},{3,0},{4,7},{5,6},{6,5},{7,4},{8,11},{9,10},{10,... | collective-permute-start | bytes 884744 | tf_op jit(solution)/shard_map/ppermute | solution.py:21
  299.0 88.4 %collective-permute-start.69 = (bf16[128,1152]{1,0:T(8,128)(2,1)S(1)}, bf16[128,1152]{1,0:T(8,128)(2,1)}, u32[]{:S(2)}, u32[]{:S(2)}) collective-permute-start(bf16[128,1152]{1,0:T(8,128)(2,1)S(1)} %get-tuple-element.55), channel_id=1, source_target_pairs={{0,1},{1,0},{2,3},{3,2},{4,5},{5,4},{6,7},{7,6},{8,9},{9,8},{10,11... | collective-permute-start | bytes 884744 | tf_op jit(solution)/shard_map/ppermute | solution.py:21
  410.3 218.2 %reduce-scatter.9.cloned.1.call-start = ((), (), s32[]{:S(2)}) async-start(), calls=%async_computation.3 | async-start | bytes 5971968
  465.2 23.6 %collective-permute-start.11 = (bf16[128,1152]{1,0:T(8,128)(2,1)}, bf16[128,1152]{1,0:T(8,128)(2,1)}, u32[]{:S(2)}, u32[]{:S(2)}) collective-permute-start(bf16[128,1152]{1,0:T(8,128)(2,1)} %get-tuple-element.108), channel_id=1, source_target_pairs={{0,1},{1,0},{2,3},{3,2},{4,5},{5,4},{6,7},{7,6},{8,9},{9,8},{10,11... | collective-permute-start | bytes 884744 | tf_op jit(solution)/shard_map/ppermute | solution.py:21
  465.5 25.9 %collective-permute-start.12 = (bf16[128,1152]{1,0:T(8,128)(2,1)}, bf16[128,1152]{1,0:T(8,128)(2,1)}, u32[]{:S(2)}, u32[]{:S(2)}) collective-permute-start(bf16[128,1152]{1,0:T(8,128)(2,1)} %get-tuple-element.110), channel_id=1, source_target_pairs={{0,2},{1,3},{2,0},{3,1},{4,6},{5,7},{6,4},{7,5},{8,10},{9,11},{10,... | collective-permute-start | bytes 884744 | tf_op jit(solution)/shard_map/ppermute | solution.py:21
  496.0 23.1 %collective-permute-start.16 = (bf16[128,1152]{1,0:T(8,128)(2,1)S(1)}, bf16[128,1152]{1,0:T(8,128)(2,1)}, u32[]{:S(2)}, u32[]{:S(2)}) collective-permute-start(bf16[128,1152]{1,0:T(8,128)(2,1)S(1)} %get-tuple-element.68), channel_id=1, source_target_pairs={{0,3},{1,2},{2,1},{3,0},{4,7},{5,6},{6,5},{7,4},{8,11},{9,10},{10,... | collective-permute-start | bytes 884744 | tf_op jit(solution)/shard_map/ppermute | solution.py:21
  510.1 30.3 %collective-permute-start.25 = (bf16[128,1152]{1,0:T(8,128)(2,1)}, bf16[128,1152]{1,0:T(8,128)(2,1)}, u32[]{:S(2)}, u32[]{:S(2)}) collective-permute-start(bf16[128,1152]{1,0:T(8,128)(2,1)} %get-tuple-element.74), channel_id=1, source_target_pairs={{0,3},{1,2},{2,1},{3,0},{4,7},{5,6},{6,5},{7,4},{8,11},{9,10},{10,... | collective-permute-start | bytes 884744 | tf_op jit(solution)/shard_map/ppermute | solution.py:21
  512.4 34.6 %collective-permute-start.63 = (f32[65,288]{1,0:T(8,128)S(1)}, f32[65,288]{1,0:T(8,128)}, u32[]{:S(2)}, u32[]{:S(2)}) collective-permute-start(f32[65,288]{1,0:T(8,128)S(1)} %add.661), channel_id=1, source_target_pairs={{0,16},{4,20},{8,24},{12,28},{16,0},{20,4},{24,8},{28,12},{1,17},{... | collective-permute-start | bytes 224648 | tf_op jit(solution)/shard_map/ppermute | solution.py:21
  551.4 25.8 %collective-permute-start.46 = (bf16[128,1152]{1,0:T(8,128)(2,1)}, bf16[128,1152]{1,0:T(8,128)(2,1)S(1)}, u32[]{:S(2)}, u32[]{:S(2)}) collective-permute-start(bf16[128,1152]{1,0:T(8,128)(2,1)} %get-tuple-element.96), channel_id=1, source_target_pairs={{0,1},{1,0},{2,3},{3,2},{4,5},{5,4},{6,7},{7,6},{8,9},{9,8},{10,11... | collective-permute-start | bytes 884744 | tf_op jit(solution)/shard_map/ppermute | solution.py:21
  552.4 26.1 %collective-permute-start.47 = (bf16[128,1152]{1,0:T(8,128)(2,1)}, bf16[128,1152]{1,0:T(8,128)(2,1)S(1)}, u32[]{:S(2)}, u32[]{:S(2)}) collective-permute-start(bf16[128,1152]{1,0:T(8,128)(2,1)} %get-tuple-element.98), channel_id=1, source_target_pairs={{0,2},{1,3},{2,0},{3,1},{4,6},{5,7},{6,4},{7,5},{8,10},{9,11},{10,... | collective-permute-start | bytes 884744 | tf_op jit(solution)/shard_map/ppermute | solution.py:21
  553.5 26.2 %collective-permute-start.48 = (bf16[128,1152]{1,0:T(8,128)(2,1)S(1)}, bf16[128,1152]{1,0:T(8,128)(2,1)S(1)}, u32[]{:S(2)}, u32[]{:S(2)}) collective-permute-start(bf16[128,1152]{1,0:T(8,128)(2,1)S(1)} %get-tuple-element.97), channel_id=1, source_target_pairs={{0,3},{1,2},{2,1},{3,0},{4,7},{5,6},{6,5},{7,4},{8,11},{9,10},{10,... | collective-permute-start | bytes 884744 | tf_op jit(solution)/shard_map/ppermute | solution.py:21
  578.6 23.5 %collective-permute-start.65 = (f32[17,1152]{1,0:T(8,128)S(1)}, f32[17,1152]{1,0:T(8,128)S(1)}, u32[]{:S(2)}, u32[]{:S(2)}) collective-permute-start(f32[17,1152]{1,0:T(8,128)S(1)} %fusion.209), channel_id=1, source_target_pairs={{0,2},{1,3},{2,0},{3,1},{4,6},{5,7},{6,4},{7,5},{8,10},{9,11},{10,... | collective-permute-start | bytes 235016 | tf_op jit(solution)/shard_map/ppermute | solution.py:21
  (170 other events, 1997.2 us)
Sparse Core Ops, SparseCore 0:
  410.4 45.6 reduce-scatter.6
  466.6 64.4 reduce-scatter.8

commit v2 on v0

v2 whole, which is shorter than its diff:
```python
import functools

import jax
import jax.numpy as jnp
from jax import lax
from jax.experimental import pallas as pl
from jax.experimental.pallas import tpu as pltpu
from jax.sharding import PartitionSpec as P

HDIM = 72


EPSILON = 1e-06
MASKED = -1e30
PRECISE = lax.Precision.HIGHEST
CHUNKS = 2
KEY_TILE = 512
QUERY_BLOCK = 256
ROW_BLOCK = 256
ROOT = 0.7978845608028654
CUBIC = 0.044715


def peers(axis):
    return range(1, lax.axis_size(axis))


def swap(value, axis, mask):
    count = lax.axis_size(axis)
    return lax.ppermute(value, axis, [(i, i ^ mask) for i in range(count)])


def gather_pieces(value, axis):
    return [value] + [swap(value, axis, mask) for mask in peers(axis)]


def butterfly_sum(value, axis):
    mask = 1
    while mask < lax.axis_size(axis):
        value = value + swap(value, axis, mask)
        mask *= 2
    return value


def three_parts(values):
    first = lax.reduce_precision(values, 8, 7)
    second = lax.reduce_precision(values - first, 8, 7)
    third = values - first - second
    return [part.astype(jnp.bfloat16) for part in (first, second, third)]


def swap_pieces(pieces, axis):
    return [pieces[0]] + [swap(pieces[mask], axis, mask) for mask in peers(axis)]


def pick(which, cases):
    result = cases[0]
    for number, case in enumerate(cases[1:], 1):
        result = jnp.where(which == number, case, result)
    return result


def step_along(value, axis, ahead):
    count = lax.axis_size(axis)
    pairs = [(i, i + 1) if ahead else (i + 1, i) for i in range(count - 1)]
    return lax.ppermute(value, axis, pairs)


LOG2E = 1.4426950408889634
MIB = 1 << 20


def head_window(head, features):
    place = head * HDIM
    start = place // 128 * 128
    return start, min(features, start + 256)


def head_only(block, head):
    features = block.shape[1]
    start, stop = head_window(head, features)
    window = block[:, start:stop]
    lane = lax.broadcasted_iota(jnp.int32, window.shape, 1) + (start - head * HDIM)
    return jnp.where((lane >= 0) & (lane < HDIM), window, jnp.zeros_like(window))


def visible_keys(first_ref, length_ref, base, tile_rows):
    first = first_ref[...] - base
    place = lax.broadcasted_iota(jnp.int32, (tile_rows, first.shape[1]), 0)
    offset = place - first
    return (offset >= 0) & (offset < length_ref[...])


def rows_dot(left, right):
    return lax.dot_general(
        left, right, (((1,), (1,)), ((), ())), preferred_element_type=jnp.float32
    )


def attend_kernel(
    low_ref, high_ref, first_ref, length_ref, query_ref, *refs, sources, tile, step_base
):
    kv_refs = refs[: len(sources)]
    low_out, wide_out, log_out, total, row_max, row_sum = refs[len(sources) :]
    features = query_ref.shape[1]
    heads = features // HDIM
    amount = query_ref.shape[0]
    step = pl.program_id(0) + step_base
    queries = [head_only(query_ref[...], head) for head in range(heads)]
    rescale = HDIM ** (-0.5) * LOG2E
    total[...] = jnp.zeros_like(total)
    row_max[...] = jnp.full_like(row_max, MASKED)
    row_sum[...] = jnp.zeros_like(row_sum)
    for source, kv_ref in zip(sources, kv_refs):
        tiles = kv_ref.shape[1] // tile

        def body(number, carry):
            place = pl.multiple_of((number - source * tiles) * tile, tile)
            keys = kv_ref[0, pl.ds(place, tile), :]
            values = kv_ref[1, pl.ds(place, tile), :].astype(jnp.float32).T
            seen = visible_keys(first_ref, length_ref, number * tile, tile)
            for head in range(heads):
                start, stop = head_window(head, features)
                scores = rows_dot(keys[:, start:stop], queries[head])
                scores = jnp.where(seen, scores, MASKED)
                old = row_max[head : head + 1, :]
                new = jnp.maximum(old, jnp.max(scores, axis=0, keepdims=True))
                shrink = jnp.exp2((old - new) * rescale)
                shares = jnp.exp2((scores - new) * rescale)
                row_max[head : head + 1, :] = new
                row_sum[head : head + 1, :] = row_sum[
                    head : head + 1, :
                ] * shrink + jnp.sum(shares, axis=0, keepdims=True)
                place_rows = slice(head * HDIM, (head + 1) * HDIM)
                total[place_rows, :] = total[place_rows, :] * shrink + jnp.dot(
                    values[place_rows, :].astype(jnp.bfloat16),
                    shares.astype(jnp.bfloat16),
                    preferred_element_type=jnp.float32,
                )
            return carry

        lax.fori_loop(
            jnp.maximum(low_ref[step], source * tiles),
            jnp.minimum(high_ref[step], (source + 1) * tiles),
            body,
            0,
        )
    log_out[...] = row_max[...] * rescale + jnp.log2(row_sum[...])
    for head in range(heads):
        place_rows = slice(head * HDIM, (head + 1) * HDIM)
        total[place_rows, :] = total[place_rows, :] / row_sum[head : head + 1, :]
    wide_out[...] = total[...]
    low_out[...] = total[...].T.astype(jnp.bfloat16)


def attend(lows, highs, firsts, lengths, query, kvs, tile, block, chunk, chunks):
    rows, features = query.shape
    heads = features // HDIM
    amount = rows // chunks
    steps = amount // block
    base = chunk * steps
    whole = pl.BlockSpec(kvs[0].shape, lambda i, *_: (0, 0, 0))
    across = pl.BlockSpec((1, block), lambda i, *_: (0, base + i))
    return pl.pallas_call(
        functools.partial(
            attend_kernel, sources=tuple(range(len(kvs))), tile=tile, step_base=base
        ),
        grid_spec=pltpu.PrefetchScalarGridSpec(
            num_scalar_prefetch=2,
            grid=(steps,),
            in_specs=[across, across, pl.BlockSpec((block, features), lambda i, *_: (base + i, 0))]
            + [whole] * len(kvs),
            out_specs=[
                pl.BlockSpec((block, features), lambda i, *_: (i, 0)),
                pl.BlockSpec((features, block), lambda i, *_: (0, i)),
                pl.BlockSpec((heads, block), lambda i, *_: (0, i)),
            ],
            scratch_shapes=[
                pltpu.VMEM((features, block), jnp.float32),
                pltpu.VMEM((heads, block), jnp.float32),
                pltpu.VMEM((heads, block), jnp.float32),
            ],
        ),
        out_shape=[
            jax.ShapeDtypeStruct((amount, features), jnp.bfloat16),
            jax.ShapeDtypeStruct((features, amount), jnp.float32),
            jax.ShapeDtypeStruct((heads, amount), jnp.float32),
        ],
        compiler_params=pltpu.CompilerParams(vmem_limit_bytes=24 * MIB),
        cost_estimate=pl.CostEstimate(
            flops=amount * 4096 * 1152, bytes_accessed=5 * MIB, transcendentals=0
        ),
    )(lows, highs, firsts, lengths, query, *kvs)


def attend_back_kernel(
    low_ref, high_ref, spot_ref, first_ref, length_ref, log_ref, query_ref, wide_ref, *refs,
    sources, tile, last, peer_count
):
    count = len(sources)
    kv_refs = refs[:count]
    pieces = refs[count:-4]
    if last:
        start_ref, pieces = pieces[-1], pieces[:-1]
    query_out, kv_out, total, kv_total = refs[-4:]
    piece_rows = pieces[0].shape[0]
    features = query_ref.shape[1]
    heads = features // HDIM
    step = pl.program_id(0)
    scaling = HDIM ** (-0.5)
    rescale = scaling * LOG2E

    @pl.when(step == 0)
    def _():
        kv_total[...] = jnp.zeros_like(kv_total)

    total[...] = start_ref[...] if last else jnp.zeros_like(total)
    queries = [head_only(query_ref[...], head) for head in range(heads)]
    parts = []
    for place in range(query_ref.shape[0] // piece_rows):
        block = step * (query_ref.shape[0] // piece_rows) + place
        part = jnp.zeros_like(pieces[0][...])
        for spot, piece in enumerate(pieces):
            owner = (spot_ref[0] ^ (spot % peer_count)) + spot // peer_count * peer_count
            part = jnp.where(block == owner, piece[...], part)
        parts.append(part)
    grad_rows = jnp.concatenate(parts, axis=0)
    grads = [head_only(grad_rows, head) for head in range(heads)]
    products = grad_rows.astype(jnp.float32).T * wide_ref[...]
    deltas = [
        jnp.sum(products[head * HDIM : (head + 1) * HDIM, :], axis=0, keepdims=True)
        for head in range(heads)
    ]
    for spot, (source, kv_ref) in enumerate(zip(sources, kv_refs)):
        tiles = kv_ref.shape[1] // tile

        def body(number, carry):
            place = pl.multiple_of((number - source * tiles) * tile, tile)
            rows = pl.ds(place, tile)
            keys = kv_ref[0, rows, :]
            values = kv_ref[1, rows, :]
            keys_down = keys.astype(jnp.float32).T
            seen = visible_keys(first_ref, length_ref, number * tile, tile)
            for head in range(heads):
                start, stop = head_window(head, features)
                scores = rows_dot(keys[:, start:stop], queries[head])
                shares = jnp.where(
                    seen, jnp.exp2(scores * rescale - log_ref[head : head + 1, :]), 0.0
                )
                grad_shares = rows_dot(values[:, start:stop], grads[head])
                grad_scores = (shares * (grad_shares - deltas[head])).astype(jnp.bfloat16)
                kv_total[spot, 1, rows, start:stop] += jnp.dot(
                    shares.astype(jnp.bfloat16), grads[head], preferred_element_type=jnp.float32
                )
                kv_total[spot, 0, rows, start:stop] += jnp.dot(
                    grad_scores, queries[head], preferred_element_type=jnp.float32
                )
                place_rows = slice(head * HDIM, (head + 1) * HDIM)
                total[place_rows, :] += jnp.dot(
                    keys_down[place_rows, :].astype(jnp.bfloat16),
                    grad_scores,
                    preferred_element_type=jnp.float32,
                )
            return carry

        lax.fori_loop(
            jnp.maximum(low_ref[step], source * tiles),
            jnp.minimum(high_ref[step], (source + 1) * tiles),
            body,
            0,
        )
    if last:
        query_out[...] = (total[...].T * scaling).astype(query_out.dtype)
    else:
        query_out[...] = total[...]

    @pl.when(step == pl.num_programs(0) - 1)
    def _():
        for spot in range(count):
            kv_out[spot, 0] = (kv_total[spot, 0] * scaling).astype(kv_out.dtype)
            kv_out[spot, 1] = kv_total[spot, 1].astype(kv_out.dtype)


def attend_back(
    spot, ranges, logs, query, grads, wide, kvs, sources, tile, block, started=None
):
    lows, highs, firsts, lengths = ranges
    pieces = [piece for chunk in grads for piece in chunk]

    rows, features = query.shape
    heads = features // HDIM
    steps = rows // block
    last = started is not None
    whole = pl.BlockSpec(kvs[0].shape, lambda i, *_: (0, 0, 0))
    across = pl.BlockSpec((1, block), lambda i, *_: (0, i))
    down = pl.BlockSpec((block, features), lambda i, *_: (i, 0))
    turned = pl.BlockSpec((features, block), lambda i, *_: (0, i))
    kv_shape = (len(kvs), 2, rows, features)
    return pl.pallas_call(
        functools.partial(
            attend_back_kernel, sources=sources, tile=tile, last=last, peer_count=len(grads[0])
        ),
        grid_spec=pltpu.PrefetchScalarGridSpec(
            num_scalar_prefetch=3,
            grid=(steps,),
            in_specs=[
                across,
                across,
                pl.BlockSpec((heads, block), lambda i, *_: (0, i)),
                down,
                turned,
            ]
            + [whole] * len(kvs)
            + [fixed(pieces[0].shape)] * len(pieces)
            + ([turned] if last else []),
            out_specs=[
                down if last else turned,
                pl.BlockSpec(kv_shape, lambda i, *_: (0, 0, 0, 0)),
            ],
            scratch_shapes=[
                pltpu.VMEM((features, block), jnp.float32),
                pltpu.VMEM(kv_shape, jnp.float32),
            ],
        ),
        out_shape=[
            jax.ShapeDtypeStruct((rows, features), jnp.bfloat16)
            if last
            else jax.ShapeDtypeStruct((features, rows), jnp.float32),
            jax.ShapeDtypeStruct(kv_shape, jnp.float32 if last else jnp.bfloat16),
        ],
        compiler_params=pltpu.CompilerParams(vmem_limit_bytes=40 * MIB),
        cost_estimate=pl.CostEstimate(
            flops=rows * (8192 if last else 2048) * 1152,
            bytes_accessed=10 * MIB,
            transcendentals=0,
        ),
    )(
        lows, highs, spot, firsts, lengths, logs, query, wide, *kvs, *pieces,
        *([started] if last else []),
    )


def key_ranges(my_images, wide_images, image_count, tile, block):
    images = jnp.arange(image_count, dtype=jnp.int32)
    before = jnp.sum((wide_images[None, :] < images[:, None]).astype(jnp.int32), axis=1)
    amount = jnp.sum((wide_images[None, :] == images[:, None]).astype(jnp.int32), axis=1)
    mine = (my_images[None, :] == images[:, None]).astype(jnp.int32)
    firsts = jnp.sum(mine * before[:, None], axis=0)
    lengths = jnp.sum(mine * amount[:, None], axis=0)
    ends = firsts + lengths
    lows = firsts[::block] // tile
    highs = (ends[block - 1 :: block] + tile - 1) // tile
    return lows, highs, firsts[None, :], lengths[None, :]


def cost(flops, moved):
    return pl.CostEstimate(flops=int(flops), bytes_accessed=int(moved), transcendentals=0)


def normed_rows(values):
    center = values - jnp.mean(values, axis=-1, keepdims=True)
    inverse = lax.rsqrt(jnp.mean(center * center, axis=-1, keepdims=True) + EPSILON)
    return center * inverse, inverse


def spread(hot_ref, table_ref):
    return jnp.dot(hot_ref[...], table_ref[...], preferred_element_type=jnp.float32)


def add_image_sums(sum_ref, spot, hot_ref, image_count, values):
    hot = hot_ref[:, :image_count]
    first = values.astype(jnp.bfloat16)
    second = (values - first.astype(jnp.float32)).astype(jnp.bfloat16)
    for part in (first, second):
        sum_ref[spot] += lax.dot_general(
            hot, part, (((0,), (0,)), ((), ())), preferred_element_type=jnp.float32
        )


def clear_at_start(*refs):
    @pl.when(pl.program_id(0) == 0)
    def _():
        for ref in refs:
            ref[...] = jnp.zeros_like(ref)


def fixed(shape):
    return pl.BlockSpec(shape, lambda i, *_: (0,) * len(shape))


def down(rows, width, base=0):
    return pl.BlockSpec((rows, width), lambda i, *_: (base + i, 0))


def column(table_rows, width, component):
    return pl.BlockSpec((None, table_rows, width), lambda i, *_: (component, 0, 0))


def shaped(shape, kind=jnp.bfloat16):
    return jax.ShapeDtypeStruct(shape, kind)


def hand_out(spot_ref, outs, values):
    rows = outs[0].shape[0]
    amount = values.shape[0] // rows
    for place in range(amount):
        target = pl.program_id(0) * amount + place
        piece = values[place * rows : (place + 1) * rows, :].astype(outs[0].dtype)
        for mask, out in enumerate(outs):

            @pl.when(target == spot_ref[0] ^ mask)
            def _(out=out, piece=piece):
                out[...] = piece


def grid_with(spot_count, grid, in_specs, out_specs):
    return pltpu.PrefetchScalarGridSpec(
        num_scalar_prefetch=spot_count, grid=grid, in_specs=in_specs, out_specs=out_specs
    )


def project_kernel(
    token_ref, hot_ref, shift_ref, scale_ref, weight_ref, bias_ref, hidden_out, query_out, kv_out
):
    normed, _ = normed_rows(token_ref[...].astype(jnp.float32))
    hidden = normed * (1.0 + spread(hot_ref, scale_ref)) + spread(hot_ref, shift_ref)
    hidden = hidden.astype(jnp.bfloat16)
    hidden_out[...] = hidden

    def projected(c):
        product = jnp.dot(hidden, weight_ref[c], preferred_element_type=jnp.float32)
        if c != 1:
            product = product + bias_ref[c // 2 : c // 2 + 1, :].astype(jnp.float32)
        return product.astype(jnp.bfloat16)

    kv_out[0] = projected(1)
    kv_out[1] = projected(2)
    query_out[...] = projected(0)


def project(tokens, hot, table, weight, bias, block):
    rows, width = tokens.shape
    features = weight.shape[2]
    high = table.shape[1]
    return pl.pallas_call(
        project_kernel,
        grid=(rows // block,),
        in_specs=[
            down(block, width),
            down(block, hot.shape[1]),
            column(high, width, 0),
            column(high, width, 1),
            fixed(weight.shape),
            fixed(bias.shape),
        ],
        out_specs=[
            down(block, width),
            down(block, features),
            pl.BlockSpec((2, block, features), lambda i: (0, i, 0)),
        ],
        out_shape=[
            shaped((rows, width)),
            shaped((rows, features)),
            shaped((2, rows, features)),
        ],
        compiler_params=pltpu.CompilerParams(vmem_limit_bytes=32 * MIB),
        cost_estimate=cost(6 * rows * width * features, 8 * MIB),
    )(tokens, hot, table, table, weight, bias)


def grad_act_kernel(cot_ref, hot_ref, gate_ref, weight_ref, grad_out, act_out, bias_out):
    clear_at_start(bias_out)
    grad = (spread(hot_ref, gate_ref) * cot_ref[...].astype(jnp.float32)).astype(jnp.bfloat16)
    grad_out[...] = grad
    bias_out[...] += jnp.sum(grad.astype(jnp.float32), axis=0, keepdims=True)
    act_out[...] = rows_dot(grad, weight_ref[...])


def grad_act_of(cotangent, hot, table, weight, block):
    rows, width = cotangent.shape
    units = weight.shape[0]
    return pl.pallas_call(
        grad_act_kernel,
        grid=(rows // block,),
        in_specs=[
            down(block, width),
            down(block, hot.shape[1]),
            column(table.shape[1], width, 5),
            fixed(weight.shape),
        ],
        out_specs=[down(block, width), down(block, units), fixed((1, width))],
        out_shape=[
            shaped((rows, width)),
            shaped((rows, units), jnp.float32),
            shaped((1, width), jnp.float32),
        ],
        compiler_params=pltpu.CompilerParams(vmem_limit_bytes=32 * MIB),
        cost_estimate=cost(2 * rows * width * units, 12 * MIB),
    )(cotangent, hot, table, weight)


def middle_kernel(spot_ref, *refs, count, image_count):
    pieces, out_refs = refs[:count], refs[count : 2 * count]
    (
        token_ref, hot_ref, gate_ref, shift_ref, scale_ref, out_bias_ref, up_ref, up_bias_ref,
        grad_act_ref, attn_out, hidden_out, act_out, grad_out, sum_out, bias_out,
    ) = refs[2 * count : -count]
    clear_at_start(sum_out, bias_out)
    attn = out_bias_ref[...].astype(jnp.float32)
    for piece, out_ref in zip(pieces, out_refs):
        attn = attn + jnp.dot(piece[...], out_ref[...], preferred_element_type=jnp.float32)
    attn_out[...] = attn
    middle = token_ref[...].astype(jnp.float32) + spread(hot_ref, gate_ref) * attn
    normed, _ = normed_rows(middle)
    hidden = normed * (1.0 + spread(hot_ref, scale_ref)) + spread(hot_ref, shift_ref)
    hidden = hidden.astype(jnp.bfloat16)
    hidden_out[...] = hidden
    pre = jnp.dot(hidden, up_ref[...], preferred_element_type=jnp.float32)
    pre = pre + up_bias_ref[...].astype(jnp.float32)
    square = pre * pre
    bend = jnp.tanh(ROOT * pre * (1.0 + CUBIC * square))
    half = 0.5 * (1.0 + bend)
    act_out[...] = (pre * half).astype(jnp.bfloat16)
    slope = half + 0.5 * ROOT * pre * (1.0 - bend * bend) * (1.0 + 3.0 * CUBIC * square)
    grad = (grad_act_ref[...] * slope).astype(jnp.bfloat16)
    grad_out[...] = grad
    bias_out[...] += jnp.sum(grad.astype(jnp.float32), axis=0, keepdims=True)
    part = rows_dot(grad, up_ref[...])
    hand_out(spot_ref, refs[-count:], part)
    add_image_sums(sum_out, 0, hot_ref, image_count, part)
    add_image_sums(sum_out, 1, hot_ref, image_count, part * normed)


def middle_of(
    spot, pieces, tokens, hot, table, out_full, out_bias, up_weight, up_bias, grad_act,
    image_count, block, chunk,
):
    rows, features = pieces[0].shape
    width, units = up_weight.shape
    high = table.shape[1]
    count = len(pieces)
    base = chunk * (rows // block)
    return pl.pallas_call(
        functools.partial(middle_kernel, count=count, image_count=image_count),
        grid_spec=grid_with(
            1,
            (rows // block,),
            [down(block, features)] * count
            + [fixed((features, width))] * count
            + [
                down(block, width, base),
                down(block, hot.shape[1], base),
                column(high, width, 2),
                column(high, width, 3),
                column(high, width, 4),
                fixed(out_bias.shape),
                fixed(up_weight.shape),
                fixed(up_bias.shape),
                down(block, units, base),
            ],
            [
                down(block, width),
                down(block, width),
                down(block, units),
                down(block, units),
                fixed((2, image_count, width)),
                fixed((1, units)),
            ]
            + [fixed((rows // count, width))] * count,
        ),
        out_shape=[
            shaped((rows, width), jnp.float32),
            shaped((rows, width)),
            shaped((rows, units)),
            shaped((rows, units)),
            shaped((2, image_count, width), jnp.float32),
            shaped((1, units), jnp.float32),
        ]
        + [shaped((rows // count, width))] * count,
        compiler_params=pltpu.CompilerParams(vmem_limit_bytes=48 * MIB),
        cost_estimate=cost(6 * rows * width * units, 16 * MIB),
    )(
        spot, *pieces, *out_full, tokens, hot, table, table, table, out_bias, up_weight, up_bias,
        grad_act,
    )


def mlp_kernel(spot_ref, act_ref, weight_ref, cot_ref, hot_ref, sum_out, *outs, image_count):
    clear_at_start(sum_out)
    part = jnp.dot(act_ref[...], weight_ref[...], preferred_element_type=jnp.float32)
    hand_out(spot_ref, outs, part)
    add_image_sums(sum_out, 0, hot_ref, image_count, part * cot_ref[...].astype(jnp.float32))


def mlp_of(spot, act, weight, cotangent, hot, image_count, block, chunk, count):
    rows, units = act.shape
    width = weight.shape[1]
    base = chunk * (rows // block)
    return pl.pallas_call(
        functools.partial(mlp_kernel, image_count=image_count),
        grid_spec=grid_with(
            1,
            (rows // block,),
            [
                down(block, units),
                fixed(weight.shape),
                down(block, width, base),
                down(block, hot.shape[1], base),
            ],
            [fixed((1, image_count, width))] + [fixed((rows // count, width))] * count,
        ),
        out_shape=[shaped((1, image_count, width), jnp.float32)]
        + [shaped((rows // count, width))] * count,
        compiler_params=pltpu.CompilerParams(vmem_limit_bytes=32 * MIB),
        cost_estimate=cost(2 * rows * width * units, 8 * MIB),
    )(spot, act, weight, cotangent, hot)


def norm_back_rows(gradient, normed, inverse):
    return (
        gradient
        - jnp.mean(gradient, axis=-1, keepdims=True)
        - normed * jnp.mean(gradient * normed, axis=-1, keepdims=True)
    ) * inverse


def sum_of(pieces):
    total = pieces[0][...].astype(jnp.float32)
    for piece in pieces[1:]:
        total = total + piece[...].astype(jnp.float32)
    return total


def grad_middle_kernel(spot_ref, *refs, count, image_count):
    pieces, out_refs = refs[:count], refs[count : 2 * count]
    (
        attn_ref, token_ref, cot_ref, hot_ref, gate_ref, scale_ref, middle_out, attn_out, sum_out,
        bias_out,
    ) = refs[2 * count : -count]
    gate = spread(hot_ref, gate_ref)
    attn = attn_ref[...]
    normed, inverse = normed_rows(token_ref[...].astype(jnp.float32) + gate * attn)
    gradient = sum_of(pieces) * (1.0 + spread(hot_ref, scale_ref))
    grad_middle = cot_ref[...].astype(jnp.float32) + norm_back_rows(gradient, normed, inverse)
    middle_out[...] = grad_middle
    grad_attn = (gate * grad_middle).astype(jnp.bfloat16)
    attn_out[...] = grad_attn
    for out_ref, block_out in zip(out_refs, refs[-count:]):
        block_out[...] = rows_dot(grad_attn, out_ref[...]).astype(jnp.bfloat16)
    bias_out[...] = jnp.sum(grad_attn.astype(jnp.float32), axis=0, keepdims=True)
    sum_out[...] = jnp.zeros_like(sum_out)
    add_image_sums(sum_out, 0, hot_ref, image_count, grad_middle * attn)


def owned(rows, width, base):
    return pl.BlockSpec((rows, width), lambda i, spot: (base + spot[0], 0))


def grad_middle_of(spot, pieces, attn, tokens, cotangent, hot, table, out_full, image_count, chunk):
    rows, width = pieces[0].shape
    features = out_full[0].shape[0]
    high = table.shape[1]
    count = len(pieces)
    base = chunk * count
    return pl.pallas_call(
        functools.partial(grad_middle_kernel, count=count, image_count=image_count),
        grid_spec=grid_with(
            1,
            (1,),
            [fixed((rows, width))] * count
            + [fixed((features, width))] * count
            + [
                owned(rows, width, 0),
                owned(rows, width, base),
                owned(rows, width, base),
                owned(rows, hot.shape[1], base),
                column(high, width, 2),
                column(high, width, 4),
            ],
            [
                fixed((rows, width)),
                fixed((rows, width)),
                fixed((1, image_count, width)),
                fixed((1, width)),
            ]
            + [fixed((rows, features))] * count,
        ),
        out_shape=[
            shaped((rows, width), jnp.float32),
            shaped((rows, width)),
            shaped((1, image_count, width), jnp.float32),
            shaped((1, width), jnp.float32),
        ]
        + [shaped((rows, features))] * count,
        compiler_params=pltpu.CompilerParams(vmem_limit_bytes=32 * MIB),
        cost_estimate=cost(2 * rows * width * width, 5 * MIB),
    )(spot, *pieces, *out_full, attn, tokens, cotangent, hot, table, table)


def layer_out_kernel(spot_ref, *refs, count):
    pieces = refs[:count]
    attn_ref, token_ref, hot_ref, gate_ref, gate_two_ref, bias_ref, rows_out = refs[count:]
    middle = token_ref[...].astype(jnp.float32) + spread(hot_ref, gate_ref) * attn_ref[...]
    mlp = sum_of(pieces) + bias_ref[...].astype(jnp.float32)
    rows_out[...] = (middle + spread(hot_ref, gate_two_ref) * mlp).astype(jnp.bfloat16)


def layer_out_of(spot, pieces, attn, tokens, hot, table, bias, chunk):
    rows, width = pieces[0].shape
    high = table.shape[1]
    base = chunk * len(pieces)
    return pl.pallas_call(
        functools.partial(layer_out_kernel, count=len(pieces)),
        grid_spec=pltpu.PrefetchScalarGridSpec(
            num_scalar_prefetch=1,
            grid=(1,),
            in_specs=[fixed((rows, width))] * len(pieces)
            + [
                owned(rows, width, 0),
                owned(rows, width, base),
                owned(rows, hot.shape[1], base),
                column(high, width, 2),
                column(high, width, 5),
                fixed(bias.shape),
            ],
            out_specs=fixed((rows, width)),
        ),
        out_shape=shaped((rows, width)),
        compiler_params=pltpu.CompilerParams(vmem_limit_bytes=16 * MIB),
        cost_estimate=cost(rows * width * 64, 3 * MIB),
    )(spot, *pieces, attn, tokens, hot, table, table, bias)


def grad_tokens_kernel(spot_ref, *refs, count):
    pieces = refs[:count]
    token_ref, hot_ref, scale_ref, middle_ref, rows_out = refs[count:]
    normed, inverse = normed_rows(token_ref[...].astype(jnp.float32))
    gradient = sum_of(pieces) * (1.0 + spread(hot_ref, scale_ref))
    rows_out[...] = (middle_ref[...] + norm_back_rows(gradient, normed, inverse)).astype(
        jnp.bfloat16
    )


def grad_tokens_of(spot, pieces, tokens, hot, table, grad_middle, chunk):
    rows, width = pieces[0].shape
    base = chunk * len(pieces)
    return pl.pallas_call(
        functools.partial(grad_tokens_kernel, count=len(pieces)),
        grid_spec=pltpu.PrefetchScalarGridSpec(
            num_scalar_prefetch=1,
            grid=(1,),
            in_specs=[fixed((rows, width))] * len(pieces)
            + [
                owned(rows, width, base),
                owned(rows, hot.shape[1], base),
                column(table.shape[1], width, 1),
                fixed((rows, width)),
            ],
            out_specs=fixed((rows, width)),
        ),
        out_shape=shaped((rows, width)),
        compiler_params=pltpu.CompilerParams(vmem_limit_bytes=16 * MIB),
        cost_estimate=cost(rows * width * 64, 3 * MIB),
    )(spot, *pieces, tokens, hot, table, grad_middle)


def grad_hidden_kernel(
    spot_ref, query_ref, near_ref, after_ref, before_ref, weight_ref, token_ref, hot_ref, kv_out,
    sum_out, bias_out, *outs, image_count,
):
    clear_at_start(sum_out, bias_out)
    normed, _ = normed_rows(token_ref[...].astype(jnp.float32))
    query = query_ref[...]
    part = rows_dot(query, weight_ref[0])
    bias_out[0:1] += jnp.sum(query.astype(jnp.float32), axis=0, keepdims=True)
    for c in range(2):
        total = (
            near_ref[0, c]
            + after_ref[c].astype(jnp.float32)
            + before_ref[c].astype(jnp.float32)
        ).astype(jnp.bfloat16)
        kv_out[c] = total
        part = part + rows_dot(total, weight_ref[c + 1])
        if c == 1:
            bias_out[1:2] += jnp.sum(total.astype(jnp.float32), axis=0, keepdims=True)
    hand_out(spot_ref, outs, part)
    add_image_sums(sum_out, 0, hot_ref, image_count, part)
    add_image_sums(sum_out, 1, hot_ref, image_count, part * normed)


def grad_hidden_of(
    spot, query, near, after, before, weight, tokens, hot, image_count, block, chunk, chunks, count
):
    rows, features = query.shape
    rows = rows // chunks
    width = tokens.shape[1]
    base = chunk * (rows // block)
    pair = pl.BlockSpec((2, block, features), lambda i, *_: (0, base + i, 0))
    return pl.pallas_call(
        functools.partial(grad_hidden_kernel, image_count=image_count),
        grid_spec=grid_with(
            1,
            (rows // block,),
            [
                down(block, features, base),
                pl.BlockSpec((1, 2, block, features), lambda i, *_: (0, 0, base + i, 0)),
                pair,
                pair,
                fixed(weight.shape),
                down(block, width, base),
                down(block, hot.shape[1], base),
            ],
            [
                pl.BlockSpec((2, block, features), lambda i, *_: (0, i, 0)),
                fixed((2, image_count, width)),
                fixed((2, features)),
            ]
            + [fixed((rows // count, width))] * count,
        ),
        out_shape=[
            shaped((2, rows, features)),
            shaped((2, image_count, width), jnp.float32),
            shaped((2, features), jnp.float32),
        ]
        + [shaped((rows // count, width))] * count,
        compiler_params=pltpu.CompilerParams(vmem_limit_bytes=32 * MIB),
        cost_estimate=cost(6 * rows * width * features, 8 * MIB),
    )(spot, query, near, after, before, weight, tokens, hot)


def place_kernel(spot_ref, *refs, count, held):
    out = refs[-1]
    place = pl.program_id(0) % count
    for c in range(held):
        for mask in range(count):

            @pl.when(
                (place == spot_ref[0] ^ mask) & (pl.program_id(0) // count == c)
            )
            def _(piece=refs[c * count + mask]):
                out[...] = piece[...].astype(out.dtype)


def place_rows(spot, chunks, kind, total=None, base=0, before=None):
    count = len(chunks[0])
    rows, width = chunks[0][0].shape
    pieces = [piece for chunk in chunks for piece in chunk]
    total = total or len(pieces) * rows
    extra = [] if before is None else [before]
    return pl.pallas_call(
        functools.partial(place_kernel, count=count, held=len(chunks)),
        grid_spec=grid_with(
            1,
            (len(pieces),),
            [fixed((rows, width))] * len(pieces) + [pl.BlockSpec(memory_space=pl.ANY)] * len(extra),
            pl.BlockSpec((rows, width), lambda i, *_: (base + i, 0)),
        ),
        out_shape=shaped((total, width), kind),
        input_output_aliases={1 + len(pieces): 0} if extra else {},
        compiler_params=pltpu.CompilerParams(vmem_limit_bytes=16 * MIB),
        cost_estimate=cost(0, 4 * MIB),
    )(spot, *pieces, *extra)


def turned_dot(left, right):
    return lax.dot_general(
        left, right, (((0,), (0,)), ((), ())), preferred_element_type=jnp.float32
    )


def mlp_weights_kernel(grad_ref, *refs, chunks):
    hidden, pre, act = refs[:chunks], refs[chunks : 2 * chunks], refs[2 * chunks : 3 * chunks]
    out = refs[-1]
    units = pre[0].shape[1]
    rows = pre[0].shape[0]
    up, low = 0.0, 0.0
    for c in range(chunks):
        up = up + turned_dot(hidden[c][...], pre[c][...])
        low = low + turned_dot(grad_ref[c * rows : (c + 1) * rows, :], act[c][...])
    out[:, :units] = up.astype(jnp.bfloat16)
    out[:, units:] = low.astype(jnp.bfloat16)


def mlp_weights(grad_mlp, hidden, pre, act):
    rows, width = grad_mlp.shape
    chunks = len(hidden)
    units = pre[0].shape[1]
    if units % 128:
        joined = [jnp.concatenate(parts, axis=0) for parts in (hidden, pre, act)]
        sides = [turned_dot(joined[0], joined[1]), turned_dot(grad_mlp, joined[2])]
        return jnp.concatenate([side.astype(jnp.bfloat16) for side in sides], axis=1)
    part = width // 3
    across = lambda high: pl.BlockSpec((high, part), lambda i: (0, i))
    return pl.pallas_call(
        functools.partial(mlp_weights_kernel, chunks=chunks),
        grid=(3,),
        in_specs=[across(rows)]
        + [across(rows // chunks)] * chunks
        + [fixed((rows // chunks, units))] * (2 * chunks),
        out_specs=pl.BlockSpec((part, 2 * units), lambda i: (i, 0)),
        out_shape=shaped((width, 2 * units)),
        compiler_params=pltpu.CompilerParams(vmem_limit_bytes=48 * MIB),
        cost_estimate=cost(4 * rows * width * units, 16 * MIB),
    )(grad_mlp, *hidden, *pre, *act)


def attn_weights_kernel(grad_ref, hidden_ref, query_ref, *refs, chunks):
    attended, kv, out = refs[:chunks], refs[chunks : 2 * chunks], refs[-1]
    rows = attended[0].shape[0]
    hidden = hidden_ref[...]
    parts = [0.0, turned_dot(hidden, query_ref[...]), 0.0, 0.0]
    for c in range(chunks):
        mine = slice(c * rows, (c + 1) * rows)
        parts[0] = parts[0] + turned_dot(grad_ref[mine, :], attended[c][...])
        for k in range(2):
            parts[2 + k] = parts[2 + k] + turned_dot(hidden_ref[mine, :], kv[c][k])
    out[...] = jnp.concatenate([part.astype(jnp.bfloat16) for part in parts], axis=1)


def attn_weights(grad_attn, hidden, grad_query, attended, grad_kv):
    rows, width = hidden.shape
    chunks = len(attended)
    features = grad_query.shape[1]
    part = width // 3
    across = pl.BlockSpec((rows, part), lambda i: (0, i))
    return pl.pallas_call(
        functools.partial(attn_weights_kernel, chunks=chunks),
        grid=(3,),
        in_specs=[across, across, fixed(grad_query.shape)]
        + [fixed(attended[0].shape)] * chunks
        + [fixed(grad_kv[0].shape)] * chunks,
        out_specs=pl.BlockSpec((part, 4 * features), lambda i: (i, 0)),
        out_shape=shaped((width, 4 * features)),
        compiler_params=pltpu.CompilerParams(vmem_limit_bytes=48 * MIB),
        cost_estimate=cost(8 * rows * width * features, 12 * MIB),
    )(grad_attn, hidden, grad_query, *attended, *grad_kv)


def on_device(
    tokens,
    conditioning,
    image_index,
    qkv_weight,
    qv_bias,
    out_weight,
    out_bias,
    up_weight,
    up_bias,
    down_weight,
    down_bias,
    ada_weight,
    ada_bias,
    cotangent,
):
    row_count, width = tokens.shape
    feature_count = qkv_weight.shape[2]
    head_size = lax.axis_size("head")
    me = lax.axis_index("head")
    spot = me.astype(jnp.int32).reshape(1)
    my_index = lax.axis_index("seq")
    image_count = conditioning.shape[0]
    columns = ada_weight.shape[2]
    my_images = lax.dynamic_slice_in_dim(image_index, my_index * row_count, row_count, 0)
    edge = jnp.full((row_count,), -1, jnp.int32)
    padded_images = jnp.concatenate([edge, image_index, edge + (image_count + 1)])
    wide_images = lax.dynamic_slice_in_dim(padded_images, my_index * row_count, 3 * row_count, 0)
    ranges = key_ranges(my_images, wide_images, image_count, KEY_TILE, QUERY_BLOCK)
    images = jnp.tile(jnp.arange(image_count, dtype=jnp.int32), 3)
    hot = (my_images[:, None] == images[None, :]).astype(jnp.bfloat16)

    cond_float = conditioning.astype(jnp.float32)
    cond_act = jax.nn.silu(cond_float).astype(jnp.bfloat16)
    mod_mine = jnp.einsum("id,dkf->kif", cond_act, ada_weight, preferred_element_type=jnp.float32)
    mod_mine = mod_mine + ada_bias.astype(jnp.float32)[:, None]
    mod_pieces = gather_pieces(mod_mine, "head")
    modulation = jnp.concatenate([pick(me ^ j, mod_pieces) for j in range(head_size)], axis=2)
    table = jnp.concatenate(three_parts(modulation), axis=1)
    out_full = gather_pieces(out_weight, "head")

    weight = qkv_weight.transpose(1, 0, 2)
    hidden_one, query, key_value = project(tokens, hot, table, weight, qv_bias, ROW_BLOCK)
    kv_before = step_along(key_value, "seq", True)
    kv_after = step_along(key_value, "seq", False)
    grad_mlp, grad_act, grad_down_bias = grad_act_of(
        cotangent, hot, table, down_weight, ROW_BLOCK
    )
    kvs = [kv_before, key_value, kv_after]
    attended, attended_wide, logs = zip(
        *[
            attend(*ranges, query, kvs, KEY_TILE, QUERY_BLOCK, c, CHUNKS)
            for c in range(CHUNKS)
        ]
    )
    attended_wide = jnp.concatenate(attended_wide, axis=1)
    logs = jnp.concatenate(logs, axis=1)

    out_bias = out_bias[None]
    up_bias = up_bias[None]
    attn, hidden_two, act, grad_pre, late_sums, up_sums, hidden_pieces = [], [], [], [], [], [], []
    for c in range(CHUNKS):
        got = middle_of(
            spot, gather_pieces(attended[c], "head"), tokens, hot, table, out_full, out_bias,
            up_weight, up_bias, grad_act, image_count, ROW_BLOCK, c,
        )
        for values, kept in zip((attn, hidden_two, act, grad_pre, late_sums, up_sums), got):
            values.append(kept)
        hidden_pieces.append(swap_pieces(got[6:], "head"))

    grad_middle, grad_attn, grad_attended, gate_sums, out_sums = [], [], [], [], []
    for c in range(CHUNKS):
        got = grad_middle_of(
            spot, hidden_pieces[c], attn[c], tokens, cotangent, hot, table, out_full,
            image_count, c,
        )
        grad_middle.append(got[0])
        grad_attn.append(gather_pieces(got[1], "head"))
        gate_sums.append(got[2])
        out_sums.append(got[3])
        grad_attended.append(swap_pieces(got[4:], "head"))

    query_started, kv_far = attend_back(
        spot, ranges, logs, query, grad_attended, attended_wide, [kv_before, kv_after], (0, 2),
        KEY_TILE, QUERY_BLOCK,
    )
    from_after = step_along(kv_far[0], "seq", False)
    from_before = step_along(kv_far[1], "seq", True)
    grad_query, kv_near = attend_back(
        spot, ranges, logs, query, grad_attended, attended_wide, [key_value], (1,),
        KEY_TILE, QUERY_BLOCK, started=query_started,
    )

    grad_kv, first_sums, qv_sums, one_pieces = [], [], [], []
    for c in range(CHUNKS):
        got = grad_hidden_of(
            spot, grad_query, kv_near, from_after, from_before, weight, tokens, hot, image_count,
            ROW_BLOCK, c, CHUNKS, head_size,
        )
        grad_kv.append(got[0])
        first_sums.append(got[1])
        qv_sums.append(got[2])
        one_pieces.append(swap_pieces(got[3:], "head"))
    grad_tokens = None
    for c in range(CHUNKS):
        rows = grad_tokens_of(spot, one_pieces[c], tokens, hot, table, grad_middle[c], c)
        grad_tokens = place_rows(
            spot, [gather_pieces(rows, "head")], jnp.float32, row_count, c * head_size, grad_tokens
        )

    mlp_sums, out_rows = [], []
    for c in range(CHUNKS):
        got = mlp_of(
            spot, act[c], down_weight, cotangent, hot, image_count, ROW_BLOCK, c, head_size
        )
        mlp_sums.append(got[0])
        rows = layer_out_of(
            spot, swap_pieces(got[1:], "head"), attn[c], tokens, hot, table, down_bias[None], c
        )
        out_rows.append(gather_pieces(rows, "head"))
    layer_out = place_rows(spot, out_rows, jnp.bfloat16)

    def own_columns(values):
        return [values[:, j * columns : (j + 1) * columns] for j in range(head_size)]

    def to_owners(values):
        parts = own_columns(values)
        return sum(swap_pieces([pick(me ^ mask, parts) for mask in range(head_size)], "head"))

    late = jnp.concatenate(
        [sum(gate_sums)[0], sum(late_sums).reshape(2 * image_count, width)]
        + [sum(mlp_sums)[0], sum(out_sums)],
        axis=0,
    )
    cot_sums = lax.dot_general(
        hot[:, :image_count], cotangent, (((0,), (0,)), ((), ())),
        preferred_element_type=jnp.float32,
    )
    cot_sums = pick(me, own_columns(cot_sums * down_bias.astype(jnp.float32)[None]))
    late_mine = to_owners(late) + jnp.pad(cot_sums, ((3 * image_count, 1), (0, 0)))
    late_mine = butterfly_sum(late_mine, "seq")
    low_bias = butterfly_sum(jnp.concatenate([sum(up_sums), grad_down_bias], axis=1), "seq")[0]
    units = up_weight.shape[1]
    grad_up_bias, grad_down_bias = low_bias[:units], low_bias[units:]
    first_mine = to_owners(sum(first_sums).reshape(2 * image_count, width))
    first_mine = butterfly_sum(jnp.concatenate([first_mine, sum(qv_sums)], axis=0), "seq")
    grad_qv_bias = first_mine[2 * image_count :]
    grad_mod = jnp.concatenate(
        [first_mine[: 2 * image_count], late_mine[: 4 * image_count]], axis=0
    ).reshape(6, image_count, columns)
    grad_ada_bias = jnp.sum(grad_mod, axis=1)
    grad_ada_weight = jnp.einsum(
        "id,kif->dkf", cond_act.astype(jnp.float32), grad_mod, precision=PRECISE
    )
    grad_cond_act = jnp.einsum(
        "kif,dkf->id", grad_mod, ada_weight.astype(jnp.float32), precision=PRECISE
    )
    out_sum = late_mine[4 * image_count :]
    spread_bias = jnp.concatenate(
        [jnp.where(me == j, out_sum, 0.0) for j in range(head_size)], axis=1
    )
    last = butterfly_sum(jnp.concatenate([grad_cond_act, spread_bias], axis=0), "head")
    _, silu_pull = jax.vjp(jax.nn.silu, cond_float)
    grad_conditioning = silu_pull(last[:image_count])[0]
    grad_out_bias = last[image_count]

    mlp_total = lax.psum_scatter(
        mlp_weights(grad_mlp, hidden_two, grad_pre, act), "seq", scatter_dimension=0, tiled=True
    ).astype(jnp.float32)
    attn_total = lax.psum_scatter(
        attn_weights(
            place_rows(spot, grad_attn, jnp.bfloat16), hidden_one, grad_query, attended, grad_kv
        ),
        "seq", scatter_dimension=0, tiled=True,
    ).astype(jnp.float32)
    return (
        layer_out,
        grad_tokens,
        grad_conditioning,
        attn_total[:, feature_count:].reshape(-1, 3, feature_count),
        grad_qv_bias,
        attn_total[:, :feature_count].T,
        grad_out_bias,
        mlp_total[:, :units],
        grad_up_bias,
        mlp_total[:, units:].T,
        grad_down_bias,
        grad_ada_weight,
        grad_ada_bias,
    )


def solution(mesh):
    placed = (
        P("seq", None),
        P(),
        P(),
        P(None, None, "head"),
        P(None, "head"),
        P("head", None),
        P(),
        P(None, "head"),
        P("head"),
        P("head", None),
        P(),
        P(None, None, "head"),
        P(None, "head"),
        P("seq", None),
    )
    return jax.shard_map(
        on_device,
        mesh=mesh,
        in_specs=placed,
        out_specs=(
            P("seq", None),
            P("seq", None),
            P(),
            P("seq", None, "head"),
            P(None, "head"),
            P("head", "seq"),
            P(),
            P("seq", "head"),
            P("head"),
            P("head", "seq"),
            P(),
            P(None, None, "head"),
            P(None, "head"),
        ),
        check_vma=False,
    )
```

time: 1100 us -> 437 us (0.40)
  waiting for transfers between devices: 639 us -> 49.5 us
  matrix products: 243 us -> 15.2 us
  Pallas kernels: 0 us -> 142 us
  starting transfers between devices: 20.1 us -> 111 us
  blocking collectives: 75.2 us -> 0 us
  local copies, waits for them, and re-layouts: 16.2 us -> 88.2 us
  other arithmetic: 80.6 us -> 9.08 us
    psum x5 -> x0, waiting for transfers between devices: 458 us -> none  [the longest x1 195 us: on_device(): lax.psum(jnp.dot(act_low, down_weight, preferred_element_type=jnp.float32...]
    dot_general x33 -> x4, matrix products: 243 us -> 15.2 us  [the longest x1 5.74 us: on_device(): jnp.einsum('id,kif->dkf', cond_act.astype(jnp.float32), grad_mod, precisi...]
    reduce_scatter x4 -> x2, waiting for transfers between devices: 180 us -> 0.01 us  [the longest x1 0.01 us: on_device(): lax.psum_scatter(attn_weights(place_rows(spot, grad_attn, jnp.bfloat16),...]
    pallas_call x0 -> x24, Pallas kernels: none -> 142 us  [the longest x2 29.4 us: middle_of(): pl.pallas_call(functools.partial(middle_kernel, count=count, image_count=...]
    ppermute x4 -> x75, starting transfers between devices: 9.81 us -> 111 us  [the longest x71 90.3 us: swap(): return lax.ppermute(value, axis, [(i, i ^ mask) for i in range(count)])]
    unnamed x144 -> x248, local copies, waits for them, and re-layouts: 8.39 us -> 63.4 us
    ppermute x4 -> x75, waiting for transfers between devices: 0.01 us -> 49.4 us  [the longest x71 49.4 us: swap(): return lax.ppermute(value, axis, [(i, i ^ mask) for i in range(count)])]
    reduce_sum x10 -> x3, other arithmetic: 49.8 us -> 0.88 us  [the longest x1 0.63 us: on_device(): grad_ada_bias = jnp.sum(grad_mod, axis=1)]
  transfers between devices with their start and end apart: 13 -> 77, of which waited for: 7 -> 18; matrix products, arithmetic and copies ran while one was open for 8% -> 9% of each run, Pallas kernels for 0% -> 27%
where the time goes in v2:
time: 437 us; the launch traced here: 431 us
  Pallas kernels  142 us (32%)
  starting transfers between devices  111 us (25%)
  local copies, waits for them, and re-layouts  88.2 us (20%)
  waiting for transfers between devices  49.5 us (11%)
  between operations  15.6 us (4%)
  matrix products  15.2 us (3%)
  other arithmetic  9.08 us (2%)
    ppermute x71, starting transfers between devices, swap(): return lax.ppermute(value, axis, [(i, i ^ mask) for i in range(count)])  90.3 us
    unnamed x248, local copies, waits for them, and re-layouts  63.4 us
    ppermute x71, waiting for transfers between devices, swap(): return lax.ppermute(value, axis, [(i, i ^ mask) for i in range(count)])  49.4 us
    pallas_call x2, Pallas kernels, middle_of(): pl.pallas_call(functools.partial(middle_kernel, count=count, image_count=...  29.4 us
    pallas_call x2, Pallas kernels, attend_back(): pl.pallas_call(functools.partial(attend_back_kernel, sources=sources, til...  22 us
    ppermute x4, starting transfers between devices, step_along(): return lax.ppermute(value, axis, pairs)  20.7 us
    pallas_call x2, Pallas kernels, attend(): pl.pallas_call(functools.partial(attend_kernel, sources=tuple(range(len(k...  17.8 us
    pallas_call x4, Pallas kernels, place_rows(): pl.pallas_call(functools.partial(place_kernel, count=count, held=len(chun...  12.6 us
  transfers between devices with their start and end apart: 77, of which 18 were waited for; matrix products, arithmetic and copies ran while one was open for 9% of the time, Pallas kernels for 27%

profile of v2, /device:TPU:0, one launch (start us, length us, event | category | flops | bytes accessed | tf_op | source)
XLA Modules:
  0.0 430.7 jit_solution(2983189184159128633)
XLA Ops:
  27.3 6.5 %shard_map.237 = (bf16[1024,1152]{1,0:T(8,128)(2,1)S(1)}, bf16[1024,288]{1,0:T(8,128)(2,1)S(1)}, bf16[2,1024,288]{2,1,0:T(8,128)(2,1)S(1)}) custom-call(bf16[1024,1152]{1,0:T(8,128)(2,1)S(1)} %copy-done, bf16[1024,48]{1,0:T(8,128)(2,1)S(1)} %get-tuple-element.241.hot_ref.refs_9_.refs_6_.refs_11_.refs_5_, ...), custom_call_target="tpu_custom_call" | custom-call | flops 2038431744 | bytes 8388608 | tf_op jit(solution)/shard_map/pallas_call | solution.py:445
  40.2 4.2 collective-permute-start.3
  56.5 9.8 %shard_map.243 = (bf16[512,288]{1,0:T(8,128)(2,1)S(1)}, f32[288,512]{1,0:T(8,128)S(1)}, f32[4,512]{1,0:T(4,128)S(1)}) custom-call(s32[4]{0:T(128)S(1)} %get-tuple-element.243.low_ref, s32[4]{0:T(128)S(1)} %get-tuple-element.242.high_ref, s32[1,1024]{1,0:T(1,128)S(1)} %bitcast.39, s32[1,1024]{1,0:T(1,128)S(1)} %bitcast.35, bf16[1024,288]{1,0:T(8,128)(2,1)S(1)} %copy-done.106, ...), custom_call_target="tpu_custom_call" | custom-call | flops 2415919104 | bytes 5242880 | tf_op jit(solution)/shard_map/pallas_call | solution.py:164
  69.9 4.9 %shard_map.239 = (bf16[1024,1152]{1,0:T(8,128)(2,1)S(1)}, f32[1024,1152]{1,0:T(8,128)S(1)}, f32[1,1152]{1,0:T(1,128)S(1)}) custom-call(bf16[1024,1152]{1,0:T(8,128)(2,1)S(1)} %copy-done.4, bf16[1024,48]{1,0:T(8,128)(2,1)S(1)} %get-tuple-element.241.hot_ref.refs_9_.refs_6_.refs_11_.refs_5_, ...), custom_call_target="tpu_custom_call" | custom-call | flops 2717908992 | bytes 12582912 | tf_op jit(solution)/shard_map/pallas_call | solution.py:482
  74.9 8.0 %shard_map.238 = (bf16[512,288]{1,0:T(8,128)(2,1)S(1)}, f32[288,512]{1,0:T(8,128)S(1)}, f32[4,512]{1,0:T(4,128)S(1)}) custom-call(s32[4]{0:T(128)S(1)} %get-tuple-element.243.low_ref, s32[4]{0:T(128)S(1)} %get-tuple-element.242.high_ref, s32[1,1024]{1,0:T(1,128)S(1)} %bitcast.40, s32[1,1024]{1,0:T(1,128)S(1)} %bitcast.36, bf16[1024,288]{1,0:T(8,128)(2,1)S(1)} %copy-done.107, ...), custom_call_target="tpu_custom_call" | custom-call | flops 2415919104 | bytes 5242880 | tf_op jit(solution)/shard_map/pallas_call | solution.py:164
  86.5 7.9 %collective-permute-done.18.refs_2_ = bf16[512,288]{1,0:T(8,128)(2,1)S(1)} collective-permute-done((bf16[512,288]{1,0:T(8,128)(2,1)S(1)}, bf16[512,288]{1,0:T(8,128)(2,1)S(1)}, u32[]{:S(2)}, u32[]{:S(2)}) %collective-permute-start.18) | collective-permute-done | bytes 294944 | tf_op jit(solution)/shard_map/ppermute | solution.py:30
  94.4 14.6 %shard_map.244 = (f32[512,1152]{1,0:T(8,128)}, bf16[512,1152]{1,0:T(8,128)(2,1)}, bf16[512,1152]{1,0:T(8,128)(2,1)}, bf16[512,1152]{1,0:T(8,128)(2,1)}, f32[2,16...) custom-call(s32[1]{0:T(128)} %bitcast.spot_ref, ...), custom_call_target="tpu_custom_call" | custom-call | flops 4076863488 | bytes 16777216 | tf_op jit(solution)/shard_map/pallas_call | solution.py:543
  112.6 14.8 %shard_map.240 = (f32[512,1152]{1,0:T(8,128)}, bf16[512,1152]{1,0:T(8,128)(2,1)}, bf16[512,1152]{1,0:T(8,128)(2,1)}, bf16[512,1152]{1,0:T(8,128)(2,1)}, f32[2,16...) custom-call(s32[1]{0:T(128)} %bitcast.spot_ref, ...), custom_call_target="tpu_custom_call" | custom-call | flops 4076863488 | bytes 16777216 | tf_op jit(solution)/shard_map/pallas_call | solution.py:543
  131.8 4.4 %shard_map.249 = (f32[128,1152]{1,0:T(8,128)S(1)}, bf16[128,1152]{1,0:T(8,128)(2,1)}, f32[1,16,1152]{2,1,0:T(8,128)S(1)}, f32[1,1152]{1,0:T(1,128)S(1)}, bf16[12...) custom-call(s32[1]{0:T(128)} %bitcast.spot_ref, ...), custom_call_target="tpu_custom_call" | custom-call | flops 339738624 | bytes 5242880 | tf_op jit(solution)/shard_map/pallas_call | solution.py:665
  153.5 6.4 %shard_map.250 = (f32[288,1024]{1,0:T(8,128)S(1)}, bf16[2,2,1024,288]{3,2,1,0:T(8,128)(2,1)S(1)}) custom-call(s32[4]{0:T(128)S(1)} %copy-done.76, s32[4]{0:T(128)S(1)} %copy-done.73, s32[1]{0:T(128)} %bitcast.spot_ref, s32[1,1024]{1,0:T(1,128)S(1)} %bitcast.41, s32[1,1024]{1,0:T(1,128)S(1)} %bitcast.37, ...), custom_call_target="tpu_custom_call" | custom-call | flops 2415919104 | bytes 10485760 | tf_op jit(solution)/shard_map/pallas_call | solution.py:299
  168.4 13.9 %collective-permute-start.39 = (bf16[2,1024,288]{1,2,0:T(8,128)(2,1)}, bf16[2,1024,288]{1,2,0:T(8,128)(2,1)}, u32[]{:S(2)}, u32[]{:S(2)}) collective-permute-start(bf16[2,1024,288]{1,2,0:T(8,128)(2,1)} %copy.58), channel_id=1, source_target_pairs={{0,4},{4,8},{8,12},{12,16},{16,20},{20,24},{24,28},{1,5},{5,9},{9,... | collective-permute-start | bytes 3538952 | tf_op jit(solution)/shard_map/ppermute | solution.py:66
  200.1 15.5 %shard_map.251 = (bf16[1024,288]{1,0:T(8,128)(2,1)S(1)}, f32[1,2,1024,288]{3,2,1,0:T(8,128)S(1)}) custom-call(s32[4]{0:T(128)S(1)} %copy-done.77, s32[4]{0:T(128)S(1)} %copy-done.74, s32[1]{0:T(128)} %bitcast.spot_ref, s32[1,1024]{1,0:T(1,128)S(1)} %bitcast.42, s32[1,1024]{1,0:T(1,128)S(1)} %bitcast.38, f32[4,1024]{1,0:T(4,128)S(1)} %copy-done.71, ...), custom_call_target="tpu_custom_call" | custom-call | flops 9663676416 | bytes 10485760 | tf_op jit(solution)/shard_map/pallas_call | solution.py:299
  232.8 4.4 %shard_map.254 = (bf16[2,512,288]{2,1,0:T(8,128)(2,1)S(1)}, f32[2,16,1152]{2,1,0:T(8,128)S(1)}, f32[2,288]{1,0:T(2,128)S(1)}, bf16[128,1152]{1,0:T(8,128)(2,1)S(...) custom-call(s32[1]{0:T(128)} %bitcast.spot_ref, ...), custom_call_target="tpu_custom_call" | custom-call | flops 1019215872 | bytes 8388608 | tf_op jit(solution)/shard_map/pallas_call | solution.py:799
  240.1 5.4 %shard_map.252 = (bf16[2,512,288]{2,1,0:T(8,128)(2,1)S(1)}, f32[2,16,1152]{2,1,0:T(8,128)S(1)}, f32[2,288]{1,0:T(2,128)S(1)}, bf16[128,1152]{1,0:T(8,128)(2,1)S(...) custom-call(s32[1]{0:T(128)} %bitcast.spot_ref, ...), custom_call_target="tpu_custom_call" | custom-call | flops 1019215872 | bytes 8388608 | tf_op jit(solution)/shard_map/pallas_call | solution.py:799
  246.9 8.0 %shard_map.259 = bf16[1152,1152]{1,0:T(8,128)(2,1)} custom-call(bf16[1024,1152]{1,0:T(8,128)(2,1)S(1)} %copy-done.16, bf16[1024,1152]{1,0:T(8,128)(2,1)} %copy-done.24, bf16[1024,288]{1,0:T(8,128)(2,1)S(1)} %copy-done.23, bf16[512,288]{1,0:T(8,128)(2,1)S(1)} %copy-done.28, bf16[512,288]{1,0:T(8,128)(2,1)S(1)} %copy-done.26, ...), custom_call_target="tpu_custom_call" | custom-call | flops 2717908992 | bytes 12582912 | tf_op jit(solution)/shard_map/pallas_call | solution.py:926
  261.4 9.9 %shard_map.260 = bf16[1152,2304]{1,0:T(8,128)(2,1)} custom-call(bf16[1024,1152]{1,0:T(8,128)(2,1)} %copy-done.110, bf16[512,1152]{1,0:T(8,128)(2,1)S(1)} %copy-done.80, bf16[512,1152]{1,0:T(8,128)(2,1)S(1)} %copy-done.78, bf16[512,1152]{1,0:T(8,128)(2,1)S(1)} %copy-done.81, bf16[512,1152]{1,0:T(8,128)(2,1)S(1)} %copy-done.79, ...), custom_call_target="tpu_custom_call" | custom-call | flops 5435817984 | bytes 16777216 | tf_op jit(solution)/shard_map/pallas_call | solution.py:894
  313.9 4.4 %collective-permute-start.13 = (bf16[128,1152]{1,0:T(8,128)(2,1)}, bf16[128,1152]{1,0:T(8,128)(2,1)}, u32[]{:S(2)}, u32[]{:S(2)}) collective-permute-start(bf16[128,1152]{1,0:T(8,128)(2,1)} %get-tuple-element.97), channel_id=1, source_target_pairs={{0,3},{1,2},{2,1},{3,0},{4,7},{5,6},{6,5},{7,4},{8,11},{9,10},{10,... | collective-permute-start | bytes 884744 | tf_op jit(solution)/shard_map/ppermute | solution.py:30
  332.7 4.3 collective-permute-start.23
  341.4 7.1 %collective-permute-done.57 = f32[34,288]{1,0:T(8,128)S(1)} collective-permute-done((f32[34,288]{1,0:T(8,128)S(1)}, f32[34,288]{1,0:T(8,128)S(1)}, u32[]{:S(2)}, u32[]{:S(2)}) %collective-permute-start.57) | collective-permute-done | bytes 39200 | tf_op jit(solution)/shard_map/ppermute | solution.py:30
  355.5 5.8 %collective-permute-done.14.refs_1_ = bf16[128,1152]{1,0:T(8,128)(2,1)S(1)} collective-permute-done((bf16[128,1152]{1,0:T(8,128)(2,1)}, bf16[128,1152]{1,0:T(8,128)(2,1)S(1)}, u32[]{:S(2)}, u32[]{:S(2)}) %collective-permute-start.14) | collective-permute-done | bytes 294944 | tf_op jit(solution)/shard_map/ppermute | solution.py:30
  361.2 4.6 %shard_map.247 = bf16[1024,1152]{1,0:T(8,128)(2,1)} custom-call(s32[1]{0:T(128)} %bitcast.spot_ref, bf16[128,1152]{1,0:T(8,128)(2,1)} %shard_map.242.refs_0_, bf16[128,1152]{1,0:T(8,128)(2,1)S(1)} %collective-permute-done.14.refs_1_, bf16[128,1152]{1,0:T(8,128)(2,1)S(1)} %collective-permute-done.15.refs_2_, ...), custom_call_target="tpu_custom_call" | custom-call | bytes 4194304 | tf_op jit(solution)/shard_map/pallas_call | solution.py:850
  379.4 5.0 %collective-permute-done.47.refs_2_ = bf16[128,1152]{1,0:T(8,128)(2,1)S(1)} collective-permute-done((bf16[128,1152]{1,0:T(8,128)(2,1)S(1)}, bf16[128,1152]{1,0:T(8,128)(2,1)S(1)}, u32[]{:S(2)}, u32[]{:S(2)}) %collective-permute-start.47) | collective-permute-done | bytes 294944 | tf_op jit(solution)/shard_map/ppermute | solution.py:30
  387.9 5.7 %fusion.10 = f32[1152,6,288]{0,2,1:T(8,128)} fusion(f32[6,16,288]{2,1,0:T(8,128)S(1)} %bitcast.47, bf16[16,1152]{1,0:T(8,128)(2,1)S(1)} %copy-done.116), kind=kOutput, calls=%fused_computation.55 | convolution fusion | flops 382316544 | bytes 8110080 | tf_op jit(solution)/shard_map/id,kif->dkf/dot_general | solution.py:1090
  402.7 4.5 %collective-permute-start.45 = (bf16[128,1152]{1,0:T(8,128)(2,1)S(1)}, bf16[128,1152]{1,0:T(8,128)(2,1)S(1)}, u32[]{:S(2)}, u32[]{:S(2)}) collective-permute-start(bf16[128,1152]{1,0:T(8,128)(2,1)S(1)} %shard_map.253.refs_0_), channel_id=1, source_target_pairs={{0,3},{1,2},{2,1},{3,0},{4,7},{5,6},{6,5},{7,4},{8,11},{9,10},{10,... | collective-permute-start | bytes 884744 | tf_op jit(solution)/shard_map/ppermute | solution.py:30
  (486 shorter events, 234.9 us)
Async XLA Ops:
  7.2 410.3 %reduce-scatter.3.cloned.1.call-start = ((), (), s32[]{:S(2)}) async-start(), calls=%async_computation.2 | async-start | bytes 2985984 | tf_op jit(solution)/shard_map/reduce_scatter | solution.py:1108
  44.4 24.6 %collective-permute-start.10 = (bf16[288,1152]{1,0:T(8,128)(2,1)}, bf16[288,1152]{1,0:T(8,128)(2,1)}, u32[]{:S(2)}, u32[]{:S(2)}) collective-permute-start(bf16[288,1152]{1,0:T(8,128)(2,1)} %refs_4_.9), channel_id=1, source_target_pairs={{0,3},{1,2},{2,1},{3,0},{4,7},{5,6},{6,5},{7,4},{8,11},{9,10},{10,... | collective-permute-start | bytes 1990664 | tf_op jit(solution)/shard_map/ppermute | solution.py:30
  46.0 37.0 %collective-permute-start.9 = (bf16[288,1152]{1,0:T(8,128)(2,1)}, bf16[288,1152]{1,0:T(8,128)(2,1)}, u32[]{:S(2)}, u32[]{:S(2)}) collective-permute-start(bf16[288,1152]{1,0:T(8,128)(2,1)} %refs_4_.9), channel_id=1, source_target_pairs={{0,2},{1,3},{2,0},{3,1},{4,6},{5,7},{6,4},{7,5},{8,10},{9,11},{10,... | collective-permute-start | bytes 1990664 | tf_op jit(solution)/shard_map/ppermute | solution.py:30
  47.2 37.3 %collective-permute-start.8 = (bf16[288,1152]{1,0:T(8,128)(2,1)}, bf16[288,1152]{1,0:T(8,128)(2,1)}, u32[]{:S(2)}, u32[]{:S(2)}) collective-permute-start(bf16[288,1152]{1,0:T(8,128)(2,1)} %refs_4_.9), channel_id=1, source_target_pairs={{0,1},{1,0},{2,3},{3,2},{4,5},{5,4},{6,7},{7,6},{8,9},{9,8},{10,11... | collective-permute-start | bytes 1990664 | tf_op jit(solution)/shard_map/ppermute | solution.py:30
  67.9 26.5 %collective-permute-start.18 = (bf16[512,288]{1,0:T(8,128)(2,1)S(1)}, bf16[512,288]{1,0:T(8,128)(2,1)S(1)}, u32[]{:S(2)}, u32[]{:S(2)}) collective-permute-start(bf16[512,288]{1,0:T(8,128)(2,1)S(1)} %get-tuple-element.99.refs_0_.refs_1_), channel_id=1, source_target_pairs={{0,2},{1,3},{2,0},{3,1},{4,6},{5,7},{6,4},{7,5},{8,10},{9,11},{10,... | collective-permute-start | bytes 884744 | tf_op jit(solution)/shard_map/ppermute | solution.py:30
  69.1 25.3 %collective-permute-start.17 = (bf16[512,288]{1,0:T(8,128)(2,1)S(1)}, bf16[512,288]{1,0:T(8,128)(2,1)S(1)}, u32[]{:S(2)}, u32[]{:S(2)}) collective-permute-start(bf16[512,288]{1,0:T(8,128)(2,1)S(1)} %get-tuple-element.99.refs_0_.refs_1_), channel_id=1, source_target_pairs={{0,1},{1,0},{2,3},{3,2},{4,5},{5,4},{6,7},{7,6},{8,9},{9,8},{10,11... | collective-permute-start | bytes 884744 | tf_op jit(solution)/shard_map/ppermute | solution.py:30
  83.0 28.2 %collective-permute-start.7 = (bf16[512,288]{1,0:T(8,128)(2,1)S(1)}, bf16[512,288]{1,0:T(8,128)(2,1)S(1)}, u32[]{:S(2)}, u32[]{:S(2)}) collective-permute-start(bf16[512,288]{1,0:T(8,128)(2,1)S(1)} %get-tuple-element.91.refs_0_), channel_id=1, source_target_pairs={{0,3},{1,2},{2,1},{3,0},{4,7},{5,6},{6,5},{7,4},{8,11},{9,10},{10,... | collective-permute-start | bytes 884744 | tf_op jit(solution)/shard_map/ppermute | solution.py:30
  84.5 28.0 %collective-permute-start.6 = (bf16[512,288]{1,0:T(8,128)(2,1)S(1)}, bf16[512,288]{1,0:T(8,128)(2,1)S(1)}, u32[]{:S(2)}, u32[]{:S(2)}) collective-permute-start(bf16[512,288]{1,0:T(8,128)(2,1)S(1)} %get-tuple-element.91.refs_0_), channel_id=1, source_target_pairs={{0,2},{1,3},{2,0},{3,1},{4,6},{5,7},{6,4},{7,5},{8,10},{9,11},{10,... | collective-permute-start | bytes 884744 | tf_op jit(solution)/shard_map/ppermute | solution.py:30
  85.8 26.8 %collective-permute-start.5 = (bf16[512,288]{1,0:T(8,128)(2,1)S(1)}, bf16[512,288]{1,0:T(8,128)(2,1)S(1)}, u32[]{:S(2)}, u32[]{:S(2)}) collective-permute-start(bf16[512,288]{1,0:T(8,128)(2,1)S(1)} %get-tuple-element.91.refs_0_), channel_id=1, source_target_pairs={{0,1},{1,0},{2,3},{3,2},{4,5},{5,4},{6,7},{7,6},{8,9},{9,8},{10,11... | collective-permute-start | bytes 884744 | tf_op jit(solution)/shard_map/ppermute | solution.py:30
  149.6 32.7 %collective-permute-start.71 = (bf16[128,1152]{1,0:T(8,128)(2,1)}, bf16[128,1152]{1,0:T(8,128)(2,1)}, u32[]{:S(2)}, u32[]{:S(2)}) collective-permute-start(bf16[128,1152]{1,0:T(8,128)(2,1)} %get-tuple-element.153.refs_4_), channel_id=1, source_target_pairs={{0,3},{1,2},{2,1},{3,0},{4,7},{5,6},{6,5},{7,4},{8,11},{9,10},{10,... | collective-permute-start | bytes 884744 | tf_op jit(solution)/shard_map/ppermute | solution.py:30
  151.0 32.5 %collective-permute-start.70 = (bf16[128,1152]{1,0:T(8,128)(2,1)}, bf16[128,1152]{1,0:T(8,128)(2,1)}, u32[]{:S(2)}, u32[]{:S(2)}) collective-permute-start(bf16[128,1152]{1,0:T(8,128)(2,1)} %get-tuple-element.153.refs_4_), channel_id=1, source_target_pairs={{0,2},{1,3},{2,0},{3,1},{4,6},{5,7},{6,4},{7,5},{8,10},{9,11},{10,... | collective-permute-start | bytes 884744 | tf_op jit(solution)/shard_map/ppermute | solution.py:30
  152.1 32.1 %collective-permute-start.69 = (bf16[128,1152]{1,0:T(8,128)(2,1)}, bf16[128,1152]{1,0:T(8,128)(2,1)}, u32[]{:S(2)}, u32[]{:S(2)}) collective-permute-start(bf16[128,1152]{1,0:T(8,128)(2,1)} %get-tuple-element.153.refs_4_), channel_id=1, source_target_pairs={{0,1},{1,0},{2,3},{3,2},{4,5},{5,4},{6,7},{7,6},{8,9},{9,8},{10,11... | collective-permute-start | bytes 884744 | tf_op jit(solution)/shard_map/ppermute | solution.py:30
  164.6 55.6 %collective-permute-start.38 = (bf16[2,1024,288]{1,2,0:T(8,128)(2,1)}, bf16[2,1024,288]{1,2,0:T(8,128)(2,1)}, u32[]{:S(2)}, u32[]{:S(2)}) collective-permute-start(bf16[2,1024,288]{1,2,0:T(8,128)(2,1)} %copy.57), channel_id=1, source_target_pairs={{4,0},{8,4},{12,8},{16,12},{20,16},{24,20},{28,24},{5,1},{9,5},{13... | collective-permute-start | bytes 3538952 | tf_op jit(solution)/shard_map/ppermute | solution.py:66
  168.4 54.4 %collective-permute-start.39 = (bf16[2,1024,288]{1,2,0:T(8,128)(2,1)}, bf16[2,1024,288]{1,2,0:T(8,128)(2,1)}, u32[]{:S(2)}, u32[]{:S(2)}) collective-permute-start(bf16[2,1024,288]{1,2,0:T(8,128)(2,1)} %copy.58), channel_id=1, source_target_pairs={{0,4},{4,8},{8,12},{12,16},{16,20},{20,24},{24,28},{1,5},{5,9},{9,... | collective-permute-start | bytes 3538952 | tf_op jit(solution)/shard_map/ppermute | solution.py:66
  182.3 33.3 %collective-permute-start.68 = (bf16[128,1152]{1,0:T(8,128)(2,1)}, bf16[128,1152]{1,0:T(8,128)(2,1)S(1)}, u32[]{:S(2)}, u32[]{:S(2)}) collective-permute-start(bf16[128,1152]{1,0:T(8,128)(2,1)} %copy-done.48), channel_id=1, source_target_pairs={{0,3},{1,2},{2,1},{3,0},{4,7},{5,6},{6,5},{7,4},{8,11},{9,10},{10,... | collective-permute-start | bytes 884744 | tf_op jit(solution)/shard_map/ppermute | solution.py:30
  183.4 32.2 %collective-permute-start.67 = (bf16[128,1152]{1,0:T(8,128)(2,1)}, bf16[128,1152]{1,0:T(8,128)(2,1)S(1)}, u32[]{:S(2)}, u32[]{:S(2)}) collective-permute-start(bf16[128,1152]{1,0:T(8,128)(2,1)} %copy-done.48), channel_id=1, source_target_pairs={{0,2},{1,3},{2,0},{3,1},{4,6},{5,7},{6,4},{7,5},{8,10},{9,11},{10,... | collective-permute-start | bytes 884744 | tf_op jit(solution)/shard_map/ppermute | solution.py:30
  184.2 31.4 %collective-permute-start.66 = (bf16[128,1152]{1,0:T(8,128)(2,1)}, bf16[128,1152]{1,0:T(8,128)(2,1)S(1)}, u32[]{:S(2)}, u32[]{:S(2)}) collective-permute-start(bf16[128,1152]{1,0:T(8,128)(2,1)} %copy-done.48), channel_id=1, source_target_pairs={{0,1},{1,0},{2,3},{3,2},{4,5},{5,4},{6,7},{7,6},{8,9},{9,8},{10,11... | collective-permute-start | bytes 884744 | tf_op jit(solution)/shard_map/ppermute | solution.py:30
  254.9 165.7 %reduce-scatter.5.cloned.1.call-start = ((), (), s32[]{:S(2)}) async-start(), calls=%async_computation.3 | async-start | bytes 5971968 | tf_op jit(solution)/shard_map/reduce_scatter | solution.py:1105
  328.4 24.1 %collective-permute-start.25 = (bf16[128,1152]{1,0:T(8,128)(2,1)}, bf16[128,1152]{1,0:T(8,128)(2,1)}, u32[]{:S(2)}, u32[]{:S(2)}) collective-permute-start(bf16[128,1152]{1,0:T(8,128)(2,1)} %shard_map.246.refs_4_), channel_id=1, source_target_pairs={{0,3},{1,2},{2,1},{3,0},{4,7},{5,6},{6,5},{7,4},{8,11},{9,10},{10,... | collective-permute-start | bytes 884744 | tf_op jit(solution)/shard_map/ppermute | solution.py:30
  330.1 24.6 %collective-permute-start.24 = (bf16[128,1152]{1,0:T(8,128)(2,1)}, bf16[128,1152]{1,0:T(8,128)(2,1)}, u32[]{:S(2)}, u32[]{:S(2)}) collective-permute-start(bf16[128,1152]{1,0:T(8,128)(2,1)} %shard_map.246.refs_4_), channel_id=1, source_target_pairs={{0,2},{1,3},{2,0},{3,1},{4,6},{5,7},{6,4},{7,5},{8,10},{9,11},{10,... | collective-permute-start | bytes 884744 | tf_op jit(solution)/shard_map/ppermute | solution.py:30
  370.0 24.9 %collective-permute-start.40 = (bf16[128,1152]{1,0:T(8,128)(2,1)}, bf16[128,1152]{1,0:T(8,128)(2,1)}, u32[]{:S(2)}, u32[]{:S(2)}) collective-permute-start(bf16[128,1152]{1,0:T(8,128)(2,1)} %get-tuple-element.131), channel_id=1, source_target_pairs={{0,1},{1,0},{2,3},{3,2},{4,5},{5,4},{6,7},{7,6},{8,9},{9,8},{10,11... | collective-permute-start | bytes 884744 | tf_op jit(solution)/shard_map/ppermute | solution.py:30
  371.7 27.3 %collective-permute-start.41 = (bf16[128,1152]{1,0:T(8,128)(2,1)}, bf16[128,1152]{1,0:T(8,128)(2,1)}, u32[]{:S(2)}, u32[]{:S(2)}) collective-permute-start(bf16[128,1152]{1,0:T(8,128)(2,1)} %get-tuple-element.132), channel_id=1, source_target_pairs={{0,2},{1,3},{2,0},{3,1},{4,6},{5,7},{6,4},{7,5},{8,10},{9,11},{10,... | collective-permute-start | bytes 884744 | tf_op jit(solution)/shard_map/ppermute | solution.py:30
  376.1 22.9 %collective-permute-start.42 = (bf16[128,1152]{1,0:T(8,128)(2,1)}, bf16[128,1152]{1,0:T(8,128)(2,1)}, u32[]{:S(2)}, u32[]{:S(2)}) collective-permute-start(bf16[128,1152]{1,0:T(8,128)(2,1)} %get-tuple-element.133), channel_id=1, source_target_pairs={{0,3},{1,2},{2,1},{3,0},{4,7},{5,6},{6,5},{7,4},{8,11},{9,10},{10,... | collective-permute-start | bytes 884744 | tf_op jit(solution)/shard_map/ppermute | solution.py:30
  384.3 22.9 %collective-permute-start.65 = (f32[17,1152]{1,0:T(8,128)S(1)}, f32[17,1152]{1,0:T(8,128)}, u32[]{:S(2)}, u32[]{:S(2)}) collective-permute-start(f32[17,1152]{1,0:T(8,128)S(1)} %fusion.19), channel_id=1, source_target_pairs={{0,2},{1,3},{2,0},{3,1},{4,6},{5,7},{6,4},{7,5},{8,10},{9,11},{10,... | collective-permute-start | bytes 235016 | tf_op jit(solution)/shard_map/ppermute | solution.py:30
  (175 other events, 1464.1 us)
Sparse Core Ops, SparseCore 0:
  255.1 37.3 reduce-scatter.2
  294.8 67.1 reduce-scatter.4

commit v3 on v0

v3 whole, which is shorter than its diff:
```python
import functools

import jax
import jax.numpy as jnp
from jax import lax
from jax.experimental import pallas as pl
from jax.experimental.pallas import tpu as pltpu
from jax.sharding import PartitionSpec as P

HDIM = 72


EPSILON = 1e-06
MASKED = -1e30
PRECISE = lax.Precision.HIGHEST
CHUNKS = 2
KEY_TILE = 512
QUERY_BLOCK = 256
ROW_BLOCK = 256
ROOT = 0.7978845608028654
CUBIC = 0.044715
LOG2E = 1.4426950408889634
MIB = 1 << 20
PACE = 1.15e9


def peers(axis):
    return range(1, lax.axis_size(axis))


def swap(value, axis, mask):
    count = lax.axis_size(axis)
    return lax.ppermute(value, axis, [(i, i ^ mask) for i in range(count)])


def gather_pieces(value, axis):
    return [value] + [swap(value, axis, mask) for mask in peers(axis)]


def fold_pieces(stack, axis):
    amount = stack.shape[0]
    while amount > 1:
        amount //= 2
        stack = stack[:amount] + swap(stack[amount:], axis, amount)
    return stack[0]


def swap_pieces(pieces, axis):
    return [pieces[0]] + [swap(pieces[mask], axis, mask) for mask in peers(axis)]


def butterfly_sum(value, axis):
    mask = 1
    while mask < lax.axis_size(axis):
        value = value + swap(value, axis, mask)
        mask *= 2
    return value


def step_along(value, axis, ahead):
    count = lax.axis_size(axis)
    pairs = [(i, i + 1) if ahead else (i + 1, i) for i in range(count - 1)]
    return lax.ppermute(value, axis, pairs)


def three_parts(values):
    first = lax.reduce_precision(values, 8, 7)
    second = lax.reduce_precision(values - first, 8, 7)
    third = values - first - second
    return [part.astype(jnp.bfloat16) for part in (first, second, third)]


def pick(which, cases):
    result = cases[0]
    for number, case in enumerate(cases[1:], 1):
        result = jnp.where(which == number, case, result)
    return result


def tied_call(
    kernel, prefetch, operands, after, *, grid, in_specs, out_specs, out_shape, vmem, cost,
    scratch_shapes=(), into=(),
):
    after = [*into, *after]
    count, ties = len(prefetch), len(after)

    def body(*refs):
        return kernel(*refs[:count], *refs[count + ties :])

    return pl.pallas_call(
        body,
        grid_spec=pltpu.PrefetchScalarGridSpec(
            num_scalar_prefetch=count,
            grid=grid,
            in_specs=[pl.BlockSpec(memory_space=pl.ANY)] * ties + in_specs,
            out_specs=out_specs,
            scratch_shapes=scratch_shapes,
        ),
        out_shape=out_shape,
        input_output_aliases={count + number: number for number in range(len(into))},
        compiler_params=pltpu.CompilerParams(vmem_limit_bytes=vmem * MIB),
        cost_estimate=cost,
    )(*prefetch, *after, *operands)


def cost(micros):
    return pl.CostEstimate(
        flops=max(1, int(micros * PACE)), bytes_accessed=1, transcendentals=0
    )


def fixed(shape):
    return pl.BlockSpec(shape, lambda i, *_: (0,) * len(shape))


def held(shape):
    return pl.BlockSpec(
        shape, lambda i, *_: (0,) * len(shape), pipeline_mode=pl.Buffered(buffer_count=1)
    )


def down(rows, width, base=0):
    return pl.BlockSpec((rows, width), lambda i, *_: (base + i, 0))


def owned(rows, width, base):
    return pl.BlockSpec((rows, width), lambda i, spot: (base + spot[0], 0))


def column(table_rows, width, component):
    return pl.BlockSpec(
        (None, table_rows, width),
        lambda i, *_: (component, 0, 0),
        pipeline_mode=pl.Buffered(buffer_count=1),
    )


def whole_lanes(width):
    return -(-width // 128) * 128


def shaped(shape, kind=jnp.bfloat16):
    return jax.ShapeDtypeStruct(shape, kind)


def rows_dot(left, right):
    return lax.dot_general(
        left, right, (((1,), (1,)), ((), ())), preferred_element_type=jnp.float32
    )


def turned_dot(left, right):
    return lax.dot_general(
        left, right, (((0,), (0,)), ((), ())), preferred_element_type=jnp.float32
    )


def normed_rows(values):
    center = values - jnp.mean(values, axis=-1, keepdims=True)
    inverse = lax.rsqrt(jnp.mean(center * center, axis=-1, keepdims=True) + EPSILON)
    return center * inverse, inverse


def norm_back_rows(gradient, normed, inverse):
    return (
        gradient
        - jnp.mean(gradient, axis=-1, keepdims=True)
        - normed * jnp.mean(gradient * normed, axis=-1, keepdims=True)
    ) * inverse


def spread(hot_ref, table_ref):
    return jnp.dot(hot_ref[...], table_ref[...], preferred_element_type=jnp.float32)


def add_image_sums(sum_ref, spot, hot_ref, image_count, values):
    hot = hot_ref[:, :image_count]
    first = values.astype(jnp.bfloat16)
    second = (values - first.astype(jnp.float32)).astype(jnp.bfloat16)
    sum_ref[spot] += turned_dot(hot, first) + turned_dot(hot, second)


def clear_at_start(*refs):
    @pl.when(pl.program_id(0) == 0)
    def _():
        for ref in refs:
            ref[...] = jnp.zeros_like(ref)


def hand_out(spot_ref, outs, values, own):
    amount = values.shape[0] // own
    for place in range(amount):
        target = pl.program_id(0) * amount + place
        piece = values[place * own : (place + 1) * own, :].astype(outs[0].dtype)
        rows = pl.ds(pl.multiple_of(target // len(outs) * own, own), own)
        for mask, out in enumerate(outs):

            @pl.when(target % len(outs) == spot_ref[0] ^ mask)
            def _(out=out, piece=piece, rows=rows):
                out[rows, :] = piece


def sum_of(pieces):
    total = pieces[0][...].astype(jnp.float32)
    for piece in pieces[1:]:
        total = total + piece[...].astype(jnp.float32)
    return total


def head_window(place, features):
    start = place // 128 * 128
    return slice(start, min(features, start + 256))


def head_only(block, place):
    lanes = head_window(place, block.shape[1])
    window = block[:, lanes]
    lane = lax.broadcasted_iota(jnp.int32, window.shape, 1) + (lanes.start - place)
    return jnp.where((lane >= 0) & (lane < HDIM), window, jnp.zeros_like(window))


def visible_keys(first_ref, length_ref, base, tile_rows):
    first = first_ref[...] - base
    place = lax.broadcasted_iota(jnp.int32, (tile_rows, first.shape[1]), 0)
    offset = place - first
    return (offset >= 0) & (offset < length_ref[...])


def each_tile(low, high, source, tiles, body):
    lax.fori_loop(
        jnp.maximum(low, source * tiles),
        jnp.minimum(high, (source + 1) * tiles),
        lambda number, carry: body(number, carry),
        0,
    )


def attend_kernel(
    low_ref, high_ref, first_ref, length_ref, query_ref, *refs, tile, step_base
):
    kv_refs = refs[:3]
    low_out, wide_out, log_out, total, row_max, row_sum = refs[3:]
    features = query_ref.shape[1]
    heads = features // HDIM
    step = pl.program_id(0) + step_base
    queries = [head_only(query_ref[...], head * HDIM) for head in range(heads)]
    rescale = HDIM ** (-0.5) * LOG2E
    value_start = features // 128 * 128
    total[...] = jnp.zeros_like(total)
    row_max[...] = jnp.full_like(row_max, MASKED)
    row_sum[...] = jnp.zeros_like(row_sum)
    for source, kv_ref in enumerate(kv_refs):
        tiles = kv_ref.shape[0] // tile

        def body(number, carry, source=source, kv_ref=kv_ref, tiles=tiles):
            rows = pl.ds(pl.multiple_of((number - source * tiles) * tile, tile), tile)
            keys = kv_ref[rows, :features]
            values = kv_ref[rows, value_start:].astype(jnp.float32).T
            seen = visible_keys(first_ref, length_ref, number * tile, tile)
            for head in range(heads):
                scores = rows_dot(keys[:, head_window(head * HDIM, features)], queries[head])
                scores = jnp.where(seen, scores, MASKED)
                old = row_max[head : head + 1, :]
                new = jnp.maximum(old, jnp.max(scores, axis=0, keepdims=True))
                shrink = jnp.exp2((old - new) * rescale)
                shares = jnp.exp2((scores - new) * rescale)
                row_max[head : head + 1, :] = new
                row_sum[head : head + 1, :] = row_sum[
                    head : head + 1, :
                ] * shrink + jnp.sum(shares, axis=0, keepdims=True)
                mine = slice(head * HDIM, (head + 1) * HDIM)
                place = features - value_start + head * HDIM
                total[mine, :] = total[mine, :] * shrink + jnp.dot(
                    values[place : place + HDIM, :].astype(jnp.bfloat16),
                    shares.astype(jnp.bfloat16),
                    preferred_element_type=jnp.float32,
                )
            return carry

        each_tile(low_ref[step], high_ref[step], source, tiles, body)
    log_out[...] = row_max[...] * rescale + jnp.log2(row_sum[...])
    for head in range(heads):
        mine = slice(head * HDIM, (head + 1) * HDIM)
        total[mine, :] = total[mine, :] / row_sum[head : head + 1, :]
    wide_out[...] = total[...]
    low_out[...] = total[...].T.astype(jnp.bfloat16)


def attend(ranges, query, kvs, tile, block, chunk, chunks, after):
    lows, highs, firsts, lengths = ranges
    rows, features = query.shape
    heads = features // HDIM
    amount = rows // chunks
    steps = amount // block
    base = chunk * steps
    across = pl.BlockSpec((1, block), lambda i, *_: (0, base + i))
    return tied_call(
        functools.partial(attend_kernel, tile=tile, step_base=base),
        (lows, highs),
        (firsts, lengths, query, *kvs),
        after,
        grid=(steps,),
        in_specs=[across, across, down(block, features, base)] + [held(kvs[0].shape)] * 3,
        out_specs=[
            down(block, features),
            pl.BlockSpec((features, block), lambda i, *_: (0, i)),
            pl.BlockSpec((heads, block), lambda i, *_: (0, i)),
        ],
        out_shape=[
            shaped((amount, features)),
            shaped((features, amount), jnp.float32),
            shaped((heads, amount), jnp.float32),
        ],
        scratch_shapes=[
            pltpu.VMEM((features, block), jnp.float32),
            pltpu.VMEM((heads, block), jnp.float32),
            pltpu.VMEM((heads, block), jnp.float32),
        ],
        vmem=16,
        cost=cost(10),
    )


def attend_back_steps(
    step, low_ref, high_ref, first_ref, length_ref, log_ref, query_ref, grad_rows, wide, kv_refs,
    sources, total, kv_totals, tile,
):
    features = query_ref.shape[1]
    heads = features // HDIM
    rescale = HDIM ** (-0.5) * LOG2E
    queries = [head_only(query_ref[...], head * HDIM) for head in range(heads)]
    shifted = jnp.concatenate([jnp.zeros_like(grad_rows), grad_rows], axis=1)
    grads = [head_only(shifted, features + head * HDIM) for head in range(heads)]
    products = grad_rows.astype(jnp.float32).T * wide
    deltas = [
        jnp.sum(products[head * HDIM : (head + 1) * HDIM, :], axis=0, keepdims=True)
        for head in range(heads)
    ]
    for source, kv_ref, kv_total in zip(sources, kv_refs, kv_totals):
        tiles = kv_ref.shape[0] // tile

        def body(number, carry, source=source, kv_ref=kv_ref, kv_total=kv_total, tiles=tiles):
            rows = pl.ds(pl.multiple_of((number - source * tiles) * tile, tile), tile)
            pairs = kv_ref[rows, :]
            keys_down = kv_ref[rows, :features].astype(jnp.float32).T
            seen = visible_keys(first_ref, length_ref, number * tile, tile)
            for head in range(heads):
                key_lanes = head_window(head * HDIM, features)
                value_lanes = head_window(features + head * HDIM, 2 * features)
                scores = rows_dot(pairs[:, key_lanes], queries[head])
                shares = jnp.where(
                    seen, jnp.exp2(scores * rescale - log_ref[head : head + 1, :]), 0.0
                )
                grad_shares = rows_dot(pairs[:, value_lanes], grads[head])
                grad_scores = (shares * (grad_shares - deltas[head])).astype(jnp.bfloat16)
                kv_total[rows, value_lanes] += jnp.dot(
                    shares.astype(jnp.bfloat16), grads[head], preferred_element_type=jnp.float32
                )
                kv_total[rows, key_lanes] += jnp.dot(
                    grad_scores, queries[head], preferred_element_type=jnp.float32
                )
                mine = slice(head * HDIM, (head + 1) * HDIM)
                total[mine, :] += jnp.dot(
                    keys_down[mine, :].astype(jnp.bfloat16),
                    grad_scores,
                    preferred_element_type=jnp.float32,
                )
            return carry

        each_tile(low_ref[step], high_ref[step], source, tiles, body)


def write_pairs(out, kv_total, features):
    values = kv_total[...]
    lane = lax.broadcasted_iota(jnp.int32, values.shape, 1)
    out[...] = jnp.where(lane < features, values * HDIM ** (-0.5), values).astype(out.dtype)


def attend_far_kernel(
    low_ref, high_ref, spot_ref, first_ref, length_ref, log_ref, query_ref, wide_ref, before_ref,
    after_ref, *refs, tile, count,
):
    pieces = refs[:-7]
    query_out, grad_out, before_out, after_out, total, before_total, after_total = refs[-7:]
    step = pl.program_id(0)
    block, features = query_ref.shape
    piece_rows = pieces[0].shape[0]
    clear_at_start(before_total, after_total)
    total[...] = jnp.zeros_like(total)
    parts = []
    for place in range(block // piece_rows):
        target = step * (block // piece_rows) + place
        part = jnp.zeros_like(pieces[0][...])
        for number, piece in enumerate(pieces):
            owner = (spot_ref[0] ^ (number % count)) + number // count * count
            part = jnp.where(target == owner, piece[...], part)
        parts.append(part)
    grad_rows = jnp.concatenate(parts, axis=0)
    grad_out[...] = grad_rows
    attend_back_steps(
        step, low_ref, high_ref, first_ref, length_ref, log_ref, query_ref, grad_rows,
        wide_ref[...], (before_ref, after_ref), (0, 2), total, (before_total, after_total), tile,
    )
    query_out[...] = total[...]

    @pl.when(step == pl.num_programs(0) - 1)
    def _():
        write_pairs(before_out, before_total, features)
        write_pairs(after_out, after_total, features)


def attend_near_kernel(
    low_ref, high_ref, first_ref, length_ref, log_ref, query_ref, wide_ref, kv_ref, grad_ref,
    start_ref, query_out, kv_out, total, kv_total, *, tile,
):
    step = pl.program_id(0)
    clear_at_start(kv_total)
    total[...] = start_ref[...]
    attend_back_steps(
        step, low_ref, high_ref, first_ref, length_ref, log_ref, query_ref, grad_ref[...],
        wide_ref[...], (kv_ref,), (1,), total, (kv_total,), tile,
    )
    query_out[...] = (total[...].T * HDIM ** (-0.5)).astype(query_out.dtype)

    @pl.when(step == pl.num_programs(0) - 1)
    def _():
        write_pairs(kv_out, kv_total, query_ref.shape[1])


def attend_far(spot, ranges, logs, query, grads, wide, before, later, tile, block, after):
    lows, highs, firsts, lengths = ranges
    pieces = [piece for chunk in grads for piece in chunk]
    rows, features = query.shape
    across = pl.BlockSpec((1, block), lambda i, *_: (0, i))
    turned = pl.BlockSpec((features, block), lambda i, *_: (0, i))
    logged = pl.BlockSpec((features // HDIM, block), lambda i, *_: (0, i))
    pairs = (rows, whole_lanes(2 * features))
    return tied_call(
        functools.partial(attend_far_kernel, tile=tile, count=len(grads[0])),
        (lows, highs, spot),
        (firsts, lengths, logs, query, wide, before, later, *pieces),
        after,
        grid=(rows // block,),
        in_specs=[across, across, logged, down(block, features), turned, held(pairs), held(pairs)]
        + [held(pieces[0].shape)] * len(pieces),
        out_specs=[turned, down(block, features), fixed(pairs), fixed(pairs)],
        out_shape=[
            shaped((features, rows), jnp.float32),
            shaped((rows, features)),
            shaped(pairs),
            shaped(pairs),
        ],
        scratch_shapes=[
            pltpu.VMEM((features, block), jnp.float32),
            pltpu.VMEM(pairs, jnp.float32),
            pltpu.VMEM(pairs, jnp.float32),
        ],
        vmem=28,
        cost=cost(8),
    )


def attend_near(ranges, logs, query, grad, wide, kv, started, tile, block, after):
    lows, highs, firsts, lengths = ranges
    rows, features = query.shape
    across = pl.BlockSpec((1, block), lambda i, *_: (0, i))
    turned = pl.BlockSpec((features, block), lambda i, *_: (0, i))
    logged = pl.BlockSpec((features // HDIM, block), lambda i, *_: (0, i))
    pairs = (rows, whole_lanes(2 * features))
    return tied_call(
        functools.partial(attend_near_kernel, tile=tile),
        (lows, highs),
        (firsts, lengths, logs, query, wide, kv, grad, started),
        after,
        grid=(rows // block,),
        in_specs=[
            across, across, logged, down(block, features), turned, held(pairs),
            down(block, features), turned,
        ],
        out_specs=[down(block, features), fixed(pairs)],
        out_shape=[shaped((rows, features)), shaped(pairs, jnp.float32)],
        scratch_shapes=[
            pltpu.VMEM((features, block), jnp.float32),
            pltpu.VMEM(pairs, jnp.float32),
        ],
        vmem=24,
        cost=cost(16),
    )


def key_ranges(my_images, wide_images, image_count, tile, block):
    images = jnp.arange(image_count, dtype=jnp.int32)
    before = jnp.sum((wide_images[None, :] < images[:, None]).astype(jnp.int32), axis=1)
    amount = jnp.sum((wide_images[None, :] == images[:, None]).astype(jnp.int32), axis=1)
    mine = (my_images[None, :] == images[:, None]).astype(jnp.int32)
    firsts = jnp.sum(mine * before[:, None], axis=0)
    lengths = jnp.sum(mine * amount[:, None], axis=0)
    ends = firsts + lengths
    lows = firsts[::block] // tile
    highs = (ends[block - 1 :: block] + tile - 1) // tile
    return lows, highs, firsts[None, :], lengths[None, :]


def project_kernel(
    token_ref, hot_ref, shift_ref, scale_ref, weight_ref, bias_ref, hidden_out, query_out, kv_out
):
    features = query_out.shape[1]
    normed, _ = normed_rows(token_ref[...].astype(jnp.float32))
    hidden = normed * (1.0 + spread(hot_ref, scale_ref)) + spread(hot_ref, shift_ref)
    hidden = hidden.astype(jnp.bfloat16)
    hidden_out[...] = hidden
    projected = jnp.dot(hidden, weight_ref[...], preferred_element_type=jnp.float32)
    projected = (projected + bias_ref[...]).astype(jnp.bfloat16)
    query_out[...] = projected[:, :features]
    spare = kv_out.shape[1] - 2 * features
    empty = jnp.zeros((projected.shape[0], spare), projected.dtype)
    kv_out[...] = jnp.concatenate([projected[:, features:], empty][: 1 + (spare > 0)], axis=1)


def project(tokens, hot, table, weight, bias, block, after):
    rows, width = tokens.shape
    features = weight.shape[1] // 3
    high = table.shape[1]
    return tied_call(
        project_kernel,
        (),
        (tokens, hot, table, table, weight, bias),
        after,
        grid=(rows // block,),
        in_specs=[
            down(block, width),
            down(block, hot.shape[1]),
            column(high, width, 0),
            column(high, width, 1),
            held(weight.shape),
            held(bias.shape),
        ],
        out_specs=[
            down(block, width),
            down(block, features),
            down(block, whole_lanes(2 * features)),
        ],
        out_shape=[
            shaped((rows, width)),
            shaped((rows, features)),
            shaped((rows, whole_lanes(2 * features))),
        ],
        vmem=20,
        cost=cost(6),
    )


def grad_act_kernel(
    cot_ref, hot_ref, gate_ref, weight_ref, grad_out, act_out, bias_out, sum_out, *, image_count
):
    clear_at_start(bias_out, sum_out)
    cot = cot_ref[...]
    grad = (spread(hot_ref, gate_ref) * cot.astype(jnp.float32)).astype(jnp.bfloat16)
    grad_out[...] = grad
    bias_out[...] += jnp.sum(grad.astype(jnp.float32), axis=0, keepdims=True)
    sum_out[...] += turned_dot(hot_ref[:, :image_count], cot)
    act_out[...] = rows_dot(grad, weight_ref[...])


def grad_act_of(cotangent, hot, table, weight, image_count, block, after):
    rows, width = cotangent.shape
    units = weight.shape[0]
    return tied_call(
        functools.partial(grad_act_kernel, image_count=image_count),
        (),
        (cotangent, hot, table, weight),
        after,
        grid=(rows // block,),
        in_specs=[
            down(block, width),
            down(block, hot.shape[1]),
            column(table.shape[1], width, 5),
            held(weight.shape),
        ],
        out_specs=[
            down(block, width),
            down(block, units),
            fixed((1, width)),
            fixed((image_count, width)),
        ],
        out_shape=[
            shaped((rows, width)),
            shaped((rows, units), jnp.float32),
            shaped((1, width), jnp.float32),
            shaped((image_count, width), jnp.float32),
        ],
        vmem=20,
        cost=cost(5),
    )


def peer_rows(spot_ref, mask, rows):
    return pl.ds(pl.multiple_of((spot_ref[0] ^ mask) * rows, rows), rows)


def middle_kernel(spot_ref, *refs, count, image_count):
    pieces = refs[:count]
    (
        out_ref, token_ref, hot_ref, gate_ref, shift_ref, scale_ref, out_bias_ref, up_ref,
        up_bias_ref, grad_act_ref, attn_out, hidden_out, act_out, grad_out, sum_out, bias_out,
    ) = refs[count:-count]
    clear_at_start(sum_out, bias_out)
    attn = out_bias_ref[...].astype(jnp.float32)
    for mask, piece in enumerate(pieces):
        rows = peer_rows(spot_ref, mask, piece.shape[1])
        attn = attn + jnp.dot(piece[...], out_ref[rows, :], preferred_element_type=jnp.float32)
    attn_out[...] = attn
    middle = token_ref[...].astype(jnp.float32) + spread(hot_ref, gate_ref) * attn
    normed, _ = normed_rows(middle)
    hidden = normed * (1.0 + spread(hot_ref, scale_ref)) + spread(hot_ref, shift_ref)
    hidden = hidden.astype(jnp.bfloat16)
    hidden_out[...] = hidden
    pre = jnp.dot(hidden, up_ref[...], preferred_element_type=jnp.float32)
    pre = pre + up_bias_ref[...].astype(jnp.float32)
    square = pre * pre
    bend = jnp.tanh(ROOT * pre * (1.0 + CUBIC * square))
    half = 0.5 * (1.0 + bend)
    act_out[...] = (pre * half).astype(jnp.bfloat16)
    slope = half + 0.5 * ROOT * pre * (1.0 - bend * bend) * (1.0 + 3.0 * CUBIC * square)
    grad = (grad_act_ref[...] * slope).astype(jnp.bfloat16)
    grad_out[...] = grad
    bias_out[...] += jnp.sum(grad.astype(jnp.float32), axis=0, keepdims=True)
    part = rows_dot(grad, up_ref[...])
    hand_out(spot_ref, refs[-count:], part, refs[-1].shape[0])
    add_image_sums(sum_out, 0, hot_ref, image_count, part)
    add_image_sums(sum_out, 1, hot_ref, image_count, part * normed)


def middle_of(
    spot, pieces, tokens, hot, table, out_full, out_bias, up_weight, up_bias, grad_act,
    image_count, block, chunk, into, after,
):
    rows, features = pieces[0].shape
    width, units = up_weight.shape
    whole = tokens.shape[0]
    high = table.shape[1]
    count = len(pieces)
    base = chunk * (rows // block)
    return tied_call(
        functools.partial(middle_kernel, count=count, image_count=image_count),
        (spot,),
        (
            *pieces, out_full, tokens, hot, table, table, table, out_bias, up_weight, up_bias,
            grad_act,
        ),
        after,
        grid=(rows // block,),
        in_specs=[down(block, features)] * count
        + [
            held(out_full.shape),
            down(block, width, base),
            down(block, hot.shape[1], base),
            column(high, width, 2),
            column(high, width, 3),
            column(high, width, 4),
            held(out_bias.shape),
            held(up_weight.shape),
            held(up_bias.shape),
            down(block, units, base),
        ],
        out_specs=[
            down(block, width, base),
            down(block, width, base),
            down(block, units, base),
            down(block, units, base),
            fixed((2, image_count, width)),
            fixed((1, units)),
        ]
        + [fixed((rows // count, width))] * count,
        into=into,
        out_shape=[
            shaped((whole, width), jnp.float32),
            shaped((whole, width)),
            shaped((whole, units)),
            shaped((whole, units)),
            shaped((2, image_count, width), jnp.float32),
            shaped((1, units), jnp.float32),
        ]
        + [shaped((rows // count, width))] * count,
        vmem=36,
        cost=cost(12),
    )


def mlp_kernel(act_ref, weight_ref, cot_ref, hot_ref, part_out, sum_out, *, image_count):
    clear_at_start(sum_out)
    part = jnp.dot(act_ref[...], weight_ref[...], preferred_element_type=jnp.float32)
    part_out[...] = part.astype(jnp.bfloat16)
    add_image_sums(sum_out, 0, hot_ref, image_count, part * cot_ref[...].astype(jnp.float32))


def mlp_of(act, weight, cotangent, hot, image_count, block, after):
    rows, units = act.shape
    width = weight.shape[1]
    return tied_call(
        functools.partial(mlp_kernel, image_count=image_count),
        (),
        (act, weight, cotangent, hot),
        after,
        grid=(rows // block,),
        in_specs=[
            down(block, units),
            held(weight.shape),
            down(block, width),
            down(block, hot.shape[1]),
        ],
        out_specs=[down(block, width), fixed((1, image_count, width))],
        out_shape=[shaped((rows, width)), shaped((1, image_count, width), jnp.float32)],
        vmem=20,
        cost=cost(6),
    )


def grad_middle_kernel(spot_ref, *refs, count, image_count):
    pieces = refs[:count]
    (
        out_ref, attn_ref, token_ref, cot_ref, hot_ref, gate_ref, scale_ref, middle_out, attn_out,
        sum_out, bias_out,
    ) = refs[count:-count]
    gate = spread(hot_ref, gate_ref)
    attn = attn_ref[...]
    normed, inverse = normed_rows(token_ref[...].astype(jnp.float32) + gate * attn)
    gradient = sum_of(pieces) * (1.0 + spread(hot_ref, scale_ref))
    grad_middle = cot_ref[...].astype(jnp.float32) + norm_back_rows(gradient, normed, inverse)
    middle_out[...] = grad_middle
    grad_attn = (gate * grad_middle).astype(jnp.bfloat16)
    attn_out[...] = grad_attn
    for mask, block_out in enumerate(refs[-count:]):
        rows = peer_rows(spot_ref, mask, block_out.shape[1])
        block_out[...] = rows_dot(grad_attn, out_ref[rows, :]).astype(jnp.bfloat16)
    bias_out[...] = jnp.sum(grad_attn.astype(jnp.float32), axis=0, keepdims=True)
    sum_out[...] = jnp.zeros_like(sum_out)
    add_image_sums(sum_out, 0, hot_ref, image_count, grad_middle * attn)


def grad_middle_of(
    spot, pieces, attn, tokens, cotangent, hot, table, out_full, image_count, chunk, after
):
    rows, width = pieces[0].shape
    features = out_full.shape[0] // len(pieces)
    high = table.shape[1]
    count = len(pieces)
    base = chunk * count
    return tied_call(
        functools.partial(grad_middle_kernel, count=count, image_count=image_count),
        (spot,),
        (*pieces, out_full, attn, tokens, cotangent, hot, table, table),
        after,
        grid=(1,),
        in_specs=[held((rows, width))] * count
        + [
            held(out_full.shape),
            owned(rows, width, base),
            owned(rows, width, base),
            owned(rows, width, base),
            owned(rows, hot.shape[1], base),
            column(high, width, 2),
            column(high, width, 4),
        ],
        out_specs=[
            fixed((rows, width)),
            fixed((rows, width)),
            fixed((1, image_count, width)),
            fixed((1, width)),
        ]
        + [fixed((rows, features))] * count,
        out_shape=[
            shaped((rows, width), jnp.float32),
            shaped((rows, width)),
            shaped((1, image_count, width), jnp.float32),
            shaped((1, width), jnp.float32),
        ]
        + [shaped((rows, features))] * count,
        vmem=16,
        cost=cost(4),
    )


def layer_out_kernel(
    mlp_ref, attn_ref, token_ref, hot_ref, gate_ref, gate_two_ref, bias_ref, rows_out
):
    middle = token_ref[...].astype(jnp.float32) + spread(hot_ref, gate_ref) * attn_ref[...]
    mlp = mlp_ref[...].astype(jnp.float32) + bias_ref[...].astype(jnp.float32)
    rows_out[...] = (middle + spread(hot_ref, gate_two_ref) * mlp).astype(jnp.bfloat16)


def layer_out_of(mlp, attn, tokens, hot, table, bias, block, after):
    rows, width = tokens.shape
    high = table.shape[1]
    return tied_call(
        layer_out_kernel,
        (),
        (mlp, attn, tokens, hot, table, table, bias),
        after,
        grid=(rows // block,),
        in_specs=[
            down(block, width),
            down(block, width),
            down(block, width),
            down(block, hot.shape[1]),
            column(high, width, 2),
            column(high, width, 5),
            held(bias.shape),
        ],
        out_specs=down(block, width),
        out_shape=shaped((rows, width)),
        vmem=20,
        cost=cost(4),
    )


def owned_chunks(rows, width, count):
    return pl.BlockSpec((rows, width), lambda c, spot: (c * count + spot[0], 0))


def grad_tokens_kernel(spot_ref, *refs, count):
    pieces = refs[:count]
    token_ref, hot_ref, scale_ref, *middle_refs, rows_out = refs[count:]
    normed, inverse = normed_rows(token_ref[...].astype(jnp.float32))
    gradient = sum_of(pieces) * (1.0 + spread(hot_ref, scale_ref))
    middle = pick(pl.program_id(0), [middle_ref[...] for middle_ref in middle_refs])
    rows_out[...] = (middle + norm_back_rows(gradient, normed, inverse)).astype(jnp.bfloat16)


def grad_tokens_of(spot, pieces, tokens, hot, table, grad_middle, after):
    chunks = len(grad_middle)
    rows, width = grad_middle[0].shape
    count = len(pieces)
    return tied_call(
        functools.partial(grad_tokens_kernel, count=count),
        (spot,),
        (*pieces, tokens, hot, table, *grad_middle),
        after,
        grid=(chunks,),
        in_specs=[down(rows, width)] * count
        + [
            owned_chunks(rows, width, count),
            owned_chunks(rows, hot.shape[1], count),
            column(table.shape[1], width, 1),
        ]
        + [held((rows, width))] * chunks,
        out_specs=down(rows, width),
        out_shape=shaped((rows * chunks, width)),
        vmem=12,
        cost=cost(4),
    )


def grad_hidden_kernel(
    spot_ref, query_ref, near_ref, later_ref, before_ref, weight_ref, token_ref, hot_ref, all_out,
    sum_out, bias_out, *outs, image_count, own,
):
    clear_at_start(sum_out, bias_out)
    normed, _ = normed_rows(token_ref[...].astype(jnp.float32))
    pairs = (
        near_ref[...] + later_ref[...].astype(jnp.float32) + before_ref[...].astype(jnp.float32)
    ).astype(jnp.bfloat16)
    features = query_ref.shape[1]
    grad = jnp.concatenate([query_ref[...], pairs[:, : 2 * features]], axis=1)
    all_out[...] = grad
    bias_out[...] += jnp.sum(grad.astype(jnp.float32), axis=0, keepdims=True)
    part = rows_dot(grad, weight_ref[...])
    hand_out(spot_ref, outs, part, own)
    add_image_sums(sum_out, 0, hot_ref, image_count, part)
    add_image_sums(sum_out, 1, hot_ref, image_count, part * normed)


def grad_hidden_of(
    spot, query, near, later, before, weight, tokens, hot, image_count, block, own, count, after
):
    rows, features = query.shape
    width = tokens.shape[1]
    pair = down(block, whole_lanes(2 * features))
    return tied_call(
        functools.partial(grad_hidden_kernel, image_count=image_count, own=own),
        (spot,),
        (query, near, later, before, weight, tokens, hot),
        after,
        grid=(rows // block,),
        in_specs=[
            down(block, features),
            pair,
            pair,
            pair,
            held(weight.shape),
            down(block, width),
            down(block, hot.shape[1]),
        ],
        out_specs=[
            down(block, 3 * features),
            fixed((2, image_count, width)),
            fixed((1, 3 * features)),
        ]
        + [fixed((rows // count, width))] * count,
        out_shape=[
            shaped((rows, 3 * features)),
            shaped((2, image_count, width), jnp.float32),
            shaped((1, 3 * features), jnp.float32),
        ]
        + [shaped((rows // count, width))] * count,
        vmem=20,
        cost=cost(8),
    )


def place_kernel(spot_ref, *refs, chunks):
    out, pieces = refs[-1], refs[:-1]
    own = out.shape[0]
    for c in range(chunks):
        for mask, piece in enumerate(pieces):

            @pl.when(pl.program_id(0) == (spot_ref[0] ^ mask) + c * len(pieces))
            def _(piece=piece, c=c):
                out[...] = piece[c * own : (c + 1) * own, :].astype(out.dtype)


def place_rows(spot, pieces, chunks, kind, after):
    rows, width = pieces[0].shape
    own = rows // chunks
    return tied_call(
        functools.partial(place_kernel, chunks=chunks),
        (spot,),
        pieces,
        after,
        grid=(len(pieces) * chunks,),
        in_specs=[held((rows, width))] * len(pieces),
        out_specs=down(own, width),
        out_shape=shaped((rows * len(pieces), width), kind),
        vmem=12,
        cost=cost(3),
    )


def split_kernel(spot_ref, *refs, sizes, kept, count):
    values, place = [], 0
    for size in sizes:
        values.append(sum_of(refs[place : place + size]))
        place += size
    values = jnp.concatenate(values, axis=0)
    columns = values.shape[1] // count
    split_out, kept_out = refs[-2:]
    for mask in range(count):
        result = values[:, :columns]
        for j in range(1, count):
            result = jnp.where(
                spot_ref[0] ^ mask == j, values[:, j * columns : (j + 1) * columns], result
            )
        split_out[mask] = result
    rows = []
    for size in kept:
        value = sum_of(refs[place : place + size])
        place += size
        for j in range(value.shape[1] // columns):
            rows.append(value[:, j * columns : (j + 1) * columns])
    kept_out[...] = jnp.concatenate(rows, axis=0)


def split_columns(spot, groups, kept, count, after):
    operands = [value for group in groups + kept for value in group]
    rows = sum(group[0].shape[0] for group in groups)
    columns = operands[0].shape[1] // count
    shapes = [
        (count, rows, columns),
        (sum(group[0].shape[1] for group in kept) // columns, columns),
    ]
    return tied_call(
        functools.partial(
            split_kernel,
            sizes=[len(group) for group in groups],
            kept=[len(group) for group in kept],
            count=count,
        ),
        (spot,),
        operands,
        after,
        grid=(1,),
        in_specs=[held(value.shape) for value in operands],
        out_specs=[fixed(shape) for shape in shapes],
        out_shape=[shaped(shape, jnp.float32) for shape in shapes],
        vmem=12,
        cost=cost(1),
    )


def mlp_weights_kernel(hidden_ref, grad_ref, pre_ref, act_ref, *refs):
    own_refs, own_out, out = refs[:-2], refs[-2], refs[-1]
    units = pre_ref.shape[1]
    own = own_refs[0].shape[0]

    @pl.when(pl.program_id(0) == 0)
    def _():
        for c, own_ref in enumerate(own_refs):
            own_out[c * own : (c + 1) * own, :] = own_ref[...]

    out[:, :units] = turned_dot(hidden_ref[...], pre_ref[...]).astype(jnp.bfloat16)
    out[:, units:] = turned_dot(grad_ref[...], act_ref[...]).astype(jnp.bfloat16)


def mlp_weights(grad_mlp, hidden, pre, act, owned_rows, after):
    rows, width = grad_mlp.shape
    units = pre.shape[1]
    if units % 128:
        sides = [turned_dot(hidden, pre), turned_dot(grad_mlp, act)]
        joined = jnp.concatenate([side.astype(jnp.bfloat16) for side in sides], axis=1)
        return jnp.concatenate(owned_rows, axis=0), joined
    part = width // 3
    across = pl.BlockSpec((rows, part), lambda i, *_: (0, i))
    own = owned_rows[0].shape
    all_owned = (own[0] * len(owned_rows), width)
    return tied_call(
        mlp_weights_kernel,
        (),
        (hidden, grad_mlp, pre, act, *owned_rows),
        after,
        grid=(3,),
        in_specs=[across, across, held((rows, units)), held((rows, units))]
        + [held(own)] * len(owned_rows),
        out_specs=[
            fixed(all_owned),
            pl.BlockSpec((part, 2 * units), lambda i, *_: (i, 0)),
        ],
        out_shape=[shaped(all_owned), shaped((width, 2 * units))],
        vmem=28,
        cost=cost(7),
    )


def attn_weights_kernel(spot_ref, side_ref, hidden_ref, *refs, chunks, count, blocks):
    grad_ref, attended = refs[0], refs[1 : 1 + chunks]
    pieces, outs = refs[1 + chunks : 1 + chunks + count], refs[1 + chunks + count :]
    own = pieces[0].shape[0] // chunks
    high, low = turned_dot(hidden_ref[...], grad_ref[...]), 0.0
    for mask, piece in enumerate(pieces):
        place = pl.ds(pl.multiple_of((spot_ref[0] ^ mask) * own, own), own)
        theirs = jnp.concatenate([attended[c][place, :] for c in range(chunks)], axis=0)
        low = low + turned_dot(piece[...], theirs)
    total = jnp.concatenate([low.astype(jnp.bfloat16), high.astype(jnp.bfloat16)], axis=1)
    if not blocks:
        outs[0][...] = total
        return
    size = total.shape[0] // blocks
    for pair in range(blocks // 2):
        left = total[2 * pair * size : (2 * pair + 1) * size, :]
        right = total[(2 * pair + 1) * size : (2 * pair + 2) * size, :]
        outs[0][pair] = jnp.where(side_ref[0] == 0, left, right)
        outs[1][pair] = jnp.where(side_ref[0] == 0, right, left)


def attn_weights(spot, side, hidden, attended, grad, pieces, blocks, after):
    rows, width = hidden.shape
    chunks = len(attended)
    features = attended[0].shape[1]
    operands = (hidden, grad, *attended, *pieces)
    if blocks:
        shapes = [(blocks // 2, width // blocks, 4 * features)] * 2
    else:
        shapes = [(width, 4 * features)]
    return tied_call(
        functools.partial(
            attn_weights_kernel, chunks=chunks, count=len(pieces), blocks=blocks
        ),
        (spot, side),
        operands,
        after,
        grid=(1,),
        in_specs=[held(value.shape) for value in operands],
        out_specs=[fixed(shape) for shape in shapes],
        out_shape=[shaped(shape) for shape in shapes],
        vmem=40,
        cost=cost(7),
    )


def fold_kernel(side_ref, kept_ref, got_ref, keep_out, send_out):
    for pair in range(keep_out.shape[0]):
        left, right = [
            kept_ref[block].astype(jnp.float32) + got_ref[block].astype(jnp.float32)
            for block in (2 * pair, 2 * pair + 1)
        ]
        keep_out[pair] = jnp.where(side_ref[0] == 0, left, right).astype(keep_out.dtype)
        send_out[pair] = jnp.where(side_ref[0] == 0, right, left).astype(send_out.dtype)


def fold_blocks(side, kept, got, after):
    blocks, size, width = kept.shape
    shape = (blocks // 2, size, width)
    return tied_call(
        fold_kernel,
        (side,),
        (kept, got),
        after,
        grid=(1,),
        in_specs=[held(kept.shape)] * 2,
        out_specs=[fixed(shape)] * 2,
        out_shape=[shaped(shape)] * 2,
        vmem=12,
        cost=cost(2),
    )


def attn_total_kernel(*refs, count):
    pieces, (out_out, qkv_out) = refs[:count], refs[count:]
    total = sum_of(pieces)[0]
    features = out_out.shape[0]
    out_out[...] = total[:, :features].T
    for c in range(3):
        qkv_out[c] = total[:, (c + 1) * features : (c + 2) * features]


def attn_total_of(pieces, features, after):
    _, size, width = pieces[0].shape
    return tied_call(
        functools.partial(attn_total_kernel, count=len(pieces)),
        (),
        pieces,
        after,
        grid=(1,),
        in_specs=[held((1, size, width))] * len(pieces),
        out_specs=[fixed((features, size)), fixed((3, size, features))],
        out_shape=[
            shaped((features, size), jnp.float32),
            shaped((3, size, features), jnp.float32),
        ],
        vmem=12,
        cost=cost(1),
    )


def on_device(
    tokens,
    conditioning,
    image_index,
    qkv_weight,
    qv_bias,
    out_weight,
    out_bias,
    up_weight,
    up_bias,
    down_weight,
    down_bias,
    ada_weight,
    ada_bias,
    cotangent,
):
    row_count, width = tokens.shape
    feature_count = qkv_weight.shape[2]
    head_size = lax.axis_size("head")
    me = lax.axis_index("head")
    spot = me.astype(jnp.int32).reshape(1)
    my_index = lax.axis_index("seq")
    seq_size = lax.axis_size("seq")
    side = (my_index % 2).astype(jnp.int32).reshape(1)
    blocks = seq_size if width % (16 * seq_size) == 0 else 0
    image_count = conditioning.shape[0]
    columns = ada_weight.shape[2]
    my_images = lax.dynamic_slice_in_dim(image_index, my_index * row_count, row_count, 0)
    edge = jnp.full((row_count,), -1, jnp.int32)
    padded_images = jnp.concatenate([edge, image_index, edge + (image_count + 1)])
    wide_images = lax.dynamic_slice_in_dim(padded_images, my_index * row_count, 3 * row_count, 0)
    ranges = key_ranges(my_images, wide_images, image_count, KEY_TILE, QUERY_BLOCK)
    images = jnp.tile(jnp.arange(image_count, dtype=jnp.int32), 3)
    hot = (my_images[:, None] == images[None, :]).astype(jnp.bfloat16)

    out_full = lax.all_gather(out_weight, "head", axis=0, tiled=True)
    cond_float = conditioning.astype(jnp.float32)
    cond_act = jax.nn.silu(cond_float).astype(jnp.bfloat16)
    mod_mine = jnp.einsum("id,dkf->kif", cond_act, ada_weight, preferred_element_type=jnp.float32)
    mod_mine = mod_mine + ada_bias.astype(jnp.float32)[:, None]
    mod_pieces = gather_pieces(mod_mine, "head")
    modulation = jnp.concatenate([pick(me ^ j, mod_pieces) for j in range(head_size)], axis=2)
    table = jnp.concatenate(three_parts(modulation), axis=1)

    weight = qkv_weight.reshape(width, 3 * feature_count)
    qv_wide = qv_bias.astype(jnp.float32)
    bias = jnp.concatenate([qv_wide[0], jnp.zeros_like(qv_wide[0]), qv_wide[1]])[None]
    hidden_one, query, kv = project(tokens, hot, table, weight, bias, ROW_BLOCK, [])
    kv_before = step_along(kv, "seq", True)
    kv_after = step_along(kv, "seq", False)
    grad_mlp, grad_act, grad_down_bias, cot_sums = grad_act_of(
        cotangent, hot, table, down_weight, image_count, ROW_BLOCK, [hidden_one]
    )
    kvs = [kv_before, kv, kv_after]
    attended, attended_wide, logs, last = [], [], [], [grad_down_bias]
    for c in range(CHUNKS):
        got = attend(ranges, query, kvs, KEY_TILE, QUERY_BLOCK, c, CHUNKS, last)
        for values, kept in zip((attended, attended_wide, logs), got):
            values.append(kept)
        last = [got[2]]
    attended_wide = jnp.concatenate(attended_wide, axis=1)
    logs = jnp.concatenate(logs, axis=1)

    late_sums, up_sums, hidden_pieces, into, last = [], [], [], [], [logs]
    for c in range(CHUNKS):
        got = middle_of(
            spot, gather_pieces(attended[c], "head"), tokens, hot, table, out_full, out_bias[None],
            up_weight, up_bias[None], grad_act, image_count, ROW_BLOCK, c, into, last,
        )
        into = got[:4]
        late_sums.append(got[4].reshape(2 * image_count, width))
        up_sums.append(got[5])
        hidden_pieces.append(swap_pieces(got[6:], "head"))
        last = []
    attn, hidden_two, act, grad_pre = into
    mlp_part, mlp_sums = mlp_of(
        act, down_weight, cotangent, hot, image_count, ROW_BLOCK, hidden_pieces[0]
    )
    mlp = lax.psum(mlp_part, "head")

    grad_middle, grad_attn, grad_attended, gate_sums, out_sums = [], [], [], [], []
    last = [mlp_sums]
    for c in range(CHUNKS):
        got = grad_middle_of(
            spot, hidden_pieces[c], attn, tokens, cotangent, hot, table, out_full, image_count, c,
            last,
        )
        grad_middle.append(got[0])
        grad_attn.append(got[1])
        gate_sums.append(got[2][0])
        out_sums.append(got[3])
        grad_attended.append(swap_pieces(got[4:], "head"))
        last = [got[3]]
    grad_own, weight_part = mlp_weights(
        grad_mlp, hidden_two, grad_pre, act, grad_attn, last + grad_attended[0]
    )

    query_started, grad_rows, to_before, to_after = attend_far(
        spot, ranges, logs, query, grad_attended, attended_wide, kv_before, kv_after,
        KEY_TILE, QUERY_BLOCK, [grad_own],
    )
    grad_attn = gather_pieces(grad_own, "head")
    from_after = step_along(to_before, "seq", False)
    from_before = step_along(to_after, "seq", True)
    grad_query, kv_near = attend_near(
        ranges, logs, query, grad_rows, attended_wide, kv, query_started, KEY_TILE, QUERY_BLOCK,
        [],
    )

    grad_all, first_sums, qkv_sums, *one_pieces = grad_hidden_of(
        spot, grad_query, kv_near, from_after, from_before, weight, tokens, hot, image_count,
        ROW_BLOCK, row_count // CHUNKS // head_size, head_size, grad_attn,
    )
    one_pieces = swap_pieces(one_pieces, "head")
    attn_part = attn_weights(
        spot, side, hidden_one, attended, grad_all, grad_attn, blocks, []
    )
    layer_out = layer_out_of(
        mlp, attn, tokens, hot, table, down_bias[None], ROW_BLOCK, [attn_part[0]]
    )
    own_tokens = grad_tokens_of(
        spot, one_pieces, tokens, hot, table, grad_middle, [layer_out]
    )
    sum_stack, kept_rows = split_columns(
        spot,
        [[first_sums.reshape(2 * image_count, width)], gate_sums, late_sums, [mlp_sums[0]]]
        + [out_sums],
        [[qkv_sums], up_sums, [grad_down_bias]],
        head_size,
        [own_tokens],
    )
    token_pieces = gather_pieces(own_tokens, "head")
    if blocks:
        kept, sent = attn_part
        mask = 1
        while mask < blocks // 2:
            mask *= 2
            kept, sent = fold_blocks(
                ((my_index // mask) % 2).astype(jnp.int32).reshape(1),
                kept,
                swap(sent, "seq", mask // 2),
                [kept_rows],
            )
        attn_got = [kept, swap(sent, "seq", mask)]
    own_down = lax.dynamic_slice_in_dim(down_bias, me * columns, columns, 0).astype(jnp.float32)
    own_cot = lax.dynamic_slice_in_dim(cot_sums, me * columns, columns, 1) * own_down[None]
    mods = 6 * image_count
    sums = fold_pieces(sum_stack, "head")
    sums = sums + jnp.pad(own_cot, ((5 * image_count, 1), (0, 0)))
    sums = butterfly_sum(jnp.concatenate([sums, kept_rows], axis=0), "seq")
    grad_mod = sums[:mods].reshape(6, image_count, columns)
    out_sum = sums[mods : mods + 1]
    grad_qv_bias = sums[mods + 1 : mods + 4 : 2]
    low_bias = sums[mods + 4 :].reshape(-1)
    units = up_weight.shape[1]
    grad_up_bias, grad_down_bias = low_bias[:units], low_bias[units:]
    mod_parts = jnp.concatenate(three_parts(grad_mod), axis=1)
    grad_cond_act = jnp.einsum(
        "kif,dkf->id", mod_parts, ada_weight, preferred_element_type=jnp.float32
    )
    grad_cond_act = jnp.sum(grad_cond_act.reshape(3, image_count, width), axis=0)
    spread_bias = jnp.concatenate(
        [jnp.where(me == j, out_sum, 0.0) for j in range(head_size)], axis=1
    )
    final = butterfly_sum(jnp.concatenate([grad_cond_act, spread_bias], axis=0), "head")
    _, silu_pull = jax.vjp(jax.nn.silu, cond_float)
    grad_conditioning = silu_pull(final[:image_count])[0]
    grad_out_bias = final[image_count]
    grad_ada_bias = jnp.sum(grad_mod, axis=1)
    grad_ada_weight = jnp.einsum(
        "id,kif->dkf",
        jnp.concatenate([cond_act] * 3, axis=0),
        mod_parts,
        preferred_element_type=jnp.float32,
    )

    grad_tokens = place_rows(spot, token_pieces, CHUNKS, jnp.float32, [])
    mlp_total = lax.psum_scatter(weight_part, "seq", scatter_dimension=0, tiled=True)
    mlp_total = mlp_total.astype(jnp.float32)
    if blocks:
        grad_out_weight, grad_qkv = attn_total_of(attn_got, feature_count, [])
        grad_qkv_weight = grad_qkv.transpose(1, 0, 2)
    else:
        attn_total = lax.psum_scatter(attn_part[0], "seq", scatter_dimension=0, tiled=True)
        attn_total = attn_total.astype(jnp.float32)
        grad_out_weight = attn_total[:, :feature_count].T
        grad_qkv_weight = attn_total[:, feature_count:].reshape(-1, 3, feature_count)
    return (
        layer_out,
        grad_tokens,
        grad_conditioning,
        grad_qkv_weight,
        grad_qv_bias,
        grad_out_weight,
        grad_out_bias,
        mlp_total[:, :units],
        grad_up_bias,
        mlp_total[:, units:].T,
        grad_down_bias,
        grad_ada_weight,
        grad_ada_bias,
    )


def solution(mesh):
    placed = (
        P("seq", None),
        P(),
        P(),
        P(None, None, "head"),
        P(None, "head"),
        P("head", None),
        P(),
        P(None, "head"),
        P("head"),
        P("head", None),
        P(),
        P(None, None, "head"),
        P(None, "head"),
        P("seq", None),
    )
    return jax.shard_map(
        on_device,
        mesh=mesh,
        in_specs=placed,
        out_specs=(
            P("seq", None),
            P("seq", None),
            P(),
            P("seq", None, "head"),
            P(None, "head"),
            P("head", "seq"),
            P(),
            P("seq", "head"),
            P("head"),
            P("head", "seq"),
            P(),
            P(None, None, "head"),
            P(None, "head"),
        ),
        check_vma=False,
    )
```

time: 1100 us -> 377 us (0.34)
  waiting for transfers between devices: 639 us -> 60.6 us
  matrix products: 243 us -> 8.82 us
  Pallas kernels: 0 us -> 125 us
  blocking collectives: 75.2 us -> 0 us
  other arithmetic: 80.6 us -> 6.11 us
  local copies, waits for them, and re-layouts: 16.2 us -> 80.9 us
  starting transfers between devices: 20.1 us -> 73.3 us
    psum x5 -> x1, waiting for transfers between devices: 458 us -> 15.9 us  [on_device(): mlp = lax.psum(mlp_part, 'head')]
    dot_general x33 -> x3, matrix products: 243 us -> 8.82 us  [the longest x1 4.5 us: on_device(): jnp.einsum('id,kif->dkf', jnp.concatenate([cond_act] * 3, axis=0), mod_pa...]
    reduce_scatter x4 -> x1, waiting for transfers between devices: 180 us -> 0.01 us  [on_device(): lax.psum_scatter(weight_part, 'seq', scatter_dimension=0, tiled=True)]
    pallas_call x0 -> x21, Pallas kernels: none -> 125 us  [tied_call(): pl.pallas_call(body, grid_spec=pltpu.PrefetchScalarGridSpec(num_scalar_pr...]
    ppermute x4 -> x44, starting transfers between devices: 9.81 us -> 72.7 us  [the longest x40 62.5 us: swap(): return lax.ppermute(value, axis, [(i, i ^ mask) for i in range(count)])]
    unnamed x144 -> x233, local copies, waits for them, and re-layouts: 8.39 us -> 70.4 us
    reduce_sum x10 -> x4, other arithmetic: 49.8 us -> 0.93 us  [the longest x1 0.66 us: on_device(): grad_ada_bias = jnp.sum(grad_mod, axis=1)]
    all_gather x1 -> x0, blocking collectives: 45.7 us -> none  [on_device(): modulation = lax.all_gather(mod_mine, 'head', axis=2, tiled=True)]
  transfers between devices with their start and end apart: 13 -> 47, of which waited for: 7 -> 16; matrix products, arithmetic and copies ran while one was open for 8% -> 5% of each run, Pallas kernels for 0% -> 32%
where the time goes in v3:
time: 377 us; the launch traced here: 370 us
  Pallas kernels  125 us (33%)
  local copies, waits for them, and re-layouts  80.9 us (21%)
  starting transfers between devices  73.3 us (19%)
  waiting for transfers between devices  60.6 us (16%)
  between operations  15.2 us (4%)
  matrix products  8.82 us (2%)
  other arithmetic  6.11 us (2%)
    pallas_call x21, Pallas kernels, tied_call(): pl.pallas_call(body, grid_spec=pltpu.PrefetchScalarGridSpec(num_scalar_pr...  125 us
    unnamed x233, local copies, waits for them, and re-layouts  70.4 us
    ppermute x40, starting transfers between devices, swap(): return lax.ppermute(value, axis, [(i, i ^ mask) for i in range(count)])  62.5 us
    ppermute x40, waiting for transfers between devices, swap(): return lax.ppermute(value, axis, [(i, i ^ mask) for i in range(count)])  44.6 us
    psum x1, waiting for transfers between devices, on_device(): mlp = lax.psum(mlp_part, 'head')  15.9 us
    ppermute x4, starting transfers between devices, step_along(): return lax.ppermute(value, axis, pairs)  10.2 us
  transfers between devices with their start and end apart: 47, of which 16 were waited for; matrix products, arithmetic and copies ran while one was open for 5% of the time, Pallas kernels for 32%

profile of v3, /device:TPU:0, one launch (start us, length us, event | category | flops | bytes accessed | tf_op | source)
XLA Modules:
  0.0 370.2 jit_solution(16405320669594825352)
XLA Ops:
  25.0 6.0 %shard_map.237 = (bf16[1024,1152]{1,0:T(8,128)(2,1)S(1)}, bf16[1024,288]{1,0:T(8,128)(2,1)S(1)}, bf16[1024,640]{1,0:T(8,128)(2,1)}) custom-call(bf16[1024,1152]{1,0:T(8,128)(2,1)S(1)} %copy-done.14, bf16[1024,48]{1,0:T(8,128)(2,1)S(1)} %compare_convert_fusion.refs_1_.refs_2_.refs_8_.refs_11_.refs_7_.refs_10_.refs_4_, ...), custom_call_target="tpu_custom_call" | custom-call | flops 6899999744 | bytes 1 | tf_op jit(solution)/shard_map/pallas_call | solution.py:90
  34.6 4.3 %collective-permute-start.3 = (bf16[1024,640]{1,0:T(8,128)(2,1)}, bf16[1024,640]{1,0:T(8,128)(2,1)}, u32[]{:S(2)}, u32[]{:S(2)}) collective-permute-start(bf16[1024,640]{1,0:T(8,128)(2,1)} %get-tuple-element.92.refs_7_), channel_id=1, source_target_pairs={{0,4},{4,8},{8,12},{12,16},{16,20},{20,24},{24,28},{1,5},{5,9},{9,... | collective-permute-start | bytes 3932168 | tf_op jit(solution)/shard_map/ppermute | solution.py:63
  44.6 5.1 %shard_map.238 = (bf16[1024,1152]{1,0:T(8,128)(2,1)S(1)}, f32[1024,1152]{1,0:T(8,128)S(1)}, f32[1,1152]{1,0:T(1,128)S(1)}, f32[16,1152]{1,0:T(8,128)S(1)}) custom-call(bf16[1024,1152]{1,0:T(8,128)(2,1)S(1)} %copy-done.83, bf16[1024,1152]{1,0:T(8,128)(2,1)S(1)} %copy-done.11, ...), custom_call_target="tpu_custom_call" | custom-call | flops 5750000128 | bytes 1 | tf_op jit(solution)/shard_map/pallas_call | solution.py:90
  51.8 10.3 %shard_map.239 = (bf16[512,288]{1,0:T(8,128)(2,1)S(1)}, f32[288,512]{1,0:T(8,128)S(1)}, f32[4,512]{1,0:T(4,128)S(1)}) custom-call(s32[4]{0:T(128)S(1)} %get-tuple-element.230.refs_0_, s32[4]{0:T(128)S(1)} %get-tuple-element.229.refs_1_, f32[1,1152]{1,0:T(1,128)S(1)} %get-tuple-element.90.refs_2_.refs_13_, s32[1,1024]{1,0:T(1,128)S(1)} %bitcast.38, ...), custom_call_target="tpu_custom_call" | custom-call | flops 11500000256 | bytes 1 | tf_op jit(solution)/shard_map/pallas_call | solution.py:90
  65.8 12.4 %shard_map.240 = (bf16[512,288]{1,0:T(8,128)(2,1)}, f32[288,512]{1,0:T(8,128)S(1)}, f32[4,512]{1,0:T(4,128)S(1)}) custom-call(s32[4]{0:T(128)S(1)} %get-tuple-element.230.refs_0_, s32[4]{0:T(128)S(1)} %get-tuple-element.229.refs_1_, f32[4,512]{1,0:T(4,128)S(1)} %get-tuple-element.93.refs_2_, s32[1,1024]{1,0:T(1,128)S(1)} %bitcast.39, ...), custom_call_target="tpu_custom_call" | custom-call | flops 11500000256 | bytes 1 | tf_op jit(solution)/shard_map/pallas_call | solution.py:90
  95.2 12.0 %shard_map.241 = (f32[1024,1152]{1,0:T(8,128)}, bf16[1024,1152]{1,0:T(8,128)(2,1)S(1)}, bf16[1024,1152]{1,0:T(8,128)(2,1)S(1)}, bf16[1024,1152]{1,0:T(8,128)(2,1...) custom-call(s32[1]{0:T(128)} %bitcast.refs_0_.refs_2_, ...), custom_call_target="tpu_custom_call" | custom-call | flops 13799999488 | bytes 1 | tf_op jit(solution)/shard_map/pallas_call | solution.py:90
  120.6 12.3 %shard_map.242 = (f32[1024,1152]{1,0:T(8,128)}, bf16[1024,1152]{1,0:T(8,128)(2,1)S(1)}, bf16[1024,1152]{1,0:T(8,128)(2,1)S(1)}, bf16[1024,1152]{1,0:T(8,128)(2,1...) custom-call(s32[1]{0:T(128)} %bitcast.refs_0_.refs_2_, ...), custom_call_target="tpu_custom_call", output_to_operand_aliasing={{0}: (1, {}), {1}: (2, {}), {2}: (3, {}), {3}: (4, {})} | custom-call | flops 13799999488 | bytes 1 | tf_op jit(solution)/shard_map/pallas_call | solution.py:90
  133.1 5.7 %shard_map.243 = (bf16[1024,1152]{1,0:T(8,128)(2,1)}, f32[1,16,1152]{2,1,0:T(8,128)S(1)}) custom-call(bf16[128,1152]{1,0:T(8,128)(2,1)S(1)} %get-tuple-element.97.refs_0_.refs_2_, bf16[128,1152]{1,0:T(8,128)(2,1)S(1)} %collective-permute-done.8.refs_1_.refs_3_, bf16[128,1152]{1,0:T(8,128)(2,1)S(1)} %collective-permute-done.9.refs_2_.refs_4_, ...), custom_call_target="tpu_custom_call" | custom-call | flops 6899999744 | bytes 1 | tf_op jit(solution)/shard_map/pallas_call | solution.py:90
  170.9 7.3 %shard_map.246 = (bf16[256,1152]{1,0:T(8,128)(2,1)S(1)}, bf16[1152,2304]{1,0:T(8,128)(2,1)S(1)}) custom-call(f32[1,1152]{1,0:T(1,128)S(1)} %get-tuple-element.114.refs_0_.refs_9_, bf16[128,288]{1,0:T(8,128)(2,1)S(1)} %get-tuple-element.115.refs_1_.refs_11_, bf16[128,288]{1,0:T(8,128)(2,1)S(1)} %collective-permute-done.17.refs_2_.refs_12_, ...), custom_call_target="tpu_custom_call" | custom-call | flops 8049999872 | bytes 1 | tf_op jit(solution)/shard_map/pallas_call | solution.py:90
  193.6 6.4 %shard_map.247 = (f32[288,1024]{1,0:T(8,128)S(1)}, bf16[1024,288]{1,0:T(8,128)(2,1)S(1)}, bf16[1024,640]{1,0:T(8,128)(2,1)S(1)}, bf16[1024,640]{1,0:T(8,128)(2,1)S(1)}) custom-call(s32[4]{0:T(128)S(1)} %get-tuple-element.230.refs_0_, s32[4]{0:T(128)S(1)} %get-tuple-element.229.refs_1_, s32[1]{0:T(128)} %bitcast.refs_0_.refs_2_, ...), custom_call_target="tpu_custom_call" | custom-call | flops 9200000000 | bytes 1 | tf_op jit(solution)/shard_map/pallas_call | solution.py:90
  204.6 17.8 %shard_map.248 = (bf16[1024,288]{1,0:T(8,128)(2,1)S(1)}, f32[1024,640]{1,0:T(8,128)S(1)}) custom-call(s32[4]{0:T(128)S(1)} %get-tuple-element.230.refs_0_, s32[4]{0:T(128)S(1)} %get-tuple-element.229.refs_1_, s32[1,1024]{1,0:T(1,128)S(1)} %bitcast.41, s32[1,1024]{1,0:T(1,128)S(1)} %bitcast.37, ...), custom_call_target="tpu_custom_call" | custom-call | flops 18400000000 | bytes 1 | tf_op jit(solution)/shard_map/pallas_call | solution.py:90
  222.4 7.8 %shard_map.249 = (bf16[1024,864]{1,0:T(8,128)(2,1)S(1)}, f32[2,16,1152]{2,1,0:T(8,128)S(1)}, f32[1,864]{1,0:T(1,128)S(1)}, bf16[256,1152]{1,0:T(8,128)(2,1)S(1)}...) custom-call(s32[1]{0:T(128)} %bitcast.refs_0_.refs_2_, ...), custom_call_target="tpu_custom_call" | custom-call | flops 9200000000 | bytes 1 | tf_op jit(solution)/shard_map/pallas_call | solution.py:90
  234.7 4.9 %shard_map.250 = (bf16[4,144,1152]{2,1,0:T(8,128)(2,1)S(1)}, bf16[4,144,1152]{2,1,0:T(8,128)(2,1)S(1)}) custom-call(s32[1]{0:T(128)} %bitcast.refs_0_.refs_2_, s32[1]{0:T(128)} %bitcast.1.refs_1_, bf16[1024,1152]{1,0:T(8,128)(2,1)S(1)} %copy-done.84, bf16[1024,864]{1,0:T(8,128)(2,1)S(1)} %get-tuple-element.137.refs_3_, bf16[512,288]{1,0:T(8,128)(2,1)S(1)} %copy-done.28, ...), custom_call_target="tpu_custom_call" | custom-call | flops 8049999872 | bytes 1 | tf_op jit(solution)/shard_map/pallas_call | solution.py:90
  240.7 15.9 %all-reduce.3.cloned.1.call-done.refs_1_ = bf16[1024,1152]{1,0:T(8,128)(2,1)} async-done(((bf16[1024,1152]{1,0:T(8,128)(2,1)}), bf16[1024,1152]{1,0:T(8,128)(2,1)}) %all-reduce.3.cloned.1.call-update) | async-done | bytes 2359312 | tf_op jit(solution)/shard_map/psum | solution.py:1212
  277.3 4.3 %collective-permute-start.41 = (bf16[4,144,1152]{2,1,0:T(8,128)(2,1)S(1)}, bf16[4,144,1152]{2,1,0:T(8,128)(2,1)S(1)}, u32[]{:S(2)}, u32[]{:S(2)}) collective-permute-start(bf16[4,144,1152]{2,1,0:T(8,128)(2,1)S(1)} %get-tuple-element.157), channel_id=1, source_target_pairs={{0,4},{4,0},{8,12},{12,8},{16,20},{20,16},{24,28},{28,24},{1,5},{5... | collective-permute-start | bytes 3981320 | tf_op jit(solution)/shard_map/ppermute | solution.py:33
  285.8 5.2 %collective-permute-done.35 = f32[1,97,288]{2,1,0:T(8,128)S(1)} collective-permute-done((f32[1,97,288]{2,1,0:T(8,128)S(1)}, f32[1,97,288]{2,1,0:T(8,128)S(1)}, u32[]{:S(2)}, u32[]{:S(2)}) %collective-permute-start.35) | collective-permute-done | bytes 111776 | tf_op jit(solution)/shard_map/ppermute | solution.py:33
  295.0 4.6 %collective-permute-start.37 = (f32[108,288]{1,0:T(8,128)S(1)}, f32[108,288]{1,0:T(8,128)S(1)}, u32[]{:S(2)}, u32[]{:S(2)}) collective-permute-start(f32[108,288]{1,0:T(8,128)S(1)} %fusion.28), channel_id=1, source_target_pairs={{0,8},{4,12},{8,0},{12,4},{16,24},{20,28},{24,16},{28,20},{1,9},{5... | collective-permute-start | bytes 373256 | tf_op jit(solution)/shard_map/ppermute | solution.py:33
  303.1 7.5 %collective-permute-done.37 = f32[108,288]{1,0:T(8,128)S(1)} collective-permute-done((f32[108,288]{1,0:T(8,128)S(1)}, f32[108,288]{1,0:T(8,128)S(1)}, u32[]{:S(2)}, u32[]{:S(2)}) %collective-permute-start.37) | collective-permute-done | bytes 124448 | tf_op jit(solution)/shard_map/ppermute | solution.py:33
  310.6 5.4 %collective-permute-start.38 = (f32[108,288]{1,0:T(8,128)S(1)}, f32[108,288]{1,0:T(8,128)S(1)}, u32[]{:S(2)}, u32[]{:S(2)}) collective-permute-start(f32[108,288]{1,0:T(8,128)S(1)} %add.95), channel_id=1, source_target_pairs={{0,16},{4,20},{8,24},{12,28},{16,0},{20,4},{24,8},{28,12},{1,17},{... | collective-permute-start | bytes 373256 | tf_op jit(solution)/shard_map/ppermute | solution.py:33
  320.3 5.2 %collective-permute-done.38 = f32[108,288]{1,0:T(8,128)S(1)} collective-permute-done((f32[108,288]{1,0:T(8,128)S(1)}, f32[108,288]{1,0:T(8,128)S(1)}, u32[]{:S(2)}, u32[]{:S(2)}) %collective-permute-start.38) | collective-permute-done | bytes 124448 | tf_op jit(solution)/shard_map/ppermute | solution.py:33
  328.2 5.4 %shard_map.253 = f32[1024,1152]{1,0:T(8,128)} custom-call(s32[1]{0:T(128)} %bitcast.refs_0_.refs_2_, bf16[256,1152]{1,0:T(8,128)(2,1)S(1)} %copy-done.21, bf16[256,1152]{1,0:T(8,128)(2,1)} %collective-permute-done.31.refs_2_, bf16[256,1152]{1,0:T(8,128)(2,1)} %collective-permute-done.32.refs_3_, bf16[256,1152]{1,0:T(8,128)(2,1)} %collective-permute-done.33.refs_4_), custom_call_target="tpu_custom_call" | custom-call | flops 3449999872 | bytes 1 | tf_op jit(solution)/shard_map/pallas_call | solution.py:90
  339.4 6.2 %collective-permute-start.43 = (bf16[1,144,1152]{2,1,0:T(8,128)(2,1)S(1)}, bf16[1,144,1152]{2,1,0:T(8,128)(2,1)S(1)}, u32[]{:S(2)}, u32[]{:S(2)}) collective-permute-start(bf16[1,144,1152]{2,1,0:T(8,128)(2,1)S(1)} %get-tuple-element.161), channel_id=1, source_target_pairs={{0,16},{4,20},{8,24},{12,28},{16,0},{20,4},{24,8},{28,12},{1,17},{... | collective-permute-start | bytes 995336 | tf_op jit(solution)/shard_map/ppermute | solution.py:33
  346.2 4.5 %fusion.5 = f32[1152,6,288]{0,2,1:T(8,128)} fusion(bf16[16,1152]{1,0:T(8,128)(2,1)S(1)} %get-tuple-element.227, bf16[6,16,288]{2,1,0:T(8,128)(2,1)S(1)} %get-tuple-element.224, bf16[6,16,288]{2,1,0:T(8,128)(2,1)S(1)} %get-tuple-element.225, bf16[6,16,288]{2,1,0:T(8,128)(2,1)S(1)} %get-tuple-element.226), kind=kOutput, calls=%fused_computation.31 | convolution fusion | flops 191932416 | bytes 8165376 | tf_op jit(solution)/shard_map/id,kif->dkf/dot_general | solution.py:1303
  350.7 7.7 %collective-permute-done.43.refs_1_ = bf16[1,144,1152]{2,1,0:T(8,128)(2,1)S(1)} collective-permute-done((bf16[1,144,1152]{2,1,0:T(8,128)(2,1)S(1)}, bf16[1,144,1152]{2,1,0:T(8,128)(2,1)S(1)}, u32[]{:S(2)}, u32[]{:S(2)}) %collective-permute-start.43) | collective-permute-done | bytes 331808 | tf_op jit(solution)/shard_map/ppermute | solution.py:33
  (386 shorter events, 170.9 us)
Async XLA Ops:
  7.2 77.9 %all-gather.2.cloned.1.call-start = ((), (), s32[]{:S(2)}) async-start(), calls=%async_computation.1 | async-start | bytes 3317760 | tf_op jit(solution)/shard_map/all_gather | solution.py:1169
  16.0 240.7 %all-reduce.3.cloned.1.call-start = ((), (), s32[]{:S(2)}) async-start(), calls=%async_computation.2 | async-start | bytes 4718592 | tf_op jit(solution)/shard_map/psum | solution.py:1212
  63.7 19.9 %collective-permute-start.6 = (bf16[512,288]{1,0:T(8,128)(2,1)S(1)}, bf16[512,288]{1,0:T(8,128)(2,1)S(1)}, u32[]{:S(2)}, u32[]{:S(2)}) collective-permute-start(bf16[512,288]{1,0:T(8,128)(2,1)S(1)} %get-tuple-element.95.refs_2_.refs_4_), channel_id=1, source_target_pairs={{0,2},{1,3},{2,0},{3,1},{4,6},{5,7},{6,4},{7,5},{8,10},{9,11},{10,... | collective-permute-start | bytes 884744 | tf_op jit(solution)/shard_map/ppermute | solution.py:33
  79.0 35.1 %collective-permute-start.13 = (bf16[512,288]{1,0:T(8,128)(2,1)}, bf16[512,288]{1,0:T(8,128)(2,1)}, u32[]{:S(2)}, u32[]{:S(2)}) collective-permute-start(bf16[512,288]{1,0:T(8,128)(2,1)} %get-tuple-element.105.refs_5_), channel_id=1, source_target_pairs={{0,3},{1,2},{2,1},{3,0},{4,7},{5,6},{6,5},{7,4},{8,11},{9,10},{10,... | collective-permute-start | bytes 884744 | tf_op jit(solution)/shard_map/ppermute | solution.py:33
  80.5 35.1 %collective-permute-start.12 = (bf16[512,288]{1,0:T(8,128)(2,1)}, bf16[512,288]{1,0:T(8,128)(2,1)}, u32[]{:S(2)}, u32[]{:S(2)}) collective-permute-start(bf16[512,288]{1,0:T(8,128)(2,1)} %get-tuple-element.105.refs_5_), channel_id=1, source_target_pairs={{0,2},{1,3},{2,0},{3,1},{4,6},{5,7},{6,4},{7,5},{8,10},{9,11},{10,... | collective-permute-start | bytes 884744 | tf_op jit(solution)/shard_map/ppermute | solution.py:33
  82.7 32.9 %collective-permute-start.11 = (bf16[512,288]{1,0:T(8,128)(2,1)}, bf16[512,288]{1,0:T(8,128)(2,1)}, u32[]{:S(2)}, u32[]{:S(2)}) collective-permute-start(bf16[512,288]{1,0:T(8,128)(2,1)} %get-tuple-element.105.refs_5_), channel_id=1, source_target_pairs={{0,1},{1,0},{2,3},{3,2},{4,5},{5,4},{6,7},{7,6},{8,9},{9,8},{10,11... | collective-permute-start | bytes 884744 | tf_op jit(solution)/shard_map/ppermute | solution.py:33
  112.1 20.9 %collective-permute-start.8 = (bf16[128,1152]{1,0:T(8,128)(2,1)S(1)}, bf16[128,1152]{1,0:T(8,128)(2,1)S(1)}, u32[]{:S(2)}, u32[]{:S(2)}) collective-permute-start(bf16[128,1152]{1,0:T(8,128)(2,1)S(1)} %get-tuple-element.98), channel_id=1, source_target_pairs={{0,1},{1,0},{2,3},{3,2},{4,5},{5,4},{6,7},{7,6},{8,9},{9,8},{10,11... | collective-permute-start | bytes 884744 | tf_op jit(solution)/shard_map/ppermute | solution.py:33
  138.9 221.6 %reduce-scatter.2.cloned.1.call-start = ((), (), s32[]{:S(2)}) async-start(), calls=%async_computation.3 | async-start | bytes 5971968 | tf_op jit(solution)/shard_map/reduce_scatter | solution.py:1311
  139.4 21.2 %collective-permute-start.14 = (bf16[128,1152]{1,0:T(8,128)(2,1)}, bf16[128,1152]{1,0:T(8,128)(2,1)S(1)}, u32[]{:S(2)}, u32[]{:S(2)}) collective-permute-start(bf16[128,1152]{1,0:T(8,128)(2,1)} %copy-done.41), channel_id=1, source_target_pairs={{0,1},{1,0},{2,3},{3,2},{4,5},{5,4},{6,7},{7,6},{8,9},{9,8},{10,11... | collective-permute-start | bytes 884744 | tf_op jit(solution)/shard_map/ppermute | solution.py:33
  140.9 21.2 %collective-permute-start.15 = (bf16[128,1152]{1,0:T(8,128)(2,1)}, bf16[128,1152]{1,0:T(8,128)(2,1)S(1)}, u32[]{:S(2)}, u32[]{:S(2)}) collective-permute-start(bf16[128,1152]{1,0:T(8,128)(2,1)} %copy-done.38), channel_id=1, source_target_pairs={{0,2},{1,3},{2,0},{3,1},{4,6},{5,7},{6,4},{7,5},{8,10},{9,11},{10,... | collective-permute-start | bytes 884744 | tf_op jit(solution)/shard_map/ppermute | solution.py:33
  141.4 20.7 %collective-permute-start.16 = (bf16[128,1152]{1,0:T(8,128)(2,1)}, bf16[128,1152]{1,0:T(8,128)(2,1)S(1)}, u32[]{:S(2)}, u32[]{:S(2)}) collective-permute-start(bf16[128,1152]{1,0:T(8,128)(2,1)} %copy-done.35), channel_id=1, source_target_pairs={{0,3},{1,2},{2,1},{3,0},{4,7},{5,6},{6,5},{7,4},{8,11},{9,10},{10,... | collective-permute-start | bytes 884744 | tf_op jit(solution)/shard_map/ppermute | solution.py:33
  186.8 35.5 %collective-permute-start.22 = (bf16[256,1152]{1,0:T(8,128)(2,1)S(1)}, bf16[256,1152]{1,0:T(8,128)(2,1)S(1)}, u32[]{:S(2)}, u32[]{:S(2)}) collective-permute-start(bf16[256,1152]{1,0:T(8,128)(2,1)S(1)} %copy-done.23), channel_id=1, source_target_pairs={{0,3},{1,2},{2,1},{3,0},{4,7},{5,6},{6,5},{7,4},{8,11},{9,10},{10,... | collective-permute-start | bytes 1769480 | tf_op jit(solution)/shard_map/ppermute | solution.py:33
  188.2 34.1 %collective-permute-start.21 = (bf16[256,1152]{1,0:T(8,128)(2,1)S(1)}, bf16[256,1152]{1,0:T(8,128)(2,1)S(1)}, u32[]{:S(2)}, u32[]{:S(2)}) collective-permute-start(bf16[256,1152]{1,0:T(8,128)(2,1)S(1)} %copy-done.23), channel_id=1, source_target_pairs={{0,2},{1,3},{2,0},{3,1},{4,6},{5,7},{6,4},{7,5},{8,10},{9,11},{10,... | collective-permute-start | bytes 1769480 | tf_op jit(solution)/shard_map/ppermute | solution.py:33
  190.0 32.3 %collective-permute-start.20 = (bf16[256,1152]{1,0:T(8,128)(2,1)S(1)}, bf16[256,1152]{1,0:T(8,128)(2,1)S(1)}, u32[]{:S(2)}, u32[]{:S(2)}) collective-permute-start(bf16[256,1152]{1,0:T(8,128)(2,1)S(1)} %copy-done.23), channel_id=1, source_target_pairs={{0,1},{1,0},{2,3},{3,2},{4,5},{5,4},{6,7},{7,6},{8,9},{9,8},{10,11... | collective-permute-start | bytes 1769480 | tf_op jit(solution)/shard_map/ppermute | solution.py:33
  199.9 22.4 %collective-permute-start.26 = (bf16[1024,640]{1,0:T(8,128)(2,1)S(1)}, bf16[1024,640]{1,0:T(8,128)(2,1)S(1)}, u32[]{:S(2)}, u32[]{:S(2)}) collective-permute-start(bf16[1024,640]{1,0:T(8,128)(2,1)S(1)} %get-tuple-element.135), channel_id=1, source_target_pairs={{4,0},{8,4},{12,8},{16,12},{20,16},{24,20},{28,24},{5,1},{9,5},{13... | collective-permute-start | bytes 3932168 | tf_op jit(solution)/shard_map/ppermute | solution.py:63
  201.2 21.1 %collective-permute-start.27 = (bf16[1024,640]{1,0:T(8,128)(2,1)S(1)}, bf16[1024,640]{1,0:T(8,128)(2,1)S(1)}, u32[]{:S(2)}, u32[]{:S(2)}) collective-permute-start(bf16[1024,640]{1,0:T(8,128)(2,1)S(1)} %get-tuple-element.136), channel_id=1, source_target_pairs={{0,4},{4,8},{8,12},{12,16},{16,20},{20,24},{24,28},{1,5},{5,9},{9,... | collective-permute-start | bytes 3932168 | tf_op jit(solution)/shard_map/ppermute | solution.py:63
  231.1 35.9 %collective-permute-start.28 = (bf16[256,1152]{1,0:T(8,128)(2,1)}, bf16[256,1152]{1,0:T(8,128)(2,1)S(1)}, u32[]{:S(2)}, u32[]{:S(2)}) collective-permute-start(bf16[256,1152]{1,0:T(8,128)(2,1)} %get-tuple-element.141), channel_id=1, source_target_pairs={{0,1},{1,0},{2,3},{3,2},{4,5},{5,4},{6,7},{7,6},{8,9},{9,8},{10,11... | collective-permute-start | bytes 1769480 | tf_op jit(solution)/shard_map/ppermute | solution.py:33
  233.1 34.7 %collective-permute-start.29 = (bf16[256,1152]{1,0:T(8,128)(2,1)}, bf16[256,1152]{1,0:T(8,128)(2,1)}, u32[]{:S(2)}, u32[]{:S(2)}) collective-permute-start(bf16[256,1152]{1,0:T(8,128)(2,1)} %get-tuple-element.142), channel_id=1, source_target_pairs={{0,2},{1,3},{2,0},{3,1},{4,6},{5,7},{6,4},{7,5},{8,10},{9,11},{10,... | collective-permute-start | bytes 1769480 | tf_op jit(solution)/shard_map/ppermute | solution.py:33
  233.7 36.6 %collective-permute-start.30 = (bf16[256,1152]{1,0:T(8,128)(2,1)}, bf16[256,1152]{1,0:T(8,128)(2,1)}, u32[]{:S(2)}, u32[]{:S(2)}) collective-permute-start(bf16[256,1152]{1,0:T(8,128)(2,1)} %get-tuple-element.143), channel_id=1, source_target_pairs={{0,3},{1,2},{2,1},{3,0},{4,7},{5,6},{6,5},{7,4},{8,11},{9,10},{10,... | collective-permute-start | bytes 1769480 | tf_op jit(solution)/shard_map/ppermute | solution.py:33
  277.3 38.7 %collective-permute-start.41 = (bf16[4,144,1152]{2,1,0:T(8,128)(2,1)S(1)}, bf16[4,144,1152]{2,1,0:T(8,128)(2,1)S(1)}, u32[]{:S(2)}, u32[]{:S(2)}) collective-permute-start(bf16[4,144,1152]{2,1,0:T(8,128)(2,1)S(1)} %get-tuple-element.157), channel_id=1, source_target_pairs={{0,4},{4,0},{8,12},{12,8},{16,20},{20,16},{24,28},{28,24},{1,5},{5... | collective-permute-start | bytes 3981320 | tf_op jit(solution)/shard_map/ppermute | solution.py:33
  299.6 28.6 %collective-permute-start.33 = (bf16[256,1152]{1,0:T(8,128)(2,1)}, bf16[256,1152]{1,0:T(8,128)(2,1)}, u32[]{:S(2)}, u32[]{:S(2)}) collective-permute-start(bf16[256,1152]{1,0:T(8,128)(2,1)} %copy-done.20), channel_id=1, source_target_pairs={{0,3},{1,2},{2,1},{3,0},{4,7},{5,6},{6,5},{7,4},{8,11},{9,10},{10,... | collective-permute-start | bytes 1769480 | tf_op jit(solution)/shard_map/ppermute | solution.py:33
  299.6 28.6 %collective-permute-start.32 = (bf16[256,1152]{1,0:T(8,128)(2,1)}, bf16[256,1152]{1,0:T(8,128)(2,1)}, u32[]{:S(2)}, u32[]{:S(2)}) collective-permute-start(bf16[256,1152]{1,0:T(8,128)(2,1)} %copy-done.20), channel_id=1, source_target_pairs={{0,2},{1,3},{2,0},{3,1},{4,6},{5,7},{6,4},{7,5},{8,10},{9,11},{10,... | collective-permute-start | bytes 1769480 | tf_op jit(solution)/shard_map/ppermute | solution.py:33
  301.0 27.1 %collective-permute-start.31 = (bf16[256,1152]{1,0:T(8,128)(2,1)}, bf16[256,1152]{1,0:T(8,128)(2,1)}, u32[]{:S(2)}, u32[]{:S(2)}) collective-permute-start(bf16[256,1152]{1,0:T(8,128)(2,1)} %copy-done.20), channel_id=1, source_target_pairs={{0,1},{1,0},{2,3},{3,2},{4,5},{5,4},{6,7},{7,6},{8,9},{9,8},{10,11... | collective-permute-start | bytes 1769480 | tf_op jit(solution)/shard_map/ppermute | solution.py:33
  318.6 20.6 %collective-permute-start.42 = (bf16[2,144,1152]{2,1,0:T(8,128)(2,1)S(1)}, bf16[2,144,1152]{2,1,0:T(8,128)(2,1)S(1)}, u32[]{:S(2)}, u32[]{:S(2)}) collective-permute-start(bf16[2,144,1152]{2,1,0:T(8,128)(2,1)S(1)} %get-tuple-element.159), channel_id=1, source_target_pairs={{0,8},{4,12},{8,0},{12,4},{16,24},{20,28},{24,16},{28,20},{1,9},{5... | collective-permute-start | bytes 1990664 | tf_op jit(solution)/shard_map/ppermute | solution.py:33
  (138 other events, 873.9 us)
Sparse Core Ops, SparseCore 0:
  16.1 41.6 all-gather.1
  139.0 117.6 all-reduce.2
  259.1 63.5 reduce-scatter.1

commit v4 on v3

--- a/solution.py
+++ b/solution.py
@@ -378,22 +378,21 @@
 
 def attend_far_kernel(
     low_ref, high_ref, spot_ref, first_ref, length_ref, log_ref, query_ref, wide_ref, before_ref,
-    after_ref, *refs, tile, count,
+    after_ref, *refs, tile, own,
 ):
     pieces = refs[:-7]
     query_out, grad_out, before_out, after_out, total, before_total, after_total = refs[-7:]
     step = pl.program_id(0)
     block, features = query_ref.shape
-    piece_rows = pieces[0].shape[0]
     clear_at_start(before_total, after_total)
     total[...] = jnp.zeros_like(total)
     parts = []
-    for place in range(block // piece_rows):
-        target = step * (block // piece_rows) + place
-        part = jnp.zeros_like(pieces[0][...])
-        for number, piece in enumerate(pieces):
-            owner = (spot_ref[0] ^ (number % count)) + number // count * count
-            part = jnp.where(target == owner, piece[...], part)
+    for place in range(block // own):
+        target = step * (block // own) + place
+        rows = pl.ds(pl.multiple_of(target // len(pieces) * own, own), own)
+        part = jnp.zeros((own, features), query_ref.dtype)
+        for mask, piece in enumerate(pieces):
+            part = jnp.where(target % len(pieces) == spot_ref[0] ^ mask, piece[rows, :], part)
         parts.append(part)
     grad_rows = jnp.concatenate(parts, axis=0)
     grad_out[...] = grad_rows
@@ -427,16 +426,17 @@
         write_pairs(kv_out, kv_total, query_ref.shape[1])
 
 
-def attend_far(spot, ranges, logs, query, grads, wide, before, later, tile, block, after):
+def attend_far(
+    spot, ranges, logs, query, pieces, wide, before, later, tile, block, own, after
+):
     lows, highs, firsts, lengths = ranges
-    pieces = [piece for chunk in grads for piece in chunk]
     rows, features = query.shape
     across = pl.BlockSpec((1, block), lambda i, *_: (0, i))
     turned = pl.BlockSpec((features, block), lambda i, *_: (0, i))
     logged = pl.BlockSpec((features // HDIM, block), lambda i, *_: (0, i))
     pairs = (rows, whole_lanes(2 * features))
     return tied_call(
-        functools.partial(attend_far_kernel, tile=tile, count=len(grads[0])),
+        functools.partial(attend_far_kernel, tile=tile, own=own),
         (lows, highs, spot),
         (firsts, lengths, logs, query, wide, before, later, *pieces),
         after,
@@ -716,16 +716,24 @@
     )
 
 
-def grad_middle_kernel(spot_ref, *refs, count, image_count):
-    pieces = refs[:count]
+def owned_chunks(rows, width, count):
+    return pl.BlockSpec((rows, width), lambda c, spot: (c * count + spot[0], 0))
+
+
+def grad_middle_kernel(spot_ref, *refs, count, chunks, image_count):
+    pieces = refs[: count * chunks]
     (
         out_ref, attn_ref, token_ref, cot_ref, hot_ref, gate_ref, scale_ref, middle_out, attn_out,
         sum_out, bias_out,
-    ) = refs[count:-count]
+    ) = refs[count * chunks : -count]
+    clear_at_start(sum_out, bias_out)
     gate = spread(hot_ref, gate_ref)
     attn = attn_ref[...]
     normed, inverse = normed_rows(token_ref[...].astype(jnp.float32) + gate * attn)
-    gradient = sum_of(pieces) * (1.0 + spread(hot_ref, scale_ref))
+    hidden = pick(
+        pl.program_id(0), [sum_of(pieces[c * count : (c + 1) * count]) for c in range(chunks)]
+    )
+    gradient = hidden * (1.0 + spread(hot_ref, scale_ref))
     grad_middle = cot_ref[...].astype(jnp.float32) + norm_back_rows(gradient, normed, inverse)
     middle_out[...] = grad_middle
     grad_attn = (gate * grad_middle).astype(jnp.bfloat16)
@@ -733,51 +741,54 @@
     for mask, block_out in enumerate(refs[-count:]):
         rows = peer_rows(spot_ref, mask, block_out.shape[1])
         block_out[...] = rows_dot(grad_attn, out_ref[rows, :]).astype(jnp.bfloat16)
-    bias_out[...] = jnp.sum(grad_attn.astype(jnp.float32), axis=0, keepdims=True)
-    sum_out[...] = jnp.zeros_like(sum_out)
+    bias_out[...] += jnp.sum(grad_attn.astype(jnp.float32), axis=0, keepdims=True)
     add_image_sums(sum_out, 0, hot_ref, image_count, grad_middle * attn)
 
 
 def grad_middle_of(
-    spot, pieces, attn, tokens, cotangent, hot, table, out_full, image_count, chunk, after
+    spot, chunks, attn, tokens, cotangent, hot, table, out_full, image_count, after
 ):
+    count = len(chunks[0])
+    pieces = [piece for chunk in chunks for piece in chunk]
     rows, width = pieces[0].shape
-    features = out_full.shape[0] // len(pieces)
+    features = out_full.shape[0] // count
     high = table.shape[1]
-    count = len(pieces)
-    base = chunk * count
-    return tied_call(
-        functools.partial(grad_middle_kernel, count=count, image_count=image_count),
+    whole = rows * len(chunks)
+    mine = owned_chunks(rows, width, count)
+    return tied_call(
+        functools.partial(
+            grad_middle_kernel, count=count, chunks=len(chunks), image_count=image_count
+        ),
         (spot,),
         (*pieces, out_full, attn, tokens, cotangent, hot, table, table),
         after,
-        grid=(1,),
-        in_specs=[held((rows, width))] * count
+        grid=(len(chunks),),
+        in_specs=[held((rows, width))] * len(pieces)
         + [
             held(out_full.shape),
-            owned(rows, width, base),
-            owned(rows, width, base),
-            owned(rows, width, base),
-            owned(rows, hot.shape[1], base),
+            mine,
+            mine,
+            mine,
+            owned_chunks(rows, hot.shape[1], count),
             column(high, width, 2),
             column(high, width, 4),
         ],
         out_specs=[
-            fixed((rows, width)),
-            fixed((rows, width)),
+            down(rows, width),
+            down(rows, width),
             fixed((1, image_count, width)),
             fixed((1, width)),
         ]
-        + [fixed((rows, features))] * count,
+        + [down(rows, features)] * count,
         out_shape=[
-            shaped((rows, width), jnp.float32),
-            shaped((rows, width)),
+            shaped((whole, width), jnp.float32),
+            shaped((whole, width)),
             shaped((1, image_count, width), jnp.float32),
             shaped((1, width), jnp.float32),
         ]
-        + [shaped((rows, features))] * count,
-        vmem=16,
-        cost=cost(4),
+        + [shaped((whole, features))] * count,
+        vmem=60,
+        cost=cost(6),
     )
 
 
@@ -814,27 +825,22 @@
     )
 
 
-def owned_chunks(rows, width, count):
-    return pl.BlockSpec((rows, width), lambda c, spot: (c * count + spot[0], 0))
-
-
 def grad_tokens_kernel(spot_ref, *refs, count):
     pieces = refs[:count]
-    token_ref, hot_ref, scale_ref, *middle_refs, rows_out = refs[count:]
+    token_ref, hot_ref, scale_ref, middle_ref, rows_out = refs[count:]
     normed, inverse = normed_rows(token_ref[...].astype(jnp.float32))
     gradient = sum_of(pieces) * (1.0 + spread(hot_ref, scale_ref))
-    middle = pick(pl.program_id(0), [middle_ref[...] for middle_ref in middle_refs])
-    rows_out[...] = (middle + norm_back_rows(gradient, normed, inverse)).astype(jnp.bfloat16)
-
-
-def grad_tokens_of(spot, pieces, tokens, hot, table, grad_middle, after):
-    chunks = len(grad_middle)
-    rows, width = grad_middle[0].shape
+    rows_out[...] = (middle_ref[...] + norm_back_rows(gradient, normed, inverse)).astype(jnp.bfloat16)
+
+
+def grad_tokens_of(spot, pieces, tokens, hot, table, grad_middle, chunks, after):
+    whole, width = grad_middle.shape
+    rows = whole // chunks
     count = len(pieces)
     return tied_call(
         functools.partial(grad_tokens_kernel, count=count),
         (spot,),
-        (*pieces, tokens, hot, table, *grad_middle),
+        (*pieces, tokens, hot, table, grad_middle),
         after,
         grid=(chunks,),
         in_specs=[down(rows, width)] * count
@@ -842,8 +848,8 @@
             owned_chunks(rows, width, count),
             owned_chunks(rows, hot.shape[1], count),
             column(table.shape[1], width, 1),
-        ]
-        + [held((rows, width))] * chunks,
+            down(rows, width),
+        ],
         out_specs=down(rows, width),
         out_shape=shaped((rows * chunks, width)),
         vmem=12,
@@ -987,44 +993,29 @@
     )
 
 
-def mlp_weights_kernel(hidden_ref, grad_ref, pre_ref, act_ref, *refs):
-    own_refs, own_out, out = refs[:-2], refs[-2], refs[-1]
+def mlp_weights_kernel(hidden_ref, grad_ref, pre_ref, act_ref, out):
     units = pre_ref.shape[1]
-    own = own_refs[0].shape[0]
-
-    @pl.when(pl.program_id(0) == 0)
-    def _():
-        for c, own_ref in enumerate(own_refs):
-            own_out[c * own : (c + 1) * own, :] = own_ref[...]
-
     out[:, :units] = turned_dot(hidden_ref[...], pre_ref[...]).astype(jnp.bfloat16)
     out[:, units:] = turned_dot(grad_ref[...], act_ref[...]).astype(jnp.bfloat16)
 
 
-def mlp_weights(grad_mlp, hidden, pre, act, owned_rows, after):
+def mlp_weights(grad_mlp, hidden, pre, act, after):
     rows, width = grad_mlp.shape
     units = pre.shape[1]
     if units % 128:
         sides = [turned_dot(hidden, pre), turned_dot(grad_mlp, act)]
-        joined = jnp.concatenate([side.astype(jnp.bfloat16) for side in sides], axis=1)
-        return jnp.concatenate(owned_rows, axis=0), joined
+        return jnp.concatenate([side.astype(jnp.bfloat16) for side in sides], axis=1)
     part = width // 3
     across = pl.BlockSpec((rows, part), lambda i, *_: (0, i))
-    own = owned_rows[0].shape
-    all_owned = (own[0] * len(owned_rows), width)
     return tied_call(
         mlp_weights_kernel,
         (),
-        (hidden, grad_mlp, pre, act, *owned_rows),
+        (hidden, grad_mlp, pre, act),
         after,
         grid=(3,),
-        in_specs=[across, across, held((rows, units)), held((rows, units))]
-        + [held(own)] * len(owned_rows),
-        out_specs=[
-            fixed(all_owned),
-            pl.BlockSpec((part, 2 * units), lambda i, *_: (i, 0)),
-        ],
-        out_shape=[shaped(all_owned), shaped((width, 2 * units))],
+        in_specs=[across, across, held((rows, units)), held((rows, units))],
+        out_specs=pl.BlockSpec((part, 2 * units), lambda i, *_: (i, 0)),
+        out_shape=shaped((width, 2 * units)),
         vmem=28,
         cost=cost(7),
     )
@@ -1210,27 +1201,17 @@
         act, down_weight, cotangent, hot, image_count, ROW_BLOCK, hidden_pieces[0]
     )
     mlp = lax.psum(mlp_part, "head")
-
-    grad_middle, grad_attn, grad_attended, gate_sums, out_sums = [], [], [], [], []
-    last = [mlp_sums]
-    for c in range(CHUNKS):
-        got = grad_middle_of(
-            spot, hidden_pieces[c], attn, tokens, cotangent, hot, table, out_full, image_count, c,
-            last,
-        )
-        grad_middle.append(got[0])
-        grad_attn.append(got[1])
-        gate_sums.append(got[2][0])
-        out_sums.append(got[3])
-        grad_attended.append(swap_pieces(got[4:], "head"))
-        last = [got[3]]
-    grad_own, weight_part = mlp_weights(
-        grad_mlp, hidden_two, grad_pre, act, grad_attn, last + grad_attended[0]
-    )
-
+    weight_part = mlp_weights(grad_mlp, hidden_two, grad_pre, act, [mlp_sums])
+
+    grad_middle, grad_own, gate_sums, out_sums, *attended_pieces = grad_middle_of(
+        spot, hidden_pieces, attn, tokens, cotangent, hot, table, out_full, image_count,
+        [weight_part],
+    )
+
+    own_rows = row_count // CHUNKS // head_size
     query_started, grad_rows, to_before, to_after = attend_far(
-        spot, ranges, logs, query, grad_attended, attended_wide, kv_before, kv_after,
-        KEY_TILE, QUERY_BLOCK, [grad_own],
+        spot, ranges, logs, query, swap_pieces(attended_pieces, "head"), attended_wide, kv_before,
+        kv_after, KEY_TILE, QUERY_BLOCK, own_rows, [],
     )
     grad_attn = gather_pieces(grad_own, "head")
     from_after = step_along(to_before, "seq", False)
@@ -1242,7 +1223,7 @@
 
     grad_all, first_sums, qkv_sums, *one_pieces = grad_hidden_of(
         spot, grad_query, kv_near, from_after, from_before, weight, tokens, hot, image_count,
-        ROW_BLOCK, row_count // CHUNKS // head_size, head_size, grad_attn,
+        ROW_BLOCK, own_rows, head_size, grad_attn,
     )
     one_pieces = swap_pieces(one_pieces, "head")
     attn_part = attn_weights(
@@ -1252,33 +1233,42 @@
         mlp, attn, tokens, hot, table, down_bias[None], ROW_BLOCK, [attn_part[0]]
     )
     own_tokens = grad_tokens_of(
-        spot, one_pieces, tokens, hot, table, grad_middle, [layer_out]
-    )
+        spot, one_pieces, tokens, hot, table, grad_middle, CHUNKS, [layer_out]
+    )
+    token_pieces = gather_pieces(own_tokens, "head")
+    last = own_tokens
+    if blocks:
+        kept, sent = fold_blocks(
+            ((my_index // 2) % 2).astype(jnp.int32).reshape(1),
+            attn_part[0],
+            swap(attn_part[1], "seq", 1),
+            [own_tokens],
+        )
+        last = kept
     sum_stack, kept_rows = split_columns(
         spot,
-        [[first_sums.reshape(2 * image_count, width)], gate_sums, late_sums, [mlp_sums[0]]]
-        + [out_sums],
+        [[first_sums.reshape(2 * image_count, width)], [gate_sums[0]], late_sums, [mlp_sums[0]]]
+        + [[out_sums]],
         [[qkv_sums], up_sums, [grad_down_bias]],
         head_size,
-        [own_tokens],
-    )
-    token_pieces = gather_pieces(own_tokens, "head")
+        [last],
+    )
+    sums = fold_pieces(sum_stack, "head")
     if blocks:
-        kept, sent = attn_part
-        mask = 1
+        mask = 2
         while mask < blocks // 2:
             mask *= 2
             kept, sent = fold_blocks(
                 ((my_index // mask) % 2).astype(jnp.int32).reshape(1),
                 kept,
                 swap(sent, "seq", mask // 2),
-                [kept_rows],
+                [sums],
             )
         attn_got = [kept, swap(sent, "seq", mask)]
+
     own_down = lax.dynamic_slice_in_dim(down_bias, me * columns, columns, 0).astype(jnp.float32)
     own_cot = lax.dynamic_slice_in_dim(cot_sums, me * columns, columns, 1) * own_down[None]
     mods = 6 * image_count
-    sums = fold_pieces(sum_stack, "head")
     sums = sums + jnp.pad(own_cot, ((5 * image_count, 1), (0, 0)))
     sums = butterfly_sum(jnp.concatenate([sums, kept_rows], axis=0), "seq")
     grad_mod = sums[:mods].reshape(6, image_count, columns)

time: 377 us -> 354 us (0.939)
  local copies, waits for them, and re-layouts: 80.9 us -> 55.2 us
  starting transfers between devices: 73.3 us -> 63.7 us
  Pallas kernels: 125 us -> 134 us
  waiting for transfers between devices: 60.6 us -> 67.2 us
    unnamed x233 -> x175, local copies, waits for them, and re-layouts: 70.4 us -> 47.2 us
    ppermute x40 -> x37, waiting for transfers between devices: 44.6 us -> 67.1 us  [swap(): return lax.ppermute(value, axis, [(i, i ^ mask) for i in range(count)])]
    psum x1, waiting for transfers between devices: 15.9 us -> 0.02 us  [on_device(): mlp = lax.psum(mlp_part, 'head')]
    ppermute x40 -> x37, starting transfers between devices: 62.5 us -> 53.6 us  [swap(): return lax.ppermute(value, axis, [(i, i ^ mask) for i in range(count)])]
    pallas_call x21 -> x20, Pallas kernels: 125 us -> 134 us  [tied_call(): pl.pallas_call(body, grid_spec=pltpu.PrefetchScalarGridSpec(num_scalar_pr...]
  transfers between devices with their start and end apart: 47 -> 44, of which waited for: 16 -> 17; matrix products, arithmetic and copies ran while one was open for 5% -> 5% of each run, Pallas kernels for 32% -> 37%
where the time goes in v4:
time: 354 us; the launch traced here: 350 us
  Pallas kernels  134 us (38%)
  waiting for transfers between devices  67.2 us (19%)
  starting transfers between devices  63.7 us (18%)
  local copies, waits for them, and re-layouts  55.2 us (16%)
  between operations  15.1 us (4%)
  matrix products  8.82 us (2%)
  other arithmetic  6.12 us (2%)
    pallas_call x20, Pallas kernels, tied_call(): pl.pallas_call(body, grid_spec=pltpu.PrefetchScalarGridSpec(num_scalar_pr...  134 us
    ppermute x37, waiting for transfers between devices, swap(): return lax.ppermute(value, axis, [(i, i ^ mask) for i in range(count)])  67.1 us
    ppermute x37, starting transfers between devices, swap(): return lax.ppermute(value, axis, [(i, i ^ mask) for i in range(count)])  53.6 us
    unnamed x175, local copies, waits for them, and re-layouts  47.2 us
    ppermute x4, starting transfers between devices, step_along(): return lax.ppermute(value, axis, pairs)  9.98 us
  transfers between devices with their start and end apart: 44, of which 17 were waited for; matrix products, arithmetic and copies ran while one was open for 5% of the time, Pallas kernels for 37%

profile of v4, /device:TPU:0, one launch (start us, length us, event | category | flops | bytes accessed | tf_op | source)
XLA Modules:
  0.0 349.9 jit_solution(15785510830936851915)
XLA Ops:
  7.9 3.5 fusion
  26.0 6.1 %shard_map.237 = (bf16[1024,1152]{1,0:T(8,128)(2,1)S(1)}, bf16[1024,288]{1,0:T(8,128)(2,1)S(1)}, bf16[1024,640]{1,0:T(8,128)(2,1)}) custom-call(bf16[1024,1152]{1,0:T(8,128)(2,1)S(1)} %copy-done.17, bf16[1024,48]{1,0:T(8,128)(2,1)S(1)} %compare_convert_fusion.refs_1_.refs_2_.refs_8_.refs_11_.refs_7_.refs_14_.refs_4_, ...), custom_call_target="tpu_custom_call" | custom-call | flops 6899999744 | bytes 1 | tf_op jit(solution)/shard_map/pallas_call | solution.py:90
  35.6 4.3 %collective-permute-start.3 = (bf16[1024,640]{1,0:T(8,128)(2,1)}, bf16[1024,640]{1,0:T(8,128)(2,1)}, u32[]{:S(2)}, u32[]{:S(2)}) collective-permute-start(bf16[1024,640]{1,0:T(8,128)(2,1)} %get-tuple-element.82.refs_7_), channel_id=1, source_target_pairs={{0,4},{4,8},{8,12},{12,16},{16,20},{20,24},{24,28},{1,5},{5,9},{9,... | collective-permute-start | bytes 3932168 | tf_op jit(solution)/shard_map/ppermute | solution.py:63
  45.9 5.1 %shard_map.238 = (bf16[1024,1152]{1,0:T(8,128)(2,1)S(1)}, f32[1024,1152]{1,0:T(8,128)S(1)}, f32[1,1152]{1,0:T(1,128)S(1)}, f32[16,1152]{1,0:T(8,128)S(1)}) custom-call(bf16[1024,1152]{1,0:T(8,128)(2,1)S(1)} %copy-done.59, bf16[1024,1152]{1,0:T(8,128)(2,1)S(1)} %copy-done.15, ...), custom_call_target="tpu_custom_call" | custom-call | flops 5750000128 | bytes 1 | tf_op jit(solution)/shard_map/pallas_call | solution.py:90
  53.9 10.3 %shard_map.239 = (bf16[512,288]{1,0:T(8,128)(2,1)S(1)}, f32[288,512]{1,0:T(8,128)S(1)}, f32[4,512]{1,0:T(4,128)S(1)}) custom-call(s32[4]{0:T(128)S(1)} %get-tuple-element.212.refs_0_, s32[4]{0:T(128)S(1)} %get-tuple-element.211.refs_1_, f32[1,1152]{1,0:T(1,128)S(1)} %get-tuple-element.80.refs_2_.refs_11_, s32[1,1024]{1,0:T(1,128)S(1)} %bitcast.36, ...), custom_call_target="tpu_custom_call" | custom-call | flops 11500000256 | bytes 1 | tf_op jit(solution)/shard_map/pallas_call | solution.py:90
  67.8 12.5 %shard_map.240 = (bf16[512,288]{1,0:T(8,128)(2,1)}, f32[288,512]{1,0:T(8,128)S(1)}, f32[4,512]{1,0:T(4,128)S(1)}) custom-call(s32[4]{0:T(128)S(1)} %get-tuple-element.212.refs_0_, s32[4]{0:T(128)S(1)} %get-tuple-element.211.refs_1_, f32[4,512]{1,0:T(4,128)S(1)} %get-tuple-element.83.refs_2_, s32[1,1024]{1,0:T(1,128)S(1)} %bitcast.37, ...), custom_call_target="tpu_custom_call" | custom-call | flops 11500000256 | bytes 1 | tf_op jit(solution)/shard_map/pallas_call | solution.py:90
  97.1 12.0 %shard_map.241 = (f32[1024,1152]{1,0:T(8,128)}, bf16[1024,1152]{1,0:T(8,128)(2,1)S(1)}, bf16[1024,1152]{1,0:T(8,128)(2,1)S(1)}, bf16[1024,1152]{1,0:T(8,128)(2,1...) custom-call(s32[1]{0:T(128)} %bitcast.refs_0_.refs_2_, ...), custom_call_target="tpu_custom_call" | custom-call | flops 13799999488 | bytes 1 | tf_op jit(solution)/shard_map/pallas_call | solution.py:90
  112.7 12.3 %shard_map.242 = (f32[1024,1152]{1,0:T(8,128)}, bf16[1024,1152]{1,0:T(8,128)(2,1)S(1)}, bf16[1024,1152]{1,0:T(8,128)(2,1)S(1)}, bf16[1024,1152]{1,0:T(8,128)(2,1...) custom-call(s32[1]{0:T(128)} %bitcast.refs_0_.refs_2_, ...), custom_call_target="tpu_custom_call", output_to_operand_aliasing={{0}: (1, {}), {1}: (2, {}), {2}: (3, {}), {3}: (4, {})} | custom-call | flops 13799999488 | bytes 1 | tf_op jit(solution)/shard_map/pallas_call | solution.py:90
  125.9 5.8 %shard_map.243 = (bf16[1024,1152]{1,0:T(8,128)(2,1)}, f32[1,16,1152]{2,1,0:T(8,128)S(1)}) custom-call(bf16[128,1152]{1,0:T(8,128)(2,1)S(1)} %get-tuple-element.87.refs_0_.refs_2_, bf16[128,1152]{1,0:T(8,128)(2,1)S(1)} %collective-permute-done.8.refs_1_.refs_3_, bf16[128,1152]{1,0:T(8,128)(2,1)S(1)} %collective-permute-done.9.refs_2_.refs_4_, ...), custom_call_target="tpu_custom_call" | custom-call | flops 6899999744 | bytes 1 | tf_op jit(solution)/shard_map/pallas_call | solution.py:90
  142.7 7.7 %shard_map.244.refs_1_ = bf16[1152,2304]{1,0:T(8,128)(2,1)S(1)} custom-call(f32[1,16,1152]{2,1,0:T(8,128)S(1)} %get-tuple-element.97.refs_0_, bf16[1024,1152]{1,0:T(8,128)(2,1)S(1)} %copy-done.67, bf16[1024,1152]{1,0:T(8,128)(2,1)S(1)} %copy-done.62, bf16[1024,1152]{1,0:T(8,128)(2,1)S(1)} %copy-done.71, bf16[1024,1152]{1,0:T(8,128)(2,1)S(1)} %copy-done.69), custom_call_target="tpu_custom_call" | custom-call | flops 8049999872 | bytes 1 | tf_op jit(solution)/shard_map/pallas_call | solution.py:90
  153.1 8.2 %shard_map.245 = (f32[256,1152]{1,0:T(8,128)}, bf16[256,1152]{1,0:T(8,128)(2,1)}, f32[1,16,1152]{2,1,0:T(8,128)}, f32[1,1152]{1,0:T(1,128)}, bf16[256,288]{1,0:T...) custom-call(s32[1]{0:T(128)} %bitcast.refs_0_.refs_2_, ...), custom_call_target="tpu_custom_call" | custom-call | flops 6899999744 | bytes 1 | tf_op jit(solution)/shard_map/pallas_call | solution.py:90
  171.5 11.0 %collective-permute-done.21.refs_12_ = bf16[256,288]{1,0:T(8,128)(2,1)} collective-permute-done((bf16[256,288]{1,0:T(8,128)(2,1)}, bf16[256,288]{1,0:T(8,128)(2,1)}, u32[]{:S(2)}, u32[]{:S(2)}) %collective-permute-start.21) | collective-permute-done | bytes 147488 | tf_op jit(solution)/shard_map/ppermute | solution.py:33
  183.7 6.3 %shard_map.246 = (f32[288,1024]{1,0:T(8,128)S(1)}, bf16[1024,288]{1,0:T(8,128)(2,1)S(1)}, bf16[1024,640]{1,0:T(8,128)(2,1)S(1)}, bf16[1024,640]{1,0:T(8,128)(2,1)S(1)}) custom-call(s32[4]{0:T(128)S(1)} %get-tuple-element.212.refs_0_, s32[4]{0:T(128)S(1)} %get-tuple-element.211.refs_1_, s32[1]{0:T(128)} %bitcast.refs_0_.refs_2_, s32[1,1024]{1,0:T(1,128)S(1)} %bitcast.38, ...), custom_call_target="tpu_custom_call" | custom-call | flops 9200000000 | bytes 1 | tf_op jit(solution)/shard_map/pallas_call | solution.py:90
  194.4 17.8 %shard_map.247 = (bf16[1024,288]{1,0:T(8,128)(2,1)S(1)}, f32[1024,640]{1,0:T(8,128)S(1)}) custom-call(s32[4]{0:T(128)S(1)} %get-tuple-element.212.refs_0_, s32[4]{0:T(128)S(1)} %get-tuple-element.211.refs_1_, s32[1,1024]{1,0:T(1,128)S(1)} %bitcast.39, s32[1,1024]{1,0:T(1,128)S(1)} %bitcast.35, ...), custom_call_target="tpu_custom_call" | custom-call | flops 18400000000 | bytes 1 | tf_op jit(solution)/shard_map/pallas_call | solution.py:90
  212.3 8.0 %shard_map.248 = (bf16[1024,864]{1,0:T(8,128)(2,1)S(1)}, f32[2,16,1152]{2,1,0:T(8,128)S(1)}, f32[1,864]{1,0:T(1,128)S(1)}, bf16[256,1152]{1,0:T(8,128)(2,1)S(1)}...) custom-call(s32[1]{0:T(128)} %bitcast.refs_0_.refs_2_, ...), custom_call_target="tpu_custom_call" | custom-call | flops 9200000000 | bytes 1 | tf_op jit(solution)/shard_map/pallas_call | solution.py:90
  221.1 6.8 %shard_map.249 = (bf16[4,144,1152]{2,1,0:T(8,128)(2,1)S(1)}, bf16[4,144,1152]{2,1,0:T(8,128)(2,1)}) custom-call(s32[1]{0:T(128)} %bitcast.refs_0_.refs_2_, s32[1]{0:T(128)} %bitcast.1.refs_1_, bf16[1024,1152]{1,0:T(8,128)(2,1)S(1)} %copy-done.60, bf16[1024,864]{1,0:T(8,128)(2,1)S(1)} %get-tuple-element.119.refs_3_, bf16[512,288]{1,0:T(8,128)(2,1)S(1)} %copy-done.26, ...), custom_call_target="tpu_custom_call" | custom-call | flops 8049999872 | bytes 1 | tf_op jit(solution)/shard_map/pallas_call | solution.py:90
  229.0 8.3 %collective-permute-start.31 = (bf16[4,144,1152]{2,1,0:T(8,128)(2,1)}, bf16[4,144,1152]{2,1,0:T(8,128)(2,1)}, u32[]{:S(2)}, u32[]{:S(2)}) collective-permute-start(bf16[4,144,1152]{2,1,0:T(8,128)(2,1)} %get-tuple-element.127), channel_id=1, source_target_pairs={{0,4},{4,0},{8,12},{12,8},{16,20},{20,16},{24,28},{28,24},{1,5},{5... | collective-permute-start | bytes 3981320 | tf_op jit(solution)/shard_map/ppermute | solution.py:33
  253.9 15.0 %collective-permute-done.26.refs_4_ = bf16[256,1152]{1,0:T(8,128)(2,1)} collective-permute-done((bf16[256,1152]{1,0:T(8,128)(2,1)}, bf16[256,1152]{1,0:T(8,128)(2,1)}, u32[]{:S(2)}, u32[]{:S(2)}) %collective-permute-start.26) | collective-permute-done | bytes 589856 | tf_op jit(solution)/shard_map/ppermute | solution.py:33
  277.9 6.9 %collective-permute-done.32 = f32[2,97,288]{2,1,0:T(8,128)S(1)} collective-permute-done((f32[2,97,288]{2,1,0:T(8,128)S(1)}, f32[2,97,288]{2,1,0:T(8,128)S(1)}, u32[]{:S(2)}, u32[]{:S(2)}) %collective-permute-start.32) | collective-permute-done | bytes 223520 | tf_op jit(solution)/shard_map/ppermute | solution.py:33
  295.5 5.2 %collective-permute-done.35 = f32[108,288]{1,0:T(8,128)S(1)} collective-permute-done((f32[108,288]{1,0:T(8,128)S(1)}, f32[108,288]{1,0:T(8,128)S(1)}, u32[]{:S(2)}, u32[]{:S(2)}) %collective-permute-start.35) | collective-permute-done | bytes 124448 | tf_op jit(solution)/shard_map/ppermute | solution.py:33
  301.0 4.3 %collective-permute-done.30.refs_4_ = bf16[256,1152]{1,0:T(8,128)(2,1)S(1)} collective-permute-done((bf16[256,1152]{1,0:T(8,128)(2,1)S(1)}, bf16[256,1152]{1,0:T(8,128)(2,1)S(1)}, u32[]{:S(2)}, u32[]{:S(2)}) %collective-permute-start.30) | collective-permute-done | bytes 589856 | tf_op jit(solution)/shard_map/ppermute | solution.py:33
  305.3 8.8 %collective-permute-done.29.refs_3_ = bf16[256,1152]{1,0:T(8,128)(2,1)} collective-permute-done((bf16[256,1152]{1,0:T(8,128)(2,1)S(1)}, bf16[256,1152]{1,0:T(8,128)(2,1)}, u32[]{:S(2)}, u32[]{:S(2)}) %collective-permute-start.29) | collective-permute-done | bytes 589856 | tf_op jit(solution)/shard_map/ppermute | solution.py:33
  314.9 5.2 %shard_map.252 = f32[1024,1152]{1,0:T(8,128)} custom-call(s32[1]{0:T(128)} %bitcast.refs_0_.refs_2_, bf16[256,1152]{1,0:T(8,128)(2,1)S(1)} %copy-done.23, bf16[256,1152]{1,0:T(8,128)(2,1)} %collective-permute-done.28.refs_2_, bf16[256,1152]{1,0:T(8,128)(2,1)} %collective-permute-done.29.refs_3_, bf16[256,1152]{1,0:T(8,128)(2,1)S(1)} %collective-permute-done.30.refs_4_), custom_call_target="tpu_custom_call" | custom-call | flops 3449999872 | bytes 1 | tf_op jit(solution)/shard_map/pallas_call | solution.py:90
  332.8 4.5 %fusion.4 = f32[1152,6,288]{0,2,1:T(8,128)} fusion(bf16[16,1152]{1,0:T(8,128)(2,1)S(1)} %get-tuple-element.209, bf16[6,16,288]{2,1,0:T(8,128)(2,1)S(1)} %get-tuple-element.206, bf16[6,16,288]{2,1,0:T(8,128)(2,1)S(1)} %get-tuple-element.207, bf16[6,16,288]{2,1,0:T(8,128)(2,1)S(1)} %get-tuple-element.208), kind=kOutput, calls=%fused_computation.31 | convolution fusion | flops 191932416 | bytes 8165376 | tf_op jit(solution)/shard_map/id,kif->dkf/dot_general | solution.py:1293
  (321 shorter events, 139.2 us)
Async XLA Ops:
  7.2 79.8 %all-gather.2.cloned.1.call-start = ((), (), s32[]{:S(2)}) async-start(), calls=%async_computation.1 | async-start | bytes 3317760 | tf_op jit(solution)/shard_map/all_gather | solution.py:1160
  16.0 226.8 %all-reduce.3.cloned.1.call-start = ((), (), s32[]{:S(2)}) async-start(), calls=%async_computation.2 | async-start | bytes 4718592 | tf_op jit(solution)/shard_map/psum | solution.py:1203
  34.3 19.5 %collective-permute-start.4 = (bf16[1024,640]{1,0:T(8,128)(2,1)}, bf16[1024,640]{1,0:T(8,128)(2,1)}, u32[]{:S(2)}, u32[]{:S(2)}) collective-permute-start(bf16[1024,640]{1,0:T(8,128)(2,1)} %get-tuple-element.82.refs_7_), channel_id=1, source_target_pairs={{4,0},{8,4},{12,8},{16,12},{20,16},{24,20},{28,24},{5,1},{9,5},{13... | collective-permute-start | bytes 3932168 | tf_op jit(solution)/shard_map/ppermute | solution.py:63
  64.2 19.6 %collective-permute-start.7 = (bf16[512,288]{1,0:T(8,128)(2,1)S(1)}, bf16[512,288]{1,0:T(8,128)(2,1)S(1)}, u32[]{:S(2)}, u32[]{:S(2)}) collective-permute-start(bf16[512,288]{1,0:T(8,128)(2,1)S(1)} %get-tuple-element.85.refs_2_.refs_4_), channel_id=1, source_target_pairs={{0,3},{1,2},{2,1},{3,0},{4,7},{5,6},{6,5},{7,4},{8,11},{9,10},{10,... | collective-permute-start | bytes 884744 | tf_op jit(solution)/shard_map/ppermute | solution.py:33
  65.5 20.0 %collective-permute-start.6 = (bf16[512,288]{1,0:T(8,128)(2,1)S(1)}, bf16[512,288]{1,0:T(8,128)(2,1)S(1)}, u32[]{:S(2)}, u32[]{:S(2)}) collective-permute-start(bf16[512,288]{1,0:T(8,128)(2,1)S(1)} %get-tuple-element.85.refs_2_.refs_4_), channel_id=1, source_target_pairs={{0,2},{1,3},{2,0},{3,1},{4,6},{5,7},{6,4},{7,5},{8,10},{9,11},{10,... | collective-permute-start | bytes 884744 | tf_op jit(solution)/shard_map/ppermute | solution.py:33
  81.1 29.8 %collective-permute-start.13 = (bf16[512,288]{1,0:T(8,128)(2,1)}, bf16[512,288]{1,0:T(8,128)(2,1)}, u32[]{:S(2)}, u32[]{:S(2)}) collective-permute-start(bf16[512,288]{1,0:T(8,128)(2,1)} %get-tuple-element.95.refs_5_), channel_id=1, source_target_pairs={{0,3},{1,2},{2,1},{3,0},{4,7},{5,6},{6,5},{7,4},{8,11},{9,10},{10,... | collective-permute-start | bytes 884744 | tf_op jit(solution)/shard_map/ppermute | solution.py:33
  82.2 30.4 %collective-permute-start.12 = (bf16[512,288]{1,0:T(8,128)(2,1)}, bf16[512,288]{1,0:T(8,128)(2,1)}, u32[]{:S(2)}, u32[]{:S(2)}) collective-permute-start(bf16[512,288]{1,0:T(8,128)(2,1)} %get-tuple-element.95.refs_5_), channel_id=1, source_target_pairs={{0,2},{1,3},{2,0},{3,1},{4,6},{5,7},{6,4},{7,5},{8,10},{9,11},{10,... | collective-permute-start | bytes 884744 | tf_op jit(solution)/shard_map/ppermute | solution.py:33
  84.6 28.0 %collective-permute-start.11 = (bf16[512,288]{1,0:T(8,128)(2,1)}, bf16[512,288]{1,0:T(8,128)(2,1)}, u32[]{:S(2)}, u32[]{:S(2)}) collective-permute-start(bf16[512,288]{1,0:T(8,128)(2,1)} %get-tuple-element.95.refs_5_), channel_id=1, source_target_pairs={{0,1},{1,0},{2,3},{3,2},{4,5},{5,4},{6,7},{7,6},{8,9},{9,8},{10,11... | collective-permute-start | bytes 884744 | tf_op jit(solution)/shard_map/ppermute | solution.py:33
  131.8 208.3 %reduce-scatter.2.cloned.1.call-start = ((), (), s32[]{:S(2)}) async-start(), calls=%async_computation.3 | async-start | bytes 5971968 | tf_op jit(solution)/shard_map/reduce_scatter | solution.py:1301
  131.9 20.8 %collective-permute-start.14 = (bf16[128,1152]{1,0:T(8,128)(2,1)}, bf16[128,1152]{1,0:T(8,128)(2,1)}, u32[]{:S(2)}, u32[]{:S(2)}) collective-permute-start(bf16[128,1152]{1,0:T(8,128)(2,1)} %copy-done.40), channel_id=1, source_target_pairs={{0,1},{1,0},{2,3},{3,2},{4,5},{5,4},{6,7},{7,6},{8,9},{9,8},{10,11... | collective-permute-start | bytes 884744 | tf_op jit(solution)/shard_map/ppermute | solution.py:33
  132.8 19.9 %collective-permute-start.15 = (bf16[128,1152]{1,0:T(8,128)(2,1)S(1)}, bf16[128,1152]{1,0:T(8,128)(2,1)}, u32[]{:S(2)}, u32[]{:S(2)}) collective-permute-start(bf16[128,1152]{1,0:T(8,128)(2,1)S(1)} %copy-done.39), channel_id=1, source_target_pairs={{0,2},{1,3},{2,0},{3,1},{4,6},{5,7},{6,4},{7,5},{8,10},{9,11},{10,... | collective-permute-start | bytes 884744 | tf_op jit(solution)/shard_map/ppermute | solution.py:33
  163.3 19.2 %collective-permute-start.21 = (bf16[256,288]{1,0:T(8,128)(2,1)}, bf16[256,288]{1,0:T(8,128)(2,1)}, u32[]{:S(2)}, u32[]{:S(2)}) collective-permute-start(bf16[256,288]{1,0:T(8,128)(2,1)} %get-tuple-element.111), channel_id=1, source_target_pairs={{0,2},{1,3},{2,0},{3,1},{4,6},{5,7},{6,4},{7,5},{8,10},{9,11},{10,... | collective-permute-start | bytes 442376 | tf_op jit(solution)/shard_map/ppermute | solution.py:33
  166.0 46.2 %collective-permute-start.19 = (bf16[256,1152]{1,0:T(8,128)(2,1)}, bf16[256,1152]{1,0:T(8,128)(2,1)}, u32[]{:S(2)}, u32[]{:S(2)}) collective-permute-start(bf16[256,1152]{1,0:T(8,128)(2,1)} %get-tuple-element.106.refs_1_.refs_6_), channel_id=1, source_target_pairs={{0,3},{1,2},{2,1},{3,0},{4,7},{5,6},{6,5},{7,4},{8,11},{9,10},{10,... | collective-permute-start | bytes 1769480 | tf_op jit(solution)/shard_map/ppermute | solution.py:33
  168.5 43.8 %collective-permute-start.18 = (bf16[256,1152]{1,0:T(8,128)(2,1)}, bf16[256,1152]{1,0:T(8,128)(2,1)}, u32[]{:S(2)}, u32[]{:S(2)}) collective-permute-start(bf16[256,1152]{1,0:T(8,128)(2,1)} %get-tuple-element.106.refs_1_.refs_6_), channel_id=1, source_target_pairs={{0,2},{1,3},{2,0},{3,1},{4,6},{5,7},{6,4},{7,5},{8,10},{9,11},{10,... | collective-permute-start | bytes 1769480 | tf_op jit(solution)/shard_map/ppermute | solution.py:33
  169.5 42.8 %collective-permute-start.17 = (bf16[256,1152]{1,0:T(8,128)(2,1)}, bf16[256,1152]{1,0:T(8,128)(2,1)S(1)}, u32[]{:S(2)}, u32[]{:S(2)}) collective-permute-start(bf16[256,1152]{1,0:T(8,128)(2,1)} %get-tuple-element.106.refs_1_.refs_6_), channel_id=1, source_target_pairs={{0,1},{1,0},{2,3},{3,2},{4,5},{5,4},{6,7},{7,6},{8,9},{9,8},{10,11... | collective-permute-start | bytes 1769480 | tf_op jit(solution)/shard_map/ppermute | solution.py:33
  190.0 22.3 %collective-permute-start.23 = (bf16[1024,640]{1,0:T(8,128)(2,1)S(1)}, bf16[1024,640]{1,0:T(8,128)(2,1)S(1)}, u32[]{:S(2)}, u32[]{:S(2)}) collective-permute-start(bf16[1024,640]{1,0:T(8,128)(2,1)S(1)} %get-tuple-element.117), channel_id=1, source_target_pairs={{4,0},{8,4},{12,8},{16,12},{20,16},{24,20},{28,24},{5,1},{9,5},{13... | collective-permute-start | bytes 3932168 | tf_op jit(solution)/shard_map/ppermute | solution.py:63
  191.3 21.0 %collective-permute-start.24 = (bf16[1024,640]{1,0:T(8,128)(2,1)S(1)}, bf16[1024,640]{1,0:T(8,128)(2,1)S(1)}, u32[]{:S(2)}, u32[]{:S(2)}) collective-permute-start(bf16[1024,640]{1,0:T(8,128)(2,1)S(1)} %get-tuple-element.118), channel_id=1, source_target_pairs={{0,4},{4,8},{8,12},{12,16},{16,20},{20,24},{24,28},{1,5},{5,9},{9,... | collective-permute-start | bytes 3932168 | tf_op jit(solution)/shard_map/ppermute | solution.py:63
  229.0 43.9 %collective-permute-start.31 = (bf16[4,144,1152]{2,1,0:T(8,128)(2,1)}, bf16[4,144,1152]{2,1,0:T(8,128)(2,1)}, u32[]{:S(2)}, u32[]{:S(2)}) collective-permute-start(bf16[4,144,1152]{2,1,0:T(8,128)(2,1)} %get-tuple-element.127), channel_id=1, source_target_pairs={{0,4},{4,0},{8,12},{12,8},{16,20},{20,16},{24,28},{28,24},{1,5},{5... | collective-permute-start | bytes 3981320 | tf_op jit(solution)/shard_map/ppermute | solution.py:33
  239.4 29.4 %collective-permute-start.26 = (bf16[256,1152]{1,0:T(8,128)(2,1)}, bf16[256,1152]{1,0:T(8,128)(2,1)}, u32[]{:S(2)}, u32[]{:S(2)}) collective-permute-start(bf16[256,1152]{1,0:T(8,128)(2,1)} %get-tuple-element.124), channel_id=1, source_target_pairs={{0,2},{1,3},{2,0},{3,1},{4,6},{5,7},{6,4},{7,5},{8,10},{9,11},{10,... | collective-permute-start | bytes 1769480 | tf_op jit(solution)/shard_map/ppermute | solution.py:33
  242.7 26.2 %collective-permute-start.27 = (bf16[256,1152]{1,0:T(8,128)(2,1)}, bf16[256,1152]{1,0:T(8,128)(2,1)}, u32[]{:S(2)}, u32[]{:S(2)}) collective-permute-start(bf16[256,1152]{1,0:T(8,128)(2,1)} %get-tuple-element.125), channel_id=1, source_target_pairs={{0,3},{1,2},{2,1},{3,0},{4,7},{5,6},{6,5},{7,4},{8,11},{9,10},{10,... | collective-permute-start | bytes 1769480 | tf_op jit(solution)/shard_map/ppermute | solution.py:33
  288.6 25.5 %collective-permute-start.29 = (bf16[256,1152]{1,0:T(8,128)(2,1)S(1)}, bf16[256,1152]{1,0:T(8,128)(2,1)}, u32[]{:S(2)}, u32[]{:S(2)}) collective-permute-start(bf16[256,1152]{1,0:T(8,128)(2,1)S(1)} %copy-done.23), channel_id=1, source_target_pairs={{0,2},{1,3},{2,0},{3,1},{4,6},{5,7},{6,4},{7,5},{8,10},{9,11},{10,... | collective-permute-start | bytes 1769480 | tf_op jit(solution)/shard_map/ppermute | solution.py:33
  289.3 25.6 %collective-permute-start.28 = (bf16[256,1152]{1,0:T(8,128)(2,1)S(1)}, bf16[256,1152]{1,0:T(8,128)(2,1)}, u32[]{:S(2)}, u32[]{:S(2)}) collective-permute-start(bf16[256,1152]{1,0:T(8,128)(2,1)S(1)} %copy-done.23), channel_id=1, source_target_pairs={{0,1},{1,0},{2,3},{3,2},{4,5},{5,4},{6,7},{7,6},{8,9},{9,8},{10,11... | collective-permute-start | bytes 1769480 | tf_op jit(solution)/shard_map/ppermute | solution.py:33
  294.0 29.0 %collective-permute-start.39 = (bf16[2,144,1152]{2,1,0:T(8,128)(2,1)S(1)}, bf16[2,144,1152]{2,1,0:T(8,128)(2,1)S(1)}, u32[]{:S(2)}, u32[]{:S(2)}) collective-permute-start(bf16[2,144,1152]{2,1,0:T(8,128)(2,1)S(1)} %get-tuple-element.140), channel_id=1, source_target_pairs={{0,8},{4,12},{8,0},{12,4},{16,24},{20,28},{24,16},{28,20},{1,9},{5... | collective-permute-start | bytes 1990664 | tf_op jit(solution)/shard_map/ppermute | solution.py:33
  300.8 19.3 %collective-permute-start.36 = (f32[108,288]{1,0:T(8,128)S(1)}, f32[108,288]{1,0:T(8,128)S(1)}, u32[]{:S(2)}, u32[]{:S(2)}) collective-permute-start(f32[108,288]{1,0:T(8,128)S(1)} %add.96), channel_id=1, source_target_pairs={{0,16},{4,20},{8,24},{12,28},{16,0},{20,4},{24,8},{28,12},{1,17},{... | collective-permute-start | bytes 373256 | tf_op jit(solution)/shard_map/ppermute | solution.py:33
  (106 other events, 896.9 us)
Sparse Core Ops, SparseCore 0:
  16.1 41.6 all-gather.1
  131.9 102.3 all-reduce.2
  236.7 61.0 reduce-scatter.1

commit v5 on v4

--- a/solution.py
+++ b/solution.py
@@ -1018,6 +1018,32 @@
         out_shape=shaped((width, 2 * units)),
         vmem=28,
         cost=cost(7),
+    )
+
+
+def mlp_total_kernel(total_ref, up_out, down_out):
+    units = up_out.shape[1]
+    total = total_ref[...].astype(jnp.float32)
+    up_out[...] = total[:, :units]
+    down_out[...] = total[:, units:].T
+
+
+def mlp_total_of(total, units):
+    size = total.shape[0]
+    if units % 128:
+        total = total.astype(jnp.float32)
+        return total[:, :units], total[:, units:].T
+    return tied_call(
+        mlp_total_kernel,
+        (),
+        (total,),
+        [],
+        grid=(1,),
+        in_specs=[held(total.shape)],
+        out_specs=[fixed((size, units)), fixed((units, size))],
+        out_shape=[shaped((size, units), jnp.float32), shaped((units, size), jnp.float32)],
+        vmem=12,
+        cost=cost(1),
     )
 
 
@@ -1299,7 +1325,7 @@
 
     grad_tokens = place_rows(spot, token_pieces, CHUNKS, jnp.float32, [])
     mlp_total = lax.psum_scatter(weight_part, "seq", scatter_dimension=0, tiled=True)
-    mlp_total = mlp_total.astype(jnp.float32)
+    grad_up_weight, grad_down_weight = mlp_total_of(mlp_total, units)
     if blocks:
         grad_out_weight, grad_qkv = attn_total_of(attn_got, feature_count, [])
         grad_qkv_weight = grad_qkv.transpose(1, 0, 2)
@@ -1316,9 +1342,9 @@
         grad_qv_bias,
         grad_out_weight,
         grad_out_bias,
-        mlp_total[:, :units],
+        grad_up_weight,
         grad_up_bias,
-        mlp_total[:, units:].T,
+        grad_down_weight,
         grad_down_bias,
         grad_ada_weight,
         grad_ada_bias,

time: 354 us -> 354 us (level)
    unnamed x175 -> x176, local copies, waits for them, and re-layouts: 47.2 us -> 49 us
    pallas_call x20 -> x21, Pallas kernels: 134 us -> 135 us  [tied_call(): pl.pallas_call(body, grid_spec=pltpu.PrefetchScalarGridSpec(num_scalar_pr...]
  transfers between devices with their start and end apart: 44 -> 44, of which waited for: 17 -> 18; matrix products, arithmetic and copies ran while one was open for 5% -> 5% of each run, Pallas kernels for 37% -> 37%
where the time goes in v5:
time: 354 us; the launch traced here: 350 us
  Pallas kernels  135 us (38%)
  waiting for transfers between devices  66.9 us (19%)
  starting transfers between devices  64.1 us (18%)
  local copies, waits for them, and re-layouts  55.2 us (16%)
  between operations  15.1 us (4%)
  matrix products  8.82 us (2%)
  other arithmetic  4.87 us (1%)
    pallas_call x21, Pallas kernels, tied_call(): pl.pallas_call(body, grid_spec=pltpu.PrefetchScalarGridSpec(num_scalar_pr...  135 us
    ppermute x37, waiting for transfers between devices, swap(): return lax.ppermute(value, axis, [(i, i ^ mask) for i in range(count)])  66.3 us
    ppermute x37, starting transfers between devices, swap(): return lax.ppermute(value, axis, [(i, i ^ mask) for i in range(count)])  54 us
    unnamed x176, local copies, waits for them, and re-layouts  49 us
    ppermute x4, starting transfers between devices, step_along(): return lax.ppermute(value, axis, pairs)  9.97 us
  transfers between devices with their start and end apart: 44, of which 18 were waited for; matrix products, arithmetic and copies ran while one was open for 5% of the time, Pallas kernels for 37%

profile of v5, /device:TPU:0, one launch (start us, length us, event | category | flops | bytes accessed | tf_op | source)
XLA Modules:
  0.0 349.9 jit_solution(13419951043802224793)
XLA Ops:
  7.9 3.5 fusion
  26.0 6.0 %shard_map.237 = (bf16[1024,1152]{1,0:T(8,128)(2,1)S(1)}, bf16[1024,288]{1,0:T(8,128)(2,1)S(1)}, bf16[1024,640]{1,0:T(8,128)(2,1)}) custom-call(bf16[1024,1152]{1,0:T(8,128)(2,1)S(1)} %copy-done.17, bf16[1024,48]{1,0:T(8,128)(2,1)S(1)} %compare_convert_fusion.refs_1_.refs_2_.refs_8_.refs_11_.refs_7_.refs_14_.refs_4_, ...), custom_call_target="tpu_custom_call" | custom-call | flops 6899999744 | bytes 1 | tf_op jit(solution)/shard_map/pallas_call | solution.py:90
  35.6 4.3 %collective-permute-start.3 = (bf16[1024,640]{1,0:T(8,128)(2,1)}, bf16[1024,640]{1,0:T(8,128)(2,1)}, u32[]{:S(2)}, u32[]{:S(2)}) collective-permute-start(bf16[1024,640]{1,0:T(8,128)(2,1)} %get-tuple-element.84.refs_7_), channel_id=1, source_target_pairs={{0,4},{4,8},{8,12},{12,16},{16,20},{20,24},{24,28},{1,5},{5,9},{9,... | collective-permute-start | bytes 3932168 | tf_op jit(solution)/shard_map/ppermute | solution.py:63
  45.9 5.1 %shard_map.238 = (bf16[1024,1152]{1,0:T(8,128)(2,1)S(1)}, f32[1024,1152]{1,0:T(8,128)S(1)}, f32[1,1152]{1,0:T(1,128)S(1)}, f32[16,1152]{1,0:T(8,128)S(1)}) custom-call(bf16[1024,1152]{1,0:T(8,128)(2,1)S(1)} %copy-done.60, bf16[1024,1152]{1,0:T(8,128)(2,1)S(1)} %copy-done.15, ...), custom_call_target="tpu_custom_call" | custom-call | flops 5750000128 | bytes 1 | tf_op jit(solution)/shard_map/pallas_call | solution.py:90
  53.9 10.3 %shard_map.239 = (bf16[512,288]{1,0:T(8,128)(2,1)S(1)}, f32[288,512]{1,0:T(8,128)S(1)}, f32[4,512]{1,0:T(4,128)S(1)}) custom-call(s32[4]{0:T(128)S(1)} %get-tuple-element.216.refs_0_, s32[4]{0:T(128)S(1)} %get-tuple-element.215.refs_1_, f32[1,1152]{1,0:T(1,128)S(1)} %get-tuple-element.82.refs_2_.refs_11_, s32[1,1024]{1,0:T(1,128)S(1)} %bitcast.34, ...), custom_call_target="tpu_custom_call" | custom-call | flops 11500000256 | bytes 1 | tf_op jit(solution)/shard_map/pallas_call | solution.py:90
  67.8 12.5 %shard_map.240 = (bf16[512,288]{1,0:T(8,128)(2,1)}, f32[288,512]{1,0:T(8,128)S(1)}, f32[4,512]{1,0:T(4,128)S(1)}) custom-call(s32[4]{0:T(128)S(1)} %get-tuple-element.216.refs_0_, s32[4]{0:T(128)S(1)} %get-tuple-element.215.refs_1_, f32[4,512]{1,0:T(4,128)S(1)} %get-tuple-element.85.refs_2_, s32[1,1024]{1,0:T(1,128)S(1)} %bitcast.35, ...), custom_call_target="tpu_custom_call" | custom-call | flops 11500000256 | bytes 1 | tf_op jit(solution)/shard_map/pallas_call | solution.py:90
  97.1 12.0 %shard_map.241 = (f32[1024,1152]{1,0:T(8,128)}, bf16[1024,1152]{1,0:T(8,128)(2,1)S(1)}, bf16[1024,1152]{1,0:T(8,128)(2,1)S(1)}, bf16[1024,1152]{1,0:T(8,128)(2,1...) custom-call(s32[1]{0:T(128)} %bitcast.refs_0_.refs_2_, ...), custom_call_target="tpu_custom_call" | custom-call | flops 13799999488 | bytes 1 | tf_op jit(solution)/shard_map/pallas_call | solution.py:90
  112.6 12.3 %shard_map.242 = (f32[1024,1152]{1,0:T(8,128)}, bf16[1024,1152]{1,0:T(8,128)(2,1)S(1)}, bf16[1024,1152]{1,0:T(8,128)(2,1)S(1)}, bf16[1024,1152]{1,0:T(8,128)(2,1...) custom-call(s32[1]{0:T(128)} %bitcast.refs_0_.refs_2_, ...), custom_call_target="tpu_custom_call", output_to_operand_aliasing={{0}: (1, {}), {1}: (2, {}), {2}: (3, {}), {3}: (4, {})} | custom-call | flops 13799999488 | bytes 1 | tf_op jit(solution)/shard_map/pallas_call | solution.py:90
  125.9 5.8 %shard_map.243 = (bf16[1024,1152]{1,0:T(8,128)(2,1)}, f32[1,16,1152]{2,1,0:T(8,128)S(1)}) custom-call(bf16[128,1152]{1,0:T(8,128)(2,1)S(1)} %get-tuple-element.89.refs_0_.refs_2_, bf16[128,1152]{1,0:T(8,128)(2,1)S(1)} %collective-permute-done.8.refs_1_.refs_3_, bf16[128,1152]{1,0:T(8,128)(2,1)S(1)} %collective-permute-done.9.refs_2_.refs_4_, ...), custom_call_target="tpu_custom_call" | custom-call | flops 6899999744 | bytes 1 | tf_op jit(solution)/shard_map/pallas_call | solution.py:90
  142.2 7.7 %shard_map.244.refs_1_ = bf16[1152,2304]{1,0:T(8,128)(2,1)S(1)} custom-call(f32[1,16,1152]{2,1,0:T(8,128)S(1)} %get-tuple-element.99.refs_0_, bf16[1024,1152]{1,0:T(8,128)(2,1)S(1)} %copy-done.68, bf16[1024,1152]{1,0:T(8,128)(2,1)S(1)} %copy-done.63, bf16[1024,1152]{1,0:T(8,128)(2,1)S(1)} %copy-done.72, bf16[1024,1152]{1,0:T(8,128)(2,1)S(1)} %copy-done.70), custom_call_target="tpu_custom_call" | custom-call | flops 8049999872 | bytes 1 | tf_op jit(solution)/shard_map/pallas_call | solution.py:90
  152.6 8.1 %shard_map.245 = (f32[256,1152]{1,0:T(8,128)}, bf16[256,1152]{1,0:T(8,128)(2,1)}, f32[1,16,1152]{2,1,0:T(8,128)}, f32[1,1152]{1,0:T(1,128)}, bf16[256,288]{1,0:T...) custom-call(s32[1]{0:T(128)} %bitcast.refs_0_.refs_2_, ...), custom_call_target="tpu_custom_call" | custom-call | flops 6899999744 | bytes 1 | tf_op jit(solution)/shard_map/pallas_call | solution.py:90
  170.9 10.8 %collective-permute-done.21.refs_12_ = bf16[256,288]{1,0:T(8,128)(2,1)} collective-permute-done((bf16[256,288]{1,0:T(8,128)(2,1)}, bf16[256,288]{1,0:T(8,128)(2,1)}, u32[]{:S(2)}, u32[]{:S(2)}) %collective-permute-start.21) | collective-permute-done | bytes 147488 | tf_op jit(solution)/shard_map/ppermute | solution.py:33
  182.9 6.3 %shard_map.246 = (f32[288,1024]{1,0:T(8,128)S(1)}, bf16[1024,288]{1,0:T(8,128)(2,1)S(1)}, bf16[1024,640]{1,0:T(8,128)(2,1)S(1)}, bf16[1024,640]{1,0:T(8,128)(2,1)S(1)}) custom-call(s32[4]{0:T(128)S(1)} %get-tuple-element.216.refs_0_, s32[4]{0:T(128)S(1)} %get-tuple-element.215.refs_1_, s32[1]{0:T(128)} %bitcast.refs_0_.refs_2_, s32[1,1024]{1,0:T(1,128)S(1)} %bitcast.36, ...), custom_call_target="tpu_custom_call" | custom-call | flops 9200000000 | bytes 1 | tf_op jit(solution)/shard_map/pallas_call | solution.py:90
  193.6 17.8 %shard_map.247 = (bf16[1024,288]{1,0:T(8,128)(2,1)S(1)}, f32[1024,640]{1,0:T(8,128)S(1)}) custom-call(s32[4]{0:T(128)S(1)} %get-tuple-element.216.refs_0_, s32[4]{0:T(128)S(1)} %get-tuple-element.215.refs_1_, s32[1,1024]{1,0:T(1,128)S(1)} %bitcast.37, s32[1,1024]{1,0:T(1,128)S(1)} %bitcast.33, ...), custom_call_target="tpu_custom_call" | custom-call | flops 18400000000 | bytes 1 | tf_op jit(solution)/shard_map/pallas_call | solution.py:90
  211.5 8.0 %shard_map.248 = (bf16[1024,864]{1,0:T(8,128)(2,1)S(1)}, f32[2,16,1152]{2,1,0:T(8,128)S(1)}, f32[1,864]{1,0:T(1,128)S(1)}, bf16[256,1152]{1,0:T(8,128)(2,1)S(1)}...) custom-call(s32[1]{0:T(128)} %bitcast.refs_0_.refs_2_, ...), custom_call_target="tpu_custom_call" | custom-call | flops 9200000000 | bytes 1 | tf_op jit(solution)/shard_map/pallas_call | solution.py:90
  220.4 7.0 %shard_map.249 = (bf16[4,144,1152]{2,1,0:T(8,128)(2,1)S(1)}, bf16[4,144,1152]{2,1,0:T(8,128)(2,1)}) custom-call(s32[1]{0:T(128)} %bitcast.refs_0_.refs_2_, s32[1]{0:T(128)} %bitcast.1.refs_1_, bf16[1024,1152]{1,0:T(8,128)(2,1)S(1)} %copy-done.61, bf16[1024,864]{1,0:T(8,128)(2,1)S(1)} %get-tuple-element.121.refs_3_, bf16[512,288]{1,0:T(8,128)(2,1)S(1)} %copy-done.27, ...), custom_call_target="tpu_custom_call" | custom-call | flops 8049999872 | bytes 1 | tf_op jit(solution)/shard_map/pallas_call | solution.py:90
  248.0 12.1 %collective-permute-done.26.refs_4_ = bf16[256,1152]{1,0:T(8,128)(2,1)} collective-permute-done((bf16[256,1152]{1,0:T(8,128)(2,1)}, bf16[256,1152]{1,0:T(8,128)(2,1)}, u32[]{:S(2)}, u32[]{:S(2)}) %collective-permute-start.26) | collective-permute-done | bytes 589856 | tf_op jit(solution)/shard_map/ppermute | solution.py:33
  270.0 8.0 %collective-permute-done.32 = f32[2,97,288]{2,1,0:T(8,128)S(1)} collective-permute-done((f32[2,97,288]{2,1,0:T(8,128)S(1)}, f32[2,97,288]{2,1,0:T(8,128)S(1)}, u32[]{:S(2)}, u32[]{:S(2)}) %collective-permute-start.32) | collective-permute-done | bytes 223520 | tf_op jit(solution)/shard_map/ppermute | solution.py:33
  286.6 3.5 collective-permute-start.35
  290.3 9.6 %collective-permute-done.35 = f32[108,288]{1,0:T(8,128)S(1)} collective-permute-done((f32[108,288]{1,0:T(8,128)S(1)}, f32[108,288]{1,0:T(8,128)S(1)}, u32[]{:S(2)}, u32[]{:S(2)}) %collective-permute-start.35) | collective-permute-done | bytes 124448 | tf_op jit(solution)/shard_map/ppermute | solution.py:33
  302.1 4.4 %collective-permute-done.29.refs_3_ = bf16[256,1152]{1,0:T(8,128)(2,1)} collective-permute-done((bf16[256,1152]{1,0:T(8,128)(2,1)S(1)}, bf16[256,1152]{1,0:T(8,128)(2,1)}, u32[]{:S(2)}, u32[]{:S(2)}) %collective-permute-start.29) | collective-permute-done | bytes 589856 | tf_op jit(solution)/shard_map/ppermute | solution.py:33
  307.8 5.2 %shard_map.252 = f32[1024,1152]{1,0:T(8,128)} custom-call(s32[1]{0:T(128)} %bitcast.refs_0_.refs_2_, bf16[256,1152]{1,0:T(8,128)(2,1)S(1)} %copy-done.24, bf16[256,1152]{1,0:T(8,128)(2,1)} %collective-permute-done.28.refs_2_, bf16[256,1152]{1,0:T(8,128)(2,1)} %collective-permute-done.29.refs_3_, bf16[256,1152]{1,0:T(8,128)(2,1)S(1)} %collective-permute-done.30.refs_4_), custom_call_target="tpu_custom_call" | custom-call | flops 3449999872 | bytes 1 | tf_op jit(solution)/shard_map/pallas_call | solution.py:90
  318.8 6.1 %collective-permute-start.40 = (bf16[1,144,1152]{2,1,0:T(8,128)(2,1)S(1)}, bf16[1,144,1152]{2,1,0:T(8,128)(2,1)S(1)}, u32[]{:S(2)}, u32[]{:S(2)}) collective-permute-start(bf16[1,144,1152]{2,1,0:T(8,128)(2,1)S(1)} %get-tuple-element.144), channel_id=1, source_target_pairs={{0,16},{4,20},{8,24},{12,28},{16,0},{20,4},{24,8},{28,12},{1,17},{... | collective-permute-start | bytes 995336 | tf_op jit(solution)/shard_map/ppermute | solution.py:33
  331.1 4.5 %fusion.4 = f32[1152,6,288]{0,2,1:T(8,128)} fusion(bf16[16,1152]{1,0:T(8,128)(2,1)S(1)} %get-tuple-element.213, bf16[6,16,288]{2,1,0:T(8,128)(2,1)S(1)} %get-tuple-element.210, bf16[6,16,288]{2,1,0:T(8,128)(2,1)S(1)} %get-tuple-element.211, bf16[6,16,288]{2,1,0:T(8,128)(2,1)S(1)} %get-tuple-element.212), kind=kOutput, calls=%fused_computation.30 | convolution fusion | flops 191932416 | bytes 8165376 | tf_op jit(solution)/shard_map/id,kif->dkf/dot_general | solution.py:1319
  (320 shorter events, 143.9 us)
Async XLA Ops:
  7.2 79.8 %all-gather.2.cloned.1.call-start = ((), (), s32[]{:S(2)}) async-start(), calls=%async_computation.1 | async-start | bytes 3317760 | tf_op jit(solution)/shard_map/all_gather | solution.py:1186
  16.0 220.4 %all-reduce.3.cloned.1.call-start = ((), (), s32[]{:S(2)}) async-start(), calls=%async_computation.2 | async-start | bytes 4718592 | tf_op jit(solution)/shard_map/psum | solution.py:1229
  34.3 19.5 %collective-permute-start.4 = (bf16[1024,640]{1,0:T(8,128)(2,1)}, bf16[1024,640]{1,0:T(8,128)(2,1)}, u32[]{:S(2)}, u32[]{:S(2)}) collective-permute-start(bf16[1024,640]{1,0:T(8,128)(2,1)} %get-tuple-element.84.refs_7_), channel_id=1, source_target_pairs={{4,0},{8,4},{12,8},{16,12},{20,16},{24,20},{28,24},{5,1},{9,5},{13... | collective-permute-start | bytes 3932168 | tf_op jit(solution)/shard_map/ppermute | solution.py:63
  64.2 19.5 %collective-permute-start.7 = (bf16[512,288]{1,0:T(8,128)(2,1)S(1)}, bf16[512,288]{1,0:T(8,128)(2,1)S(1)}, u32[]{:S(2)}, u32[]{:S(2)}) collective-permute-start(bf16[512,288]{1,0:T(8,128)(2,1)S(1)} %get-tuple-element.87.refs_2_.refs_4_), channel_id=1, source_target_pairs={{0,3},{1,2},{2,1},{3,0},{4,7},{5,6},{6,5},{7,4},{8,11},{9,10},{10,... | collective-permute-start | bytes 884744 | tf_op jit(solution)/shard_map/ppermute | solution.py:33
  65.5 20.0 %collective-permute-start.6 = (bf16[512,288]{1,0:T(8,128)(2,1)S(1)}, bf16[512,288]{1,0:T(8,128)(2,1)S(1)}, u32[]{:S(2)}, u32[]{:S(2)}) collective-permute-start(bf16[512,288]{1,0:T(8,128)(2,1)S(1)} %get-tuple-element.87.refs_2_.refs_4_), channel_id=1, source_target_pairs={{0,2},{1,3},{2,0},{3,1},{4,6},{5,7},{6,4},{7,5},{8,10},{9,11},{10,... | collective-permute-start | bytes 884744 | tf_op jit(solution)/shard_map/ppermute | solution.py:33
  67.0 19.3 %collective-permute-start.5 = (bf16[512,288]{1,0:T(8,128)(2,1)S(1)}, bf16[512,288]{1,0:T(8,128)(2,1)S(1)}, u32[]{:S(2)}, u32[]{:S(2)}) collective-permute-start(bf16[512,288]{1,0:T(8,128)(2,1)S(1)} %get-tuple-element.87.refs_2_.refs_4_), channel_id=1, source_target_pairs={{0,1},{1,0},{2,3},{3,2},{4,5},{5,4},{6,7},{7,6},{8,9},{9,8},{10,11... | collective-permute-start | bytes 884744 | tf_op jit(solution)/shard_map/ppermute | solution.py:33
  81.1 29.8 %collective-permute-start.13 = (bf16[512,288]{1,0:T(8,128)(2,1)}, bf16[512,288]{1,0:T(8,128)(2,1)}, u32[]{:S(2)}, u32[]{:S(2)}) collective-permute-start(bf16[512,288]{1,0:T(8,128)(2,1)} %get-tuple-element.97.refs_5_), channel_id=1, source_target_pairs={{0,3},{1,2},{2,1},{3,0},{4,7},{5,6},{6,5},{7,4},{8,11},{9,10},{10,... | collective-permute-start | bytes 884744 | tf_op jit(solution)/shard_map/ppermute | solution.py:33
  82.2 30.4 %collective-permute-start.12 = (bf16[512,288]{1,0:T(8,128)(2,1)}, bf16[512,288]{1,0:T(8,128)(2,1)}, u32[]{:S(2)}, u32[]{:S(2)}) collective-permute-start(bf16[512,288]{1,0:T(8,128)(2,1)} %get-tuple-element.97.refs_5_), channel_id=1, source_target_pairs={{0,2},{1,3},{2,0},{3,1},{4,6},{5,7},{6,4},{7,5},{8,10},{9,11},{10,... | collective-permute-start | bytes 884744 | tf_op jit(solution)/shard_map/ppermute | solution.py:33
  84.5 28.1 %collective-permute-start.11 = (bf16[512,288]{1,0:T(8,128)(2,1)}, bf16[512,288]{1,0:T(8,128)(2,1)}, u32[]{:S(2)}, u32[]{:S(2)}) collective-permute-start(bf16[512,288]{1,0:T(8,128)(2,1)} %get-tuple-element.97.refs_5_), channel_id=1, source_target_pairs={{0,1},{1,0},{2,3},{3,2},{4,5},{5,4},{6,7},{7,6},{8,9},{9,8},{10,11... | collective-permute-start | bytes 884744 | tf_op jit(solution)/shard_map/ppermute | solution.py:33
  131.8 208.0 %reduce-scatter.2.cloned.1.call-start = ((), (), s32[]{:S(2)}) async-start(), calls=%async_computation.3 | async-start | bytes 5971968 | tf_op jit(solution)/shard_map/reduce_scatter | solution.py:1327
  131.8 20.4 %collective-permute-start.14 = (bf16[128,1152]{1,0:T(8,128)(2,1)}, bf16[128,1152]{1,0:T(8,128)(2,1)}, u32[]{:S(2)}, u32[]{:S(2)}) collective-permute-start(bf16[128,1152]{1,0:T(8,128)(2,1)} %copy-done.41), channel_id=1, source_target_pairs={{0,1},{1,0},{2,3},{3,2},{4,5},{5,4},{6,7},{7,6},{8,9},{9,8},{10,11... | collective-permute-start | bytes 884744 | tf_op jit(solution)/shard_map/ppermute | solution.py:33
  132.7 19.5 %collective-permute-start.15 = (bf16[128,1152]{1,0:T(8,128)(2,1)S(1)}, bf16[128,1152]{1,0:T(8,128)(2,1)}, u32[]{:S(2)}, u32[]{:S(2)}) collective-permute-start(bf16[128,1152]{1,0:T(8,128)(2,1)S(1)} %copy-done.40), channel_id=1, source_target_pairs={{0,2},{1,3},{2,0},{3,1},{4,6},{5,7},{6,4},{7,5},{8,10},{9,11},{10,... | collective-permute-start | bytes 884744 | tf_op jit(solution)/shard_map/ppermute | solution.py:33
  165.5 46.0 %collective-permute-start.19 = (bf16[256,1152]{1,0:T(8,128)(2,1)}, bf16[256,1152]{1,0:T(8,128)(2,1)}, u32[]{:S(2)}, u32[]{:S(2)}) collective-permute-start(bf16[256,1152]{1,0:T(8,128)(2,1)} %get-tuple-element.108.refs_1_.refs_6_), channel_id=1, source_target_pairs={{0,3},{1,2},{2,1},{3,0},{4,7},{5,6},{6,5},{7,4},{8,11},{9,10},{10,... | collective-permute-start | bytes 1769480 | tf_op jit(solution)/shard_map/ppermute | solution.py:33
  167.8 43.7 %collective-permute-start.18 = (bf16[256,1152]{1,0:T(8,128)(2,1)}, bf16[256,1152]{1,0:T(8,128)(2,1)}, u32[]{:S(2)}, u32[]{:S(2)}) collective-permute-start(bf16[256,1152]{1,0:T(8,128)(2,1)} %get-tuple-element.108.refs_1_.refs_6_), channel_id=1, source_target_pairs={{0,2},{1,3},{2,0},{3,1},{4,6},{5,7},{6,4},{7,5},{8,10},{9,11},{10,... | collective-permute-start | bytes 1769480 | tf_op jit(solution)/shard_map/ppermute | solution.py:33
  168.9 42.6 %collective-permute-start.17 = (bf16[256,1152]{1,0:T(8,128)(2,1)}, bf16[256,1152]{1,0:T(8,128)(2,1)S(1)}, u32[]{:S(2)}, u32[]{:S(2)}) collective-permute-start(bf16[256,1152]{1,0:T(8,128)(2,1)} %get-tuple-element.108.refs_1_.refs_6_), channel_id=1, source_target_pairs={{0,1},{1,0},{2,3},{3,2},{4,5},{5,4},{6,7},{7,6},{8,9},{9,8},{10,11... | collective-permute-start | bytes 1769480 | tf_op jit(solution)/shard_map/ppermute | solution.py:33
  189.2 22.3 %collective-permute-start.23 = (bf16[1024,640]{1,0:T(8,128)(2,1)S(1)}, bf16[1024,640]{1,0:T(8,128)(2,1)S(1)}, u32[]{:S(2)}, u32[]{:S(2)}) collective-permute-start(bf16[1024,640]{1,0:T(8,128)(2,1)S(1)} %get-tuple-element.119), channel_id=1, source_target_pairs={{4,0},{8,4},{12,8},{16,12},{20,16},{24,20},{28,24},{5,1},{9,5},{13... | collective-permute-start | bytes 3932168 | tf_op jit(solution)/shard_map/ppermute | solution.py:63
  190.5 21.0 %collective-permute-start.24 = (bf16[1024,640]{1,0:T(8,128)(2,1)S(1)}, bf16[1024,640]{1,0:T(8,128)(2,1)S(1)}, u32[]{:S(2)}, u32[]{:S(2)}) collective-permute-start(bf16[1024,640]{1,0:T(8,128)(2,1)S(1)} %get-tuple-element.120), channel_id=1, source_target_pairs={{0,4},{4,8},{8,12},{12,16},{16,20},{20,24},{24,28},{1,5},{5,9},{9,... | collective-permute-start | bytes 3932168 | tf_op jit(solution)/shard_map/ppermute | solution.py:63
  228.5 37.7 %collective-permute-start.31 = (bf16[4,144,1152]{2,1,0:T(8,128)(2,1)}, bf16[4,144,1152]{2,1,0:T(8,128)(2,1)}, u32[]{:S(2)}, u32[]{:S(2)}) collective-permute-start(bf16[4,144,1152]{2,1,0:T(8,128)(2,1)} %get-tuple-element.129), channel_id=1, source_target_pairs={{0,4},{4,0},{8,12},{12,8},{16,20},{20,16},{24,28},{28,24},{1,5},{5... | collective-permute-start | bytes 3981320 | tf_op jit(solution)/shard_map/ppermute | solution.py:33
  231.9 28.2 %collective-permute-start.26 = (bf16[256,1152]{1,0:T(8,128)(2,1)}, bf16[256,1152]{1,0:T(8,128)(2,1)}, u32[]{:S(2)}, u32[]{:S(2)}) collective-permute-start(bf16[256,1152]{1,0:T(8,128)(2,1)} %get-tuple-element.126), channel_id=1, source_target_pairs={{0,2},{1,3},{2,0},{3,1},{4,6},{5,7},{6,4},{7,5},{8,10},{9,11},{10,... | collective-permute-start | bytes 1769480 | tf_op jit(solution)/shard_map/ppermute | solution.py:33
  234.4 27.6 %collective-permute-start.27 = (bf16[256,1152]{1,0:T(8,128)(2,1)}, bf16[256,1152]{1,0:T(8,128)(2,1)}, u32[]{:S(2)}, u32[]{:S(2)}) collective-permute-start(bf16[256,1152]{1,0:T(8,128)(2,1)} %get-tuple-element.127), channel_id=1, source_target_pairs={{0,3},{1,2},{2,1},{3,0},{4,7},{5,6},{6,5},{7,4},{8,11},{9,10},{10,... | collective-permute-start | bytes 1769480 | tf_op jit(solution)/shard_map/ppermute | solution.py:33
  279.5 22.6 %collective-permute-start.30 = (bf16[256,1152]{1,0:T(8,128)(2,1)S(1)}, bf16[256,1152]{1,0:T(8,128)(2,1)S(1)}, u32[]{:S(2)}, u32[]{:S(2)}) collective-permute-start(bf16[256,1152]{1,0:T(8,128)(2,1)S(1)} %copy-done.24), channel_id=1, source_target_pairs={{0,3},{1,2},{2,1},{3,0},{4,7},{5,6},{6,5},{7,4},{8,11},{9,10},{10,... | collective-permute-start | bytes 1769480 | tf_op jit(solution)/shard_map/ppermute | solution.py:33
  280.8 25.7 %collective-permute-start.29 = (bf16[256,1152]{1,0:T(8,128)(2,1)S(1)}, bf16[256,1152]{1,0:T(8,128)(2,1)}, u32[]{:S(2)}, u32[]{:S(2)}) collective-permute-start(bf16[256,1152]{1,0:T(8,128)(2,1)S(1)} %copy-done.24), channel_id=1, source_target_pairs={{0,2},{1,3},{2,0},{3,1},{4,6},{5,7},{6,4},{7,5},{8,10},{9,11},{10,... | collective-permute-start | bytes 1769480 | tf_op jit(solution)/shard_map/ppermute | solution.py:33
  282.4 25.4 %collective-permute-start.28 = (bf16[256,1152]{1,0:T(8,128)(2,1)S(1)}, bf16[256,1152]{1,0:T(8,128)(2,1)}, u32[]{:S(2)}, u32[]{:S(2)}) collective-permute-start(bf16[256,1152]{1,0:T(8,128)(2,1)S(1)} %copy-done.24), channel_id=1, source_target_pairs={{0,1},{1,0},{2,3},{3,2},{4,5},{5,4},{6,7},{7,6},{8,9},{9,8},{10,11... | collective-permute-start | bytes 1769480 | tf_op jit(solution)/shard_map/ppermute | solution.py:33
  290.1 28.4 %collective-permute-start.39 = (bf16[2,144,1152]{2,1,0:T(8,128)(2,1)S(1)}, bf16[2,144,1152]{2,1,0:T(8,128)(2,1)S(1)}, u32[]{:S(2)}, u32[]{:S(2)}) collective-permute-start(bf16[2,144,1152]{2,1,0:T(8,128)(2,1)S(1)} %get-tuple-element.142), channel_id=1, source_target_pairs={{0,8},{4,12},{8,0},{12,4},{16,24},{20,28},{24,16},{28,20},{1,9},{5... | collective-permute-start | bytes 1990664 | tf_op jit(solution)/shard_map/ppermute | solution.py:33
  (106 other events, 884.6 us)
Sparse Core Ops, SparseCore 0:
  16.1 41.6 all-gather.1
  131.9 104.4 all-reduce.2
  238.8 59.7 reduce-scatter.1
